TPU v7x, 256 devices: a whole 4x4x8 slice. The times are simulated.
256 devices in a mesh: blk: 64 (over z, y, core), sub: 4 (over x).
Axes of the slice: x: 4, y: 4, z: 8, core: 2. Of those that a mesh axis runs over, the one named last changes fastest.
Arguments:
- tracers: float32 [2560, 4, 5400], P(('blk', 'sub')), may hold values from -6 to 6
- velocity: float32 [2560, 4, 5400], P(('blk', 'sub')), may hold values from -3 to 3
- kappa: float32 [2560, 5400], P(('blk', 'sub')), may hold values from 0.1 to 4
- kmt: float32 [2560, 5400], P(('blk', 'sub')), may hold values from -1 to 2.5
- block_owner: int32 [1280], replicated, may hold values from 0 to 2559, as said below
- neighbours: int32 [1280, 4], replicated, may hold values from -1 to 1279, as said below
- fold_partner: int32 [1280], replicated, may hold values from -1 to 1279, as said below
Outputs:
- tracers_out: float32 [2560, 4, 5400], P(('blk', 'sub'))
Inputs may be any that keep to these rules, and one draw needn't show every extreme that they name: `block_owner`: the values are distinct. Every device holds between 3 and 10 blocks, in its first slots; devices in index order hold consecutive runs of the blocks taken along a serpentine curve over the block grid. `neighbours`: row b lists the blocks west, east, south and north of block b on a grid of 40 by 40 blocks that is periodic from west to east, or -1 where that place is land or off the grid; the north entry of the northernmost row is -1. The owner of every listed block lies at most 27 devices from the owner of block b. `fold_partner`: for a block of the northernmost row, the block of that row at the mirrored column (39 - column); -1 for all other blocks. Its owner lies at most 27 devices from block b's owner.
All inputs are finite; a program needn't handle non-finite values.
Results may differ from a plain program's by a relative error of at most 0.0003.
Values sent between devices are 32-bit elements; how exact they have to be, the bound alone decides.
A program may use at most 192 MiB of HBM per device.

v0:
```python
import jax
import jax.numpy as jnp
from jax import lax
from jax.sharding import PartitionSpec as P

IB = 90
JB = 60
REACH = 27


COURANT = 0.2


def shifted(block, axis, distance):
    devices = range(lax.axis_size(axis))
    route = [(i - distance, i) for i in devices if i - distance in devices]
    return lax.ppermute(block, axis, route)


def edge_pack(block_field):
    count, chans, rows, cols = block_field.shape
    west_edge = block_field[:, :, :, 0:2].reshape(count, chans, rows * 2)
    east_edge = block_field[:, :, :, cols - 2 :].reshape(count, chans, rows * 2)
    south_edge = block_field[:, :, 0:2, :].reshape(count, chans, 2 * cols)
    north_edge = block_field[:, :, rows - 2 :, :].reshape(count, chans, 2 * cols)
    return jnp.concatenate([west_edge, east_edge, south_edge, north_edge], axis=2)


def fetch(source, window_codes):
    safe_codes = jnp.maximum(window_codes, 0)
    picked = jnp.take(source, safe_codes.reshape(-1), axis=0)
    picked = picked.reshape(window_codes.shape + source.shape[1:])
    return jnp.where((window_codes >= 0)[..., None, None], picked, 0.0)


def extend(block_field, sources, fold_sign):
    count, chans, rows, cols = block_field.shape
    strip = 2 * rows
    west_halo = sources[:, 0, :, strip : 2 * strip].reshape(count, chans, rows, 2)
    east_halo = sources[:, 1, :, 0:strip].reshape(count, chans, rows, 2)
    south_halo = sources[:, 2, :, 2 * strip + 2 * cols :].reshape(count, chans, 2, cols)
    north_halo = sources[:, 3, :, 2 * strip : 2 * strip + 2 * cols].reshape(count, chans, 2, cols)
    mirrored = sources[:, 4, :, 2 * strip + 2 * cols :].reshape(count, chans, 2, cols)[
        :, :, ::-1, ::-1
    ]
    north_halo = north_halo + fold_sign * mirrored
    middle = jnp.concatenate([west_halo, block_field, east_halo], axis=3)
    corner = jnp.zeros((count, chans, 2, 2), block_field.dtype)
    bottom = jnp.concatenate([corner, south_halo, corner], axis=3)
    top_rows = jnp.concatenate([corner, north_halo, corner], axis=3)
    return jnp.concatenate([bottom, middle, top_rows], axis=2)


def prepare(static_ext, diffusivity):
    levels = (static_ext.shape[1] - 1) // 2
    rows = static_ext.shape[2] - 4
    cols = static_ext.shape[3] - 4
    east_vel = static_ext[:, :levels]
    north_vel = static_ext[:, levels : 2 * levels]
    depth = static_ext[:, 2 * levels :]
    level_ids = jnp.arange(levels).astype(static_ext.dtype).reshape(1, levels, 1, 1)
    wet = jnp.clip(depth - level_ids, 0.0, 1.0)
    face_x = 0.5 * (
        east_vel[:, :, 2 : rows + 2, 1 : cols + 2] + east_vel[:, :, 2 : rows + 2, 2 : cols + 3]
    )
    face_x = face_x * wet[:, :, 2 : rows + 2, 1 : cols + 2] * wet[:, :, 2 : rows + 2, 2 : cols + 3]
    face_y = 0.5 * (
        north_vel[:, :, 1 : rows + 2, 2 : cols + 2] + north_vel[:, :, 2 : rows + 3, 2 : cols + 2]
    )
    face_y = face_y * wet[:, :, 1 : rows + 2, 2 : cols + 2] * wet[:, :, 2 : rows + 3, 2 : cols + 2]
    inner = wet[:, :, 2 : rows + 2, 2 : cols + 2]
    coupling = diffusivity[:, None] * inner[:, :-1] * inner[:, 1:]
    return (face_x, face_y, inner, coupling)


def face_flux(velocity_face, left_far, left_near, right_near, right_far):
    centered = (7.0 * (left_near + right_near) - (left_far + right_far)) / 12.0
    upwind = (right_far - 3.0 * right_near + 3.0 * left_near - left_far) / 12.0
    return velocity_face * centered + jnp.abs(velocity_face) * upwind


def vertical_solve(rhs_cols, coupling):
    levels = rhs_cols.shape[2]
    partials = []
    ratios = []
    for level in range(levels):
        coef_below = coupling[:, :, level] if level < levels - 1 else 0.0
        coef_above = coupling[:, :, level - 1] if level > 0 else 0.0
        diagonal = 1.0 + coef_above + coef_below
        if level == 0:
            divider_value = diagonal
            partial_value = rhs_cols[:, :, 0] / divider_value
        else:
            divider_value = diagonal - coef_above * ratios[-1]
            partial_value = (rhs_cols[:, :, level] + coef_above * partials[-1]) / divider_value
        partials.append(partial_value)
        ratios.append(coef_below / divider_value)
    result = [None] * levels
    result[levels - 1] = partials[levels - 1]
    level = 0
    result[level] = partials[level] + ratios[level] * result[level + 1]
    return jnp.stack(result, axis=2)


def advance(tracer_ext, face_x, face_y, inner, coupling):
    count, chans = (tracer_ext.shape[0], tracer_ext.shape[1])
    levels, rows, cols = (inner.shape[1], inner.shape[2], inner.shape[3])
    ext_cols = tracer_ext.reshape(count, chans // levels, levels, rows + 4, cols + 4)
    middle = ext_cols[:, :, :, 2 : rows + 2]
    flux_x = face_flux(
        face_x[:, None],
        middle[..., 0 : cols + 1],
        middle[..., 1 : cols + 2],
        middle[..., 2 : cols + 3],
        middle[..., 3 : cols + 4],
    )
    column = ext_cols[..., 2 : cols + 2]
    flux_y = face_flux(
        face_y[:, None],
        column[:, :, :, 0 : rows + 1],
        column[:, :, :, 1 : rows + 2],
        column[:, :, :, 2 : rows + 3],
        column[:, :, :, 3 : rows + 4],
    )
    center = middle[..., 2 : cols + 2]
    divergence = flux_x[..., 1:] - flux_x[..., :-1] + (flux_y[:, :, :, 1:] - flux_y[:, :, :, :-1])
    explicit = center - COURANT * inner[:, None] * divergence
    solved = vertical_solve(explicit, coupling[:, None])
    return solved.reshape(count, chans, rows, cols)


def nearby(edge_block, fixed_fields):
    pieces = []
    for offset in range(-REACH, REACH + 1):
        if offset == 0:
            pieces.append(edge_block)
        elif fixed_fields:
            pieces.append(shifted(edge_block, ("blk", "sub"), -offset))
        else:
            pieces.append(shifted(edge_block, ("blk", "sub"), -offset))
    return jnp.concatenate(pieces, axis=0)


def per_device(tracers, velocity, kappa, kmt, block_owner, neighbours, fold_partner):
    slot_count = tracers.shape[0]
    chans = tracers.shape[1]
    sub_count = lax.axis_size("sub")
    my_index = lax.axis_index("blk") * sub_count + lax.axis_index("sub")
    slot_total = slot_count * lax.axis_size("blk") * sub_count
    block_count = block_owner.shape[0]
    slot_block = (
        jnp.full((slot_total,), -1, jnp.int32)
        .at[block_owner]
        .set(jnp.arange(block_count, dtype=jnp.int32))
    )
    mine = lax.dynamic_slice_in_dim(slot_block, my_index * slot_count, slot_count, 0)
    live_slot = mine >= 0
    safe_ids = jnp.maximum(mine, 0)
    links = jnp.concatenate([neighbours[safe_ids], fold_partner[safe_ids][:, None]], axis=1)
    links = jnp.where(live_slot[:, None], links, -1)
    link_codes = jnp.where(links >= 0, block_owner[jnp.maximum(links, 0)], -1)
    owner_dev = link_codes // slot_count
    window_codes = jnp.where(
        link_codes >= 0, (owner_dev - my_index + REACH) * slot_count + link_codes % slot_count, -1
    )
    levels = velocity.shape[1] // 2
    statics = jnp.concatenate([velocity, kmt[:, None, :]], axis=1)
    statics = statics.reshape(slot_count, 2 * levels + 1, JB, IB)
    fold_sign = jnp.concatenate(
        [-jnp.ones((2 * levels,), jnp.float32), jnp.ones((1,), jnp.float32)]
    ).reshape(1, -1, 1, 1)
    static_window = nearby(edge_pack(statics), True)
    static_ext = extend(statics, fetch(static_window, window_codes), fold_sign)
    face_x, face_y, inner, coupling = prepare(static_ext, kappa.reshape(slot_count, JB, IB))
    state = tracers.reshape(slot_count, chans, JB, IB)
    tracer_window = nearby(edge_pack(state), False)
    tracer_ext = extend(state, fetch(tracer_window, window_codes), 1.0)
    state = advance(tracer_ext, face_x, face_y, inner, coupling)
    result = state.reshape(slot_count, chans, JB * IB)
    return jnp.where(live_slot[:, None, None], result, 0.0)


def solution(mesh):
    placed = (
        P(("blk", "sub"), None, None),
        P(("blk", "sub"), None, None),
        P(("blk", "sub"), None),
        P(("blk", "sub"), None),
        P(),
        P(),
        P(),
    )
    return jax.shard_map(
        per_device,
        mesh=mesh,
        in_specs=placed,
        out_specs=P(("blk", "sub"), None, None),
        check_vma=False,
    )
```

profile of v0, /device:TPU:1, one launch (start us, length us, event | category | flops | bytes accessed | tf_op | source)
XLA Modules:
  0.0 1243.3 jit_solution(7491419737833082774)
XLA Ops:
  16.1 15.7 %collective-permute-start.54 = (f32[10,5,600]{2,1,0:T(8,128)S(1)}, f32[10,5,600]{2,1,0:T(8,128)}, u32[]{:S(2)}, u32[]{:S(2)}) collective-permute-start(f32[10,5,600]{2,1,0:T(8,128)S(1)} %pad_maximum_fusion.22), channel_id=1, source_target_pairs={{0,27},{1,28},{2,29},{3,30},{4,31},{5,32},{6,33},{7,34},{8,35},{9,... | collective-permute-start | bytes 360008 | tf_op jit(solution)/shard_map/ppermute | solution.py:17
  31.8 13.1 %collective-permute-start.55 = (f32[10,5,600]{2,1,0:T(8,128)S(1)}, f32[10,5,600]{2,1,0:T(8,128)}, u32[]{:S(2)}, u32[]{:S(2)}) collective-permute-start(f32[10,5,600]{2,1,0:T(8,128)S(1)} %pad_maximum_fusion.22), channel_id=1, source_target_pairs={{0,26},{1,27},{2,28},{3,29},{4,30},{5,31},{6,32},{7,33},{8,34},{9,... | collective-permute-start | bytes 360008 | tf_op jit(solution)/shard_map/ppermute | solution.py:17
  44.9 13.1 %collective-permute-start.56 = (f32[10,5,600]{2,1,0:T(8,128)S(1)}, f32[10,5,600]{2,1,0:T(8,128)}, u32[]{:S(2)}, u32[]{:S(2)}) collective-permute-start(f32[10,5,600]{2,1,0:T(8,128)S(1)} %pad_maximum_fusion.22), channel_id=1, source_target_pairs={{0,25},{1,26},{2,27},{3,28},{4,29},{5,30},{6,31},{7,32},{8,33},{9,... | collective-permute-start | bytes 360008 | tf_op jit(solution)/shard_map/ppermute | solution.py:17
  58.1 13.2 %collective-permute-start.57 = (f32[10,5,600]{2,1,0:T(8,128)S(1)}, f32[10,5,600]{2,1,0:T(8,128)}, u32[]{:S(2)}, u32[]{:S(2)}) collective-permute-start(f32[10,5,600]{2,1,0:T(8,128)S(1)} %pad_maximum_fusion.22), channel_id=1, source_target_pairs={{0,24},{1,25},{2,26},{3,27},{4,28},{5,29},{6,30},{7,31},{8,32},{9,... | collective-permute-start | bytes 360008 | tf_op jit(solution)/shard_map/ppermute | solution.py:17
  83.6 13.1 %collective-permute-start = (f32[10,4,600]{2,1,0:T(4,128)}, f32[10,4,600]{2,1,0:T(4,128)}, u32[]{:S(2)}, u32[]{:S(2)}) collective-permute-start(f32[10,4,600]{2,1,0:T(4,128)} %pad_maximum_fusion.23), channel_id=1, source_target_pairs={{0,27},{1,28},{2,29},{3,30},{4,31},{5,32},{6,33},{7,34},{8,35},{9,... | collective-permute-start | bytes 288008 | tf_op jit(solution)/shard_map/ppermute | solution.py:17
  96.7 16.2 %scatter_custom_fusion = s32[2560]{0:T(1024)S(1)} fusion(s32[1280]{0:T(1024)S(1)} %compare_select_fusion, s32[1280]{0:T(1024)S(1)} %iota.8, s32[]{:T(128)} %constant.37.clone.1), kind=kCustom, calls=%fused_computation.209 | custom fusion | bytes 10244 | tf_op jit(solution)/shard_map/scatter | solution.py:154
  121.0 12.5 %collective-permute-start.1 = (f32[10,4,600]{2,1,0:T(4,128)}, f32[10,4,600]{2,1,0:T(4,128)S(1)}, u32[]{:S(2)}, u32[]{:S(2)}) collective-permute-start(f32[10,4,600]{2,1,0:T(4,128)} %pad_maximum_fusion.23), channel_id=1, source_target_pairs={{0,26},{1,27},{2,28},{3,29},{4,30},{5,31},{6,32},{7,33},{8,34},{9,... | collective-permute-start | bytes 288008 | tf_op jit(solution)/shard_map/ppermute | solution.py:17
  135.4 16.3 %collective-permute-start.2 = (f32[10,4,600]{2,1,0:T(4,128)}, f32[10,4,600]{2,1,0:T(4,128)S(1)}, u32[]{:S(2)}, u32[]{:S(2)}) collective-permute-start(f32[10,4,600]{2,1,0:T(4,128)} %pad_maximum_fusion.23), channel_id=1, source_target_pairs={{0,25},{1,26},{2,27},{3,28},{4,29},{5,30},{6,31},{7,32},{8,33},{9,... | collective-permute-start | bytes 288008 | tf_op jit(solution)/shard_map/ppermute | solution.py:17
  153.8 15.8 %collective-permute-start.3 = (f32[10,4,600]{2,1,0:T(4,128)}, f32[10,4,600]{2,1,0:T(4,128)S(1)}, u32[]{:S(2)}, u32[]{:S(2)}) collective-permute-start(f32[10,4,600]{2,1,0:T(4,128)} %pad_maximum_fusion.23), channel_id=1, source_target_pairs={{0,24},{1,25},{2,26},{3,27},{4,28},{5,29},{6,30},{7,31},{8,32},{9,... | collective-permute-start | bytes 288008 | tf_op jit(solution)/shard_map/ppermute | solution.py:17
  225.4 11.4 collective-permute-start.10
  321.9 40.2 %collective-permute-start.20 = (f32[10,4,600]{2,1,0:T(4,128)}, f32[10,4,600]{2,1,0:T(4,128)S(1)}, u32[]{:S(2)}, u32[]{:S(2)}) collective-permute-start(f32[10,4,600]{2,1,0:T(4,128)} %pad_maximum_fusion.23), channel_id=1, source_target_pairs={{0,7},{1,8},{2,9},{3,10},{4,11},{5,12},{6,13},{7,14},{8,15},{9,16}... | collective-permute-start | bytes 288008 | tf_op jit(solution)/shard_map/ppermute | solution.py:17
  364.0 15.7 %collective-permute-start.21 = (f32[10,4,600]{2,1,0:T(4,128)}, f32[10,4,600]{2,1,0:T(4,128)S(1)}, u32[]{:S(2)}, u32[]{:S(2)}) collective-permute-start(f32[10,4,600]{2,1,0:T(4,128)} %pad_maximum_fusion.23), channel_id=1, source_target_pairs={{0,6},{1,7},{2,8},{3,9},{4,10},{5,11},{6,12},{7,13},{8,14},{9,15},... | collective-permute-start | bytes 288008 | tf_op jit(solution)/shard_map/ppermute | solution.py:17
  381.7 15.2 %collective-permute-start.22 = (f32[10,4,600]{2,1,0:T(4,128)}, f32[10,4,600]{2,1,0:T(4,128)S(1)}, u32[]{:S(2)}, u32[]{:S(2)}) collective-permute-start(f32[10,4,600]{2,1,0:T(4,128)} %pad_maximum_fusion.23), channel_id=1, source_target_pairs={{0,5},{1,6},{2,7},{3,8},{4,9},{5,10},{6,11},{7,12},{8,13},{9,14},{... | collective-permute-start | bytes 288008 | tf_op jit(solution)/shard_map/ppermute | solution.py:17
  398.8 14.8 %collective-permute-start.23 = (f32[10,4,600]{2,1,0:T(4,128)}, f32[10,4,600]{2,1,0:T(4,128)S(1)}, u32[]{:S(2)}, u32[]{:S(2)}) collective-permute-start(f32[10,4,600]{2,1,0:T(4,128)} %pad_maximum_fusion.23), channel_id=1, source_target_pairs={{0,4},{1,5},{2,6},{3,7},{4,8},{5,9},{6,10},{7,11},{8,12},{9,13},{1... | collective-permute-start | bytes 288008 | tf_op jit(solution)/shard_map/ppermute | solution.py:17
  416.7 13.0 %collective-permute-start.24 = (f32[10,4,600]{2,1,0:T(4,128)}, f32[10,4,600]{2,1,0:T(4,128)S(1)}, u32[]{:S(2)}, u32[]{:S(2)}) collective-permute-start(f32[10,4,600]{2,1,0:T(4,128)} %pad_maximum_fusion.23), channel_id=1, source_target_pairs={{0,3},{1,4},{2,5},{3,6},{4,7},{5,8},{6,9},{7,10},{8,11},{9,12},{10... | collective-permute-start | bytes 288008 | tf_op jit(solution)/shard_map/ppermute | solution.py:17
  434.3 12.5 %collective-permute-start.25 = (f32[10,4,600]{2,1,0:T(4,128)}, f32[10,4,600]{2,1,0:T(4,128)S(1)}, u32[]{:S(2)}, u32[]{:S(2)}) collective-permute-start(f32[10,4,600]{2,1,0:T(4,128)} %pad_maximum_fusion.23), channel_id=1, source_target_pairs={{0,2},{1,3},{2,4},{3,5},{4,6},{5,7},{6,8},{7,9},{8,10},{9,11},{10,... | collective-permute-start | bytes 288008 | tf_op jit(solution)/shard_map/ppermute | solution.py:17
  453.0 11.4 collective-permute-start.26
  470.4 11.1 collective-permute-start.27
  486.1 13.1 %collective-permute-start.28 = (f32[10,4,600]{2,1,0:T(4,128)}, f32[10,4,600]{2,1,0:T(4,128)S(1)}, u32[]{:S(2)}, u32[]{:S(2)}) collective-permute-start(f32[10,4,600]{2,1,0:T(4,128)} %pad_maximum_fusion.23), channel_id=1, source_target_pairs={{2,0},{3,1},{4,2},{5,3},{6,4},{7,5},{8,6},{9,7},{10,8},{11,9},{12,... | collective-permute-start | bytes 288008 | tf_op jit(solution)/shard_map/ppermute | solution.py:17
  505.2 11.7 collective-permute-start.29
  522.7 11.4 collective-permute-start.30
  538.3 11.8 collective-permute-start.31
  556.3 11.5 collective-permute-start.32
  575.6 10.5 collective-permute-start.33
  658.9 10.4 collective-permute-done.41
  706.9 15.2 %collective-permute-done.46 = f32[10,4,600]{2,1,0:T(4,128)S(1)} collective-permute-done((f32[10,4,600]{2,1,0:T(4,128)}, f32[10,4,600]{2,1,0:T(4,128)S(1)}, u32[]{:S(2)}, u32[]{:S(2)}) %collective-permute-start.46) | collective-permute-done | bytes 96032 | tf_op jit(solution)/shard_map/ppermute | solution.py:17
  742.1 11.3 collective-permute-done.49
  770.5 17.4 %collective-permute-done.52 = f32[10,4,600]{2,1,0:T(4,128)S(1)} collective-permute-done((f32[10,4,600]{2,1,0:T(4,128)}, f32[10,4,600]{2,1,0:T(4,128)S(1)}, u32[]{:S(2)}, u32[]{:S(2)}) %collective-permute-start.52) | collective-permute-done | bytes 96032 | tf_op jit(solution)/shard_map/ppermute | solution.py:17
  789.8 10.5 collective-permute-done.53
  828.8 10.2 collective-permute-start.60
  855.3 12.2 collective-permute-start.64
  907.0 13.6 %collective-permute-start.74 = (f32[10,5,600]{2,1,0:T(8,128)S(1)}, f32[10,5,600]{2,1,0:T(8,128)S(1)}, u32[]{:S(2)}, u32[]{:S(2)}) collective-permute-start(f32[10,5,600]{2,1,0:T(8,128)S(1)} %pad_maximum_fusion.22), channel_id=1, source_target_pairs={{0,7},{1,8},{2,9},{3,10},{4,11},{5,12},{6,13},{7,14},{8,15},{9,16}... | collective-permute-start | bytes 360008 | tf_op jit(solution)/shard_map/ppermute | solution.py:17
  921.3 13.1 %collective-permute-start.75 = (f32[10,5,600]{2,1,0:T(8,128)S(1)}, f32[10,5,600]{2,1,0:T(8,128)S(1)}, u32[]{:S(2)}, u32[]{:S(2)}) collective-permute-start(f32[10,5,600]{2,1,0:T(8,128)S(1)} %pad_maximum_fusion.22), channel_id=1, source_target_pairs={{0,6},{1,7},{2,8},{3,9},{4,10},{5,11},{6,12},{7,13},{8,14},{9,15},... | collective-permute-start | bytes 360008 | tf_op jit(solution)/shard_map/ppermute | solution.py:17
  935.2 13.1 %collective-permute-start.76 = (f32[10,5,600]{2,1,0:T(8,128)S(1)}, f32[10,5,600]{2,1,0:T(8,128)S(1)}, u32[]{:S(2)}, u32[]{:S(2)}) collective-permute-start(f32[10,5,600]{2,1,0:T(8,128)S(1)} %pad_maximum_fusion.22), channel_id=1, source_target_pairs={{0,5},{1,6},{2,7},{3,8},{4,9},{5,10},{6,11},{7,12},{8,13},{9,14},{... | collective-permute-start | bytes 360008 | tf_op jit(solution)/shard_map/ppermute | solution.py:17
  949.0 13.1 %collective-permute-start.77 = (f32[10,5,600]{2,1,0:T(8,128)S(1)}, f32[10,5,600]{2,1,0:T(8,128)S(1)}, u32[]{:S(2)}, u32[]{:S(2)}) collective-permute-start(f32[10,5,600]{2,1,0:T(8,128)S(1)} %pad_maximum_fusion.22), channel_id=1, source_target_pairs={{0,4},{1,5},{2,6},{3,7},{4,8},{5,9},{6,10},{7,11},{8,12},{9,13},{1... | collective-permute-start | bytes 360008 | tf_op jit(solution)/shard_map/ppermute | solution.py:17
  962.8 13.1 %collective-permute-start.78 = (f32[10,5,600]{2,1,0:T(8,128)S(1)}, f32[10,5,600]{2,1,0:T(8,128)S(1)}, u32[]{:S(2)}, u32[]{:S(2)}) collective-permute-start(f32[10,5,600]{2,1,0:T(8,128)S(1)} %pad_maximum_fusion.22), channel_id=1, source_target_pairs={{0,3},{1,4},{2,5},{3,6},{4,7},{5,8},{6,9},{7,10},{8,11},{9,12},{10... | collective-permute-start | bytes 360008 | tf_op jit(solution)/shard_map/ppermute | solution.py:17
  976.6 13.1 %collective-permute-start.79 = (f32[10,5,600]{2,1,0:T(8,128)S(1)}, f32[10,5,600]{2,1,0:T(8,128)S(1)}, u32[]{:S(2)}, u32[]{:S(2)}) collective-permute-start(f32[10,5,600]{2,1,0:T(8,128)S(1)} %pad_maximum_fusion.22), channel_id=1, source_target_pairs={{0,2},{1,3},{2,4},{3,5},{4,6},{5,7},{6,8},{7,9},{8,10},{9,11},{10,... | collective-permute-start | bytes 360008 | tf_op jit(solution)/shard_map/ppermute | solution.py:17
  990.5 13.1 %collective-permute-start.80 = (f32[10,5,600]{2,1,0:T(8,128)S(1)}, f32[10,5,600]{2,1,0:T(8,128)S(1)}, u32[]{:S(2)}, u32[]{:S(2)}) collective-permute-start(f32[10,5,600]{2,1,0:T(8,128)S(1)} %pad_maximum_fusion.22), channel_id=1, source_target_pairs={{0,1},{1,2},{2,3},{3,4},{4,5},{5,6},{6,7},{7,8},{8,9},{9,10},{10,1... | collective-permute-start | bytes 360008 | tf_op jit(solution)/shard_map/ppermute | solution.py:17
  1004.3 13.1 %collective-permute-start.81 = (f32[10,5,600]{2,1,0:T(8,128)S(1)}, f32[10,5,600]{2,1,0:T(8,128)S(1)}, u32[]{:S(2)}, u32[]{:S(2)}) collective-permute-start(f32[10,5,600]{2,1,0:T(8,128)S(1)} %pad_maximum_fusion.22), channel_id=1, source_target_pairs={{1,0},{2,1},{3,2},{4,3},{5,4},{6,5},{7,6},{8,7},{9,8},{10,9},{11,1... | collective-permute-start | bytes 360008 | tf_op jit(solution)/shard_map/ppermute | solution.py:17
  1018.1 13.1 %collective-permute-start.82 = (f32[10,5,600]{2,1,0:T(8,128)S(1)}, f32[10,5,600]{2,1,0:T(8,128)S(1)}, u32[]{:S(2)}, u32[]{:S(2)}) collective-permute-start(f32[10,5,600]{2,1,0:T(8,128)S(1)} %pad_maximum_fusion.22), channel_id=1, source_target_pairs={{2,0},{3,1},{4,2},{5,3},{6,4},{7,5},{8,6},{9,7},{10,8},{11,9},{12,... | collective-permute-start | bytes 360008 | tf_op jit(solution)/shard_map/ppermute | solution.py:17
  1031.9 13.1 %collective-permute-start.83 = (f32[10,5,600]{2,1,0:T(8,128)S(1)}, f32[10,5,600]{2,1,0:T(8,128)S(1)}, u32[]{:S(2)}, u32[]{:S(2)}) collective-permute-start(f32[10,5,600]{2,1,0:T(8,128)S(1)} %pad_maximum_fusion.22), channel_id=1, source_target_pairs={{3,0},{4,1},{5,2},{6,3},{7,4},{8,5},{9,6},{10,7},{11,8},{12,9},{13... | collective-permute-start | bytes 360008 | tf_op jit(solution)/shard_map/ppermute | solution.py:17
  1045.7 13.1 %collective-permute-start.84 = (f32[10,5,600]{2,1,0:T(8,128)S(1)}, f32[10,5,600]{2,1,0:T(8,128)S(1)}, u32[]{:S(2)}, u32[]{:S(2)}) collective-permute-start(f32[10,5,600]{2,1,0:T(8,128)S(1)} %pad_maximum_fusion.22), channel_id=1, source_target_pairs={{4,0},{5,1},{6,2},{7,3},{8,4},{9,5},{10,6},{11,7},{12,8},{13,9},{1... | collective-permute-start | bytes 360008 | tf_op jit(solution)/shard_map/ppermute | solution.py:17
  1059.6 12.5 %collective-permute-start.85 = (f32[10,5,600]{2,1,0:T(8,128)S(1)}, f32[10,5,600]{2,1,0:T(8,128)S(1)}, u32[]{:S(2)}, u32[]{:S(2)}) collective-permute-start(f32[10,5,600]{2,1,0:T(8,128)S(1)} %pad_maximum_fusion.22), channel_id=1, source_target_pairs={{5,0},{6,1},{7,2},{8,3},{9,4},{10,5},{11,6},{12,7},{13,8},{14,9},{... | collective-permute-start | bytes 360008 | tf_op jit(solution)/shard_map/ppermute | solution.py:17
  1073.4 13.1 %collective-permute-start.86 = (f32[10,5,600]{2,1,0:T(8,128)S(1)}, f32[10,5,600]{2,1,0:T(8,128)S(1)}, u32[]{:S(2)}, u32[]{:S(2)}) collective-permute-start(f32[10,5,600]{2,1,0:T(8,128)S(1)} %pad_maximum_fusion.22), channel_id=1, source_target_pairs={{6,0},{7,1},{8,2},{9,3},{10,4},{11,5},{12,6},{13,7},{14,8},{15,9},... | collective-permute-start | bytes 360008 | tf_op jit(solution)/shard_map/ppermute | solution.py:17
  1087.2 13.1 %collective-permute-start.87 = (f32[10,5,600]{2,1,0:T(8,128)S(1)}, f32[10,5,600]{2,1,0:T(8,128)S(1)}, u32[]{:S(2)}, u32[]{:S(2)}) collective-permute-start(f32[10,5,600]{2,1,0:T(8,128)S(1)} %pad_maximum_fusion.22), channel_id=1, source_target_pairs={{7,0},{8,1},{9,2},{10,3},{11,4},{12,5},{13,6},{14,7},{15,8},{16,9}... | collective-permute-start | bytes 360008 | tf_op jit(solution)/shard_map/ppermute | solution.py:17
  1112.2 14.6 %collective-permute-done.88 = f32[10,5,600]{2,1,0:T(8,128)S(1)} collective-permute-done((f32[10,5,600]{2,1,0:T(8,128)S(1)}, f32[10,5,600]{2,1,0:T(8,128)S(1)}, u32[]{:S(2)}, u32[]{:S(2)}) %collective-permute-start.88) | collective-permute-done | bytes 120032 | tf_op jit(solution)/shard_map/ppermute | solution.py:17
  1149.0 14.2 %collective-permute-done.96 = f32[10,5,600]{2,1,0:T(8,128)S(1)} collective-permute-done((f32[10,5,600]{2,1,0:T(8,128)S(1)}, f32[10,5,600]{2,1,0:T(8,128)S(1)}, u32[]{:S(2)}, u32[]{:S(2)}) %collective-permute-start.96) | collective-permute-done | bytes 120032 | tf_op jit(solution)/shard_map/ppermute | solution.py:17
  1188.4 19.0 %collective-permute-done.104 = f32[10,5,600]{2,1,0:T(8,128)S(1)} collective-permute-done((f32[10,5,600]{2,1,0:T(8,128)S(1)}, f32[10,5,600]{2,1,0:T(8,128)S(1)}, u32[]{:S(2)}, u32[]{:S(2)}) %collective-permute-start.104) | collective-permute-done | bytes 120032 | tf_op jit(solution)/shard_map/ppermute | solution.py:17
  (391 shorter events, 578.6 us)
Async XLA Ops:
  16.1 804.3 %collective-permute-start.54 = (f32[10,5,600]{2,1,0:T(8,128)S(1)}, f32[10,5,600]{2,1,0:T(8,128)}, u32[]{:S(2)}, u32[]{:S(2)}) collective-permute-start(f32[10,5,600]{2,1,0:T(8,128)S(1)} %pad_maximum_fusion.22), channel_id=1, source_target_pairs={{0,27},{1,28},{2,29},{3,30},{4,31},{5,32},{6,33},{7,34},{8,35},{9,... | collective-permute-start | bytes 360008 | tf_op jit(solution)/shard_map/ppermute | solution.py:17
  31.8 797.0 %collective-permute-start.55 = (f32[10,5,600]{2,1,0:T(8,128)S(1)}, f32[10,5,600]{2,1,0:T(8,128)}, u32[]{:S(2)}, u32[]{:S(2)}) collective-permute-start(f32[10,5,600]{2,1,0:T(8,128)S(1)} %pad_maximum_fusion.22), channel_id=1, source_target_pairs={{0,26},{1,27},{2,28},{3,29},{4,30},{5,31},{6,32},{7,33},{8,34},{9,... | collective-permute-start | bytes 360008 | tf_op jit(solution)/shard_map/ppermute | solution.py:17
  44.9 795.7 %collective-permute-start.56 = (f32[10,5,600]{2,1,0:T(8,128)S(1)}, f32[10,5,600]{2,1,0:T(8,128)}, u32[]{:S(2)}, u32[]{:S(2)}) collective-permute-start(f32[10,5,600]{2,1,0:T(8,128)S(1)} %pad_maximum_fusion.22), channel_id=1, source_target_pairs={{0,25},{1,26},{2,27},{3,28},{4,29},{5,30},{6,31},{7,32},{8,33},{9,... | collective-permute-start | bytes 360008 | tf_op jit(solution)/shard_map/ppermute | solution.py:17
  58.1 785.5 %collective-permute-start.57 = (f32[10,5,600]{2,1,0:T(8,128)S(1)}, f32[10,5,600]{2,1,0:T(8,128)}, u32[]{:S(2)}, u32[]{:S(2)}) collective-permute-start(f32[10,5,600]{2,1,0:T(8,128)S(1)} %pad_maximum_fusion.22), channel_id=1, source_target_pairs={{0,24},{1,25},{2,26},{3,27},{4,28},{5,29},{6,30},{7,31},{8,32},{9,... | collective-permute-start | bytes 360008 | tf_op jit(solution)/shard_map/ppermute | solution.py:17
  83.6 37.3 %collective-permute-start = (f32[10,4,600]{2,1,0:T(4,128)}, f32[10,4,600]{2,1,0:T(4,128)}, u32[]{:S(2)}, u32[]{:S(2)}) collective-permute-start(f32[10,4,600]{2,1,0:T(4,128)} %pad_maximum_fusion.23), channel_id=1, source_target_pairs={{0,27},{1,28},{2,29},{3,30},{4,31},{5,32},{6,33},{7,34},{8,35},{9,... | collective-permute-start | bytes 288008 | tf_op jit(solution)/shard_map/ppermute | solution.py:17
  321.9 42.1 %collective-permute-start.20 = (f32[10,4,600]{2,1,0:T(4,128)}, f32[10,4,600]{2,1,0:T(4,128)S(1)}, u32[]{:S(2)}, u32[]{:S(2)}) collective-permute-start(f32[10,4,600]{2,1,0:T(4,128)} %pad_maximum_fusion.23), channel_id=1, source_target_pairs={{0,7},{1,8},{2,9},{3,10},{4,11},{5,12},{6,13},{7,14},{8,15},{9,16}... | collective-permute-start | bytes 288008 | tf_op jit(solution)/shard_map/ppermute | solution.py:17
  800.4 48.7 %collective-permute-start.58 = (f32[10,5,600]{2,1,0:T(8,128)S(1)}, f32[10,5,600]{2,1,0:T(8,128)}, u32[]{:S(2)}, u32[]{:S(2)}) collective-permute-start(f32[10,5,600]{2,1,0:T(8,128)S(1)} %pad_maximum_fusion.22), channel_id=1, source_target_pairs={{0,23},{1,24},{2,25},{3,26},{4,27},{5,28},{6,29},{7,30},{8,31},{9,... | collective-permute-start | bytes 360008 | tf_op jit(solution)/shard_map/ppermute | solution.py:17
  820.4 34.9 %collective-permute-start.59 = (f32[10,5,600]{2,1,0:T(8,128)S(1)}, f32[10,5,600]{2,1,0:T(8,128)S(1)}, u32[]{:S(2)}, u32[]{:S(2)}) collective-permute-start(f32[10,5,600]{2,1,0:T(8,128)S(1)} %pad_maximum_fusion.22), channel_id=1, source_target_pairs={{0,22},{1,23},{2,24},{3,25},{4,26},{5,27},{6,28},{7,29},{8,30},{9,... | collective-permute-start | bytes 360008 | tf_op jit(solution)/shard_map/ppermute | solution.py:17
  828.8 39.4 %collective-permute-start.60 = (f32[10,5,600]{2,1,0:T(8,128)S(1)}, f32[10,5,600]{2,1,0:T(8,128)S(1)}, u32[]{:S(2)}, u32[]{:S(2)}) collective-permute-start(f32[10,5,600]{2,1,0:T(8,128)S(1)} %pad_maximum_fusion.22), channel_id=1, source_target_pairs={{0,21},{1,22},{2,23},{3,24},{4,25},{5,26},{6,27},{7,28},{8,29},{9,... | collective-permute-start | bytes 360008 | tf_op jit(solution)/shard_map/ppermute | solution.py:17
  840.6 31.2 %collective-permute-start.61 = (f32[10,5,600]{2,1,0:T(8,128)S(1)}, f32[10,5,600]{2,1,0:T(8,128)S(1)}, u32[]{:S(2)}, u32[]{:S(2)}) collective-permute-start(f32[10,5,600]{2,1,0:T(8,128)S(1)} %pad_maximum_fusion.22), channel_id=1, source_target_pairs={{0,20},{1,21},{2,22},{3,23},{4,24},{5,25},{6,26},{7,27},{8,28},{9,... | collective-permute-start | bytes 360008 | tf_op jit(solution)/shard_map/ppermute | solution.py:17
  843.6 33.2 %collective-permute-start.62 = (f32[10,5,600]{2,1,0:T(8,128)S(1)}, f32[10,5,600]{2,1,0:T(8,128)S(1)}, u32[]{:S(2)}, u32[]{:S(2)}) collective-permute-start(f32[10,5,600]{2,1,0:T(8,128)S(1)} %pad_maximum_fusion.22), channel_id=1, source_target_pairs={{0,19},{1,20},{2,21},{3,22},{4,23},{5,24},{6,25},{7,26},{8,27},{9,... | collective-permute-start | bytes 360008 | tf_op jit(solution)/shard_map/ppermute | solution.py:17
  849.0 32.1 %collective-permute-start.63 = (f32[10,5,600]{2,1,0:T(8,128)S(1)}, f32[10,5,600]{2,1,0:T(8,128)S(1)}, u32[]{:S(2)}, u32[]{:S(2)}) collective-permute-start(f32[10,5,600]{2,1,0:T(8,128)S(1)} %pad_maximum_fusion.22), channel_id=1, source_target_pairs={{0,18},{1,19},{2,20},{3,21},{4,22},{5,23},{6,24},{7,25},{8,26},{9,... | collective-permute-start | bytes 360008 | tf_op jit(solution)/shard_map/ppermute | solution.py:17
  855.3 27.9 %collective-permute-start.64 = (f32[10,5,600]{2,1,0:T(8,128)S(1)}, f32[10,5,600]{2,1,0:T(8,128)S(1)}, u32[]{:S(2)}, u32[]{:S(2)}) collective-permute-start(f32[10,5,600]{2,1,0:T(8,128)S(1)} %pad_maximum_fusion.22), channel_id=1, source_target_pairs={{0,17},{1,18},{2,19},{3,20},{4,21},{5,22},{6,23},{7,24},{8,25},{9,... | collective-permute-start | bytes 360008 | tf_op jit(solution)/shard_map/ppermute | solution.py:17
  868.2 22.7 %collective-permute-start.65 = (f32[10,5,600]{2,1,0:T(8,128)S(1)}, f32[10,5,600]{2,1,0:T(8,128)S(1)}, u32[]{:S(2)}, u32[]{:S(2)}) collective-permute-start(f32[10,5,600]{2,1,0:T(8,128)S(1)} %pad_maximum_fusion.22), channel_id=1, source_target_pairs={{0,16},{1,17},{2,18},{3,19},{4,20},{5,21},{6,22},{7,23},{8,24},{9,... | collective-permute-start | bytes 360008 | tf_op jit(solution)/shard_map/ppermute | solution.py:17
  881.2 22.0 %collective-permute-start.68 = (f32[10,5,600]{2,1,0:T(8,128)S(1)}, f32[10,5,600]{2,1,0:T(8,128)S(1)}, u32[]{:S(2)}, u32[]{:S(2)}) collective-permute-start(f32[10,5,600]{2,1,0:T(8,128)S(1)} %pad_maximum_fusion.22), channel_id=1, source_target_pairs={{0,13},{1,14},{2,15},{3,16},{4,17},{5,18},{6,19},{7,20},{8,21},{9,... | collective-permute-start | bytes 360008 | tf_op jit(solution)/shard_map/ppermute | solution.py:17
  883.2 23.8 %collective-permute-start.69 = (f32[10,5,600]{2,1,0:T(8,128)S(1)}, f32[10,5,600]{2,1,0:T(8,128)S(1)}, u32[]{:S(2)}, u32[]{:S(2)}) collective-permute-start(f32[10,5,600]{2,1,0:T(8,128)S(1)} %pad_maximum_fusion.22), channel_id=1, source_target_pairs={{0,12},{1,13},{2,14},{3,15},{4,16},{5,17},{6,18},{7,19},{8,20},{9,... | collective-permute-start | bytes 360008 | tf_op jit(solution)/shard_map/ppermute | solution.py:17
  890.9 30.4 %collective-permute-start.70 = (f32[10,5,600]{2,1,0:T(8,128)S(1)}, f32[10,5,600]{2,1,0:T(8,128)S(1)}, u32[]{:S(2)}, u32[]{:S(2)}) collective-permute-start(f32[10,5,600]{2,1,0:T(8,128)S(1)} %pad_maximum_fusion.22), channel_id=1, source_target_pairs={{0,11},{1,12},{2,13},{3,14},{4,15},{5,16},{6,17},{7,18},{8,19},{9,... | collective-permute-start | bytes 360008 | tf_op jit(solution)/shard_map/ppermute | solution.py:17
  892.9 42.3 %collective-permute-start.71 = (f32[10,5,600]{2,1,0:T(8,128)S(1)}, f32[10,5,600]{2,1,0:T(8,128)S(1)}, u32[]{:S(2)}, u32[]{:S(2)}) collective-permute-start(f32[10,5,600]{2,1,0:T(8,128)S(1)} %pad_maximum_fusion.22), channel_id=1, source_target_pairs={{0,10},{1,11},{2,12},{3,13},{4,14},{5,15},{6,16},{7,17},{8,18},{9,... | collective-permute-start | bytes 360008 | tf_op jit(solution)/shard_map/ppermute | solution.py:17
  897.2 51.8 %collective-permute-start.72 = (f32[10,5,600]{2,1,0:T(8,128)S(1)}, f32[10,5,600]{2,1,0:T(8,128)S(1)}, u32[]{:S(2)}, u32[]{:S(2)}) collective-permute-start(f32[10,5,600]{2,1,0:T(8,128)S(1)} %pad_maximum_fusion.22), channel_id=1, source_target_pairs={{0,9},{1,10},{2,11},{3,12},{4,13},{5,14},{6,15},{7,16},{8,17},{9,1... | collective-permute-start | bytes 360008 | tf_op jit(solution)/shard_map/ppermute | solution.py:17
  903.1 59.7 %collective-permute-start.73 = (f32[10,5,600]{2,1,0:T(8,128)S(1)}, f32[10,5,600]{2,1,0:T(8,128)S(1)}, u32[]{:S(2)}, u32[]{:S(2)}) collective-permute-start(f32[10,5,600]{2,1,0:T(8,128)S(1)} %pad_maximum_fusion.22), channel_id=1, source_target_pairs={{0,8},{1,9},{2,10},{3,11},{4,12},{5,13},{6,14},{7,15},{8,16},{9,17... | collective-permute-start | bytes 360008 | tf_op jit(solution)/shard_map/ppermute | solution.py:17
  907.0 69.6 %collective-permute-start.74 = (f32[10,5,600]{2,1,0:T(8,128)S(1)}, f32[10,5,600]{2,1,0:T(8,128)S(1)}, u32[]{:S(2)}, u32[]{:S(2)}) collective-permute-start(f32[10,5,600]{2,1,0:T(8,128)S(1)} %pad_maximum_fusion.22), channel_id=1, source_target_pairs={{0,7},{1,8},{2,9},{3,10},{4,11},{5,12},{6,13},{7,14},{8,15},{9,16}... | collective-permute-start | bytes 360008 | tf_op jit(solution)/shard_map/ppermute | solution.py:17
  921.3 69.1 %collective-permute-start.75 = (f32[10,5,600]{2,1,0:T(8,128)S(1)}, f32[10,5,600]{2,1,0:T(8,128)S(1)}, u32[]{:S(2)}, u32[]{:S(2)}) collective-permute-start(f32[10,5,600]{2,1,0:T(8,128)S(1)} %pad_maximum_fusion.22), channel_id=1, source_target_pairs={{0,6},{1,7},{2,8},{3,9},{4,10},{5,11},{6,12},{7,13},{8,14},{9,15},... | collective-permute-start | bytes 360008 | tf_op jit(solution)/shard_map/ppermute | solution.py:17
  935.2 69.1 %collective-permute-start.76 = (f32[10,5,600]{2,1,0:T(8,128)S(1)}, f32[10,5,600]{2,1,0:T(8,128)S(1)}, u32[]{:S(2)}, u32[]{:S(2)}) collective-permute-start(f32[10,5,600]{2,1,0:T(8,128)S(1)} %pad_maximum_fusion.22), channel_id=1, source_target_pairs={{0,5},{1,6},{2,7},{3,8},{4,9},{5,10},{6,11},{7,12},{8,13},{9,14},{... | collective-permute-start | bytes 360008 | tf_op jit(solution)/shard_map/ppermute | solution.py:17
  949.0 69.1 %collective-permute-start.77 = (f32[10,5,600]{2,1,0:T(8,128)S(1)}, f32[10,5,600]{2,1,0:T(8,128)S(1)}, u32[]{:S(2)}, u32[]{:S(2)}) collective-permute-start(f32[10,5,600]{2,1,0:T(8,128)S(1)} %pad_maximum_fusion.22), channel_id=1, source_target_pairs={{0,4},{1,5},{2,6},{3,7},{4,8},{5,9},{6,10},{7,11},{8,12},{9,13},{1... | collective-permute-start | bytes 360008 | tf_op jit(solution)/shard_map/ppermute | solution.py:17
  962.8 69.1 %collective-permute-start.78 = (f32[10,5,600]{2,1,0:T(8,128)S(1)}, f32[10,5,600]{2,1,0:T(8,128)S(1)}, u32[]{:S(2)}, u32[]{:S(2)}) collective-permute-start(f32[10,5,600]{2,1,0:T(8,128)S(1)} %pad_maximum_fusion.22), channel_id=1, source_target_pairs={{0,3},{1,4},{2,5},{3,6},{4,7},{5,8},{6,9},{7,10},{8,11},{9,12},{10... | collective-permute-start | bytes 360008 | tf_op jit(solution)/shard_map/ppermute | solution.py:17
  976.6 69.1 %collective-permute-start.79 = (f32[10,5,600]{2,1,0:T(8,128)S(1)}, f32[10,5,600]{2,1,0:T(8,128)S(1)}, u32[]{:S(2)}, u32[]{:S(2)}) collective-permute-start(f32[10,5,600]{2,1,0:T(8,128)S(1)} %pad_maximum_fusion.22), channel_id=1, source_target_pairs={{0,2},{1,3},{2,4},{3,5},{4,6},{5,7},{6,8},{7,9},{8,10},{9,11},{10,... | collective-permute-start | bytes 360008 | tf_op jit(solution)/shard_map/ppermute | solution.py:17
  990.5 69.1 %collective-permute-start.80 = (f32[10,5,600]{2,1,0:T(8,128)S(1)}, f32[10,5,600]{2,1,0:T(8,128)S(1)}, u32[]{:S(2)}, u32[]{:S(2)}) collective-permute-start(f32[10,5,600]{2,1,0:T(8,128)S(1)} %pad_maximum_fusion.22), channel_id=1, source_target_pairs={{0,1},{1,2},{2,3},{3,4},{4,5},{5,6},{6,7},{7,8},{8,9},{9,10},{10,1... | collective-permute-start | bytes 360008 | tf_op jit(solution)/shard_map/ppermute | solution.py:17
  1004.3 69.2 %collective-permute-start.81 = (f32[10,5,600]{2,1,0:T(8,128)S(1)}, f32[10,5,600]{2,1,0:T(8,128)S(1)}, u32[]{:S(2)}, u32[]{:S(2)}) collective-permute-start(f32[10,5,600]{2,1,0:T(8,128)S(1)} %pad_maximum_fusion.22), channel_id=1, source_target_pairs={{1,0},{2,1},{3,2},{4,3},{5,4},{6,5},{7,6},{8,7},{9,8},{10,9},{11,1... | collective-permute-start | bytes 360008 | tf_op jit(solution)/shard_map/ppermute | solution.py:17
  1018.1 69.2 %collective-permute-start.82 = (f32[10,5,600]{2,1,0:T(8,128)S(1)}, f32[10,5,600]{2,1,0:T(8,128)S(1)}, u32[]{:S(2)}, u32[]{:S(2)}) collective-permute-start(f32[10,5,600]{2,1,0:T(8,128)S(1)} %pad_maximum_fusion.22), channel_id=1, source_target_pairs={{2,0},{3,1},{4,2},{5,3},{6,4},{7,5},{8,6},{9,7},{10,8},{11,9},{12,... | collective-permute-start | bytes 360008 | tf_op jit(solution)/shard_map/ppermute | solution.py:17
  1031.9 69.2 %collective-permute-start.83 = (f32[10,5,600]{2,1,0:T(8,128)S(1)}, f32[10,5,600]{2,1,0:T(8,128)S(1)}, u32[]{:S(2)}, u32[]{:S(2)}) collective-permute-start(f32[10,5,600]{2,1,0:T(8,128)S(1)} %pad_maximum_fusion.22), channel_id=1, source_target_pairs={{3,0},{4,1},{5,2},{6,3},{7,4},{8,5},{9,6},{10,7},{11,8},{12,9},{13... | collective-permute-start | bytes 360008 | tf_op jit(solution)/shard_map/ppermute | solution.py:17
  1045.7 57.3 %collective-permute-start.84 = (f32[10,5,600]{2,1,0:T(8,128)S(1)}, f32[10,5,600]{2,1,0:T(8,128)S(1)}, u32[]{:S(2)}, u32[]{:S(2)}) collective-permute-start(f32[10,5,600]{2,1,0:T(8,128)S(1)} %pad_maximum_fusion.22), channel_id=1, source_target_pairs={{4,0},{5,1},{6,2},{7,3},{8,4},{9,5},{10,6},{11,7},{12,8},{13,9},{1... | collective-permute-start | bytes 360008 | tf_op jit(solution)/shard_map/ppermute | solution.py:17
  1059.6 45.5 %collective-permute-start.85 = (f32[10,5,600]{2,1,0:T(8,128)S(1)}, f32[10,5,600]{2,1,0:T(8,128)S(1)}, u32[]{:S(2)}, u32[]{:S(2)}) collective-permute-start(f32[10,5,600]{2,1,0:T(8,128)S(1)} %pad_maximum_fusion.22), channel_id=1, source_target_pairs={{5,0},{6,1},{7,2},{8,3},{9,4},{10,5},{11,6},{12,7},{13,8},{14,9},{... | collective-permute-start | bytes 360008 | tf_op jit(solution)/shard_map/ppermute | solution.py:17
  1073.4 33.6 %collective-permute-start.86 = (f32[10,5,600]{2,1,0:T(8,128)S(1)}, f32[10,5,600]{2,1,0:T(8,128)S(1)}, u32[]{:S(2)}, u32[]{:S(2)}) collective-permute-start(f32[10,5,600]{2,1,0:T(8,128)S(1)} %pad_maximum_fusion.22), channel_id=1, source_target_pairs={{6,0},{7,1},{8,2},{9,3},{10,4},{11,5},{12,6},{13,7},{14,8},{15,9},... | collective-permute-start | bytes 360008 | tf_op jit(solution)/shard_map/ppermute | solution.py:17
  1087.2 22.9 %collective-permute-start.87 = (f32[10,5,600]{2,1,0:T(8,128)S(1)}, f32[10,5,600]{2,1,0:T(8,128)S(1)}, u32[]{:S(2)}, u32[]{:S(2)}) collective-permute-start(f32[10,5,600]{2,1,0:T(8,128)S(1)} %pad_maximum_fusion.22), channel_id=1, source_target_pairs={{7,0},{8,1},{9,2},{10,3},{11,4},{12,5},{13,6},{14,7},{15,8},{16,9}... | collective-permute-start | bytes 360008 | tf_op jit(solution)/shard_map/ppermute | solution.py:17
  1101.1 25.7 %collective-permute-start.88 = (f32[10,5,600]{2,1,0:T(8,128)S(1)}, f32[10,5,600]{2,1,0:T(8,128)S(1)}, u32[]{:S(2)}, u32[]{:S(2)}) collective-permute-start(f32[10,5,600]{2,1,0:T(8,128)S(1)} %pad_maximum_fusion.22), channel_id=1, source_target_pairs={{8,0},{9,1},{10,2},{11,3},{12,4},{13,5},{14,6},{15,7},{16,8},{17,9... | collective-permute-start | bytes 360008 | tf_op jit(solution)/shard_map/ppermute | solution.py:17
  1103.1 25.7 %collective-permute-start.89 = (f32[10,5,600]{2,1,0:T(8,128)S(1)}, f32[10,5,600]{2,1,0:T(8,128)S(1)}, u32[]{:S(2)}, u32[]{:S(2)}) collective-permute-start(f32[10,5,600]{2,1,0:T(8,128)S(1)} %pad_maximum_fusion.22), channel_id=1, source_target_pairs={{9,0},{10,1},{11,2},{12,3},{13,4},{14,5},{15,6},{16,7},{17,8},{18,... | collective-permute-start | bytes 360008 | tf_op jit(solution)/shard_map/ppermute | solution.py:17
  1105.1 25.7 %collective-permute-start.90 = (f32[10,5,600]{2,1,0:T(8,128)S(1)}, f32[10,5,600]{2,1,0:T(8,128)S(1)}, u32[]{:S(2)}, u32[]{:S(2)}) collective-permute-start(f32[10,5,600]{2,1,0:T(8,128)S(1)} %pad_maximum_fusion.22), channel_id=1, source_target_pairs={{10,0},{11,1},{12,2},{13,3},{14,4},{15,5},{16,6},{17,7},{18,8},{19... | collective-permute-start | bytes 360008 | tf_op jit(solution)/shard_map/ppermute | solution.py:17
  1107.1 25.7 %collective-permute-start.91 = (f32[10,5,600]{2,1,0:T(8,128)S(1)}, f32[10,5,600]{2,1,0:T(8,128)S(1)}, u32[]{:S(2)}, u32[]{:S(2)}) collective-permute-start(f32[10,5,600]{2,1,0:T(8,128)S(1)} %pad_maximum_fusion.22), channel_id=1, source_target_pairs={{11,0},{12,1},{13,2},{14,3},{15,4},{16,5},{17,6},{18,7},{19,8},{20... | collective-permute-start | bytes 360008 | tf_op jit(solution)/shard_map/ppermute | solution.py:17
  1110.2 24.6 %collective-permute-start.92 = (f32[10,5,600]{2,1,0:T(8,128)S(1)}, f32[10,5,600]{2,1,0:T(8,128)S(1)}, u32[]{:S(2)}, u32[]{:S(2)}) collective-permute-start(f32[10,5,600]{2,1,0:T(8,128)S(1)} %pad_maximum_fusion.22), channel_id=1, source_target_pairs={{12,0},{13,1},{14,2},{15,3},{16,4},{17,5},{18,6},{19,7},{20,8},{21... | collective-permute-start | bytes 360008 | tf_op jit(solution)/shard_map/ppermute | solution.py:17
  1132.7 30.5 %collective-permute-start.96 = (f32[10,5,600]{2,1,0:T(8,128)S(1)}, f32[10,5,600]{2,1,0:T(8,128)S(1)}, u32[]{:S(2)}, u32[]{:S(2)}) collective-permute-start(f32[10,5,600]{2,1,0:T(8,128)S(1)} %pad_maximum_fusion.22), channel_id=1, source_target_pairs={{16,0},{17,1},{18,2},{19,3},{20,4},{21,5},{22,6},{23,7},{24,8},{25... | collective-permute-start | bytes 360008 | tf_op jit(solution)/shard_map/ppermute | solution.py:17
  1134.7 30.5 %collective-permute-start.97 = (f32[10,5,600]{2,1,0:T(8,128)S(1)}, f32[10,5,600]{2,1,0:T(8,128)S(1)}, u32[]{:S(2)}, u32[]{:S(2)}) collective-permute-start(f32[10,5,600]{2,1,0:T(8,128)S(1)} %pad_maximum_fusion.22), channel_id=1, source_target_pairs={{17,0},{18,1},{19,2},{20,3},{21,4},{22,5},{23,6},{24,7},{25,8},{26... | collective-permute-start | bytes 360008 | tf_op jit(solution)/shard_map/ppermute | solution.py:17
  1138.5 28.7 %collective-permute-start.98 = (f32[10,5,600]{2,1,0:T(8,128)S(1)}, f32[10,5,600]{2,1,0:T(8,128)S(1)}, u32[]{:S(2)}, u32[]{:S(2)}) collective-permute-start(f32[10,5,600]{2,1,0:T(8,128)S(1)} %pad_maximum_fusion.22), channel_id=1, source_target_pairs={{18,0},{19,1},{20,2},{21,3},{22,4},{23,5},{24,6},{25,7},{26,8},{27... | collective-permute-start | bytes 360008 | tf_op jit(solution)/shard_map/ppermute | solution.py:17
  1141.8 27.4 %collective-permute-start.99 = (f32[10,5,600]{2,1,0:T(8,128)S(1)}, f32[10,5,600]{2,1,0:T(8,128)S(1)}, u32[]{:S(2)}, u32[]{:S(2)}) collective-permute-start(f32[10,5,600]{2,1,0:T(8,128)S(1)} %pad_maximum_fusion.22), channel_id=1, source_target_pairs={{19,0},{20,1},{21,2},{22,3},{23,4},{24,5},{25,6},{26,7},{27,8},{28... | collective-permute-start | bytes 360008 | tf_op jit(solution)/shard_map/ppermute | solution.py:17
  1147.0 24.2 %collective-permute-start.100 = (f32[10,5,600]{2,1,0:T(8,128)S(1)}, f32[10,5,600]{2,1,0:T(8,128)S(1)}, u32[]{:S(2)}, u32[]{:S(2)}) collective-permute-start(f32[10,5,600]{2,1,0:T(8,128)S(1)} %pad_maximum_fusion.22), channel_id=1, source_target_pairs={{20,0},{21,1},{22,2},{23,3},{24,4},{25,5},{26,6},{27,7},{28,8},{29... | collective-permute-start | bytes 360008 | tf_op jit(solution)/shard_map/ppermute | solution.py:17
  1169.2 38.2 %collective-permute-start.104 = (f32[10,5,600]{2,1,0:T(8,128)S(1)}, f32[10,5,600]{2,1,0:T(8,128)S(1)}, u32[]{:S(2)}, u32[]{:S(2)}) collective-permute-start(f32[10,5,600]{2,1,0:T(8,128)S(1)} %pad_maximum_fusion.22), channel_id=1, source_target_pairs={{24,0},{25,1},{26,2},{27,3},{28,4},{29,5},{30,6},{31,7},{32,8},{33... | collective-permute-start | bytes 360008 | tf_op jit(solution)/shard_map/ppermute | solution.py:17
  1171.2 36.9 %collective-permute-start.105 = (f32[10,5,600]{2,1,0:T(8,128)S(1)}, f32[10,5,600]{2,1,0:T(8,128)S(1)}, u32[]{:S(2)}, u32[]{:S(2)}) collective-permute-start(f32[10,5,600]{2,1,0:T(8,128)S(1)} %pad_maximum_fusion.22), channel_id=1, source_target_pairs={{25,0},{26,1},{27,2},{28,3},{29,4},{30,5},{31,6},{32,7},{33,8},{34... | collective-permute-start | bytes 360008 | tf_op jit(solution)/shard_map/ppermute | solution.py:17
  1173.4 35.4 %collective-permute-start.106 = (f32[10,5,600]{2,1,0:T(8,128)S(1)}, f32[10,5,600]{2,1,0:T(8,128)S(1)}, u32[]{:S(2)}, u32[]{:S(2)}) collective-permute-start(f32[10,5,600]{2,1,0:T(8,128)S(1)} %pad_maximum_fusion.22), channel_id=1, source_target_pairs={{26,0},{27,1},{28,2},{29,3},{30,4},{31,5},{32,6},{33,7},{34,8},{35... | collective-permute-start | bytes 360008 | tf_op jit(solution)/shard_map/ppermute | solution.py:17
  1182.7 26.8 %collective-permute-start.107 = (f32[10,5,600]{2,1,0:T(8,128)S(1)}, f32[10,5,600]{2,1,0:T(8,128)S(1)}, u32[]{:S(2)}, u32[]{:S(2)}) collective-permute-start(f32[10,5,600]{2,1,0:T(8,128)S(1)} %pad_maximum_fusion.22), channel_id=1, source_target_pairs={{27,0},{28,1},{29,2},{30,3},{31,4},{32,5},{33,6},{34,7},{35,8},{36... | collective-permute-start | bytes 360008 | tf_op jit(solution)/shard_map/ppermute | solution.py:17
  (69 other events, 1103.5 us)
where the time goes:
time: 1260 us; the launch traced here: 1240 us
  starting transfers between devices  742 us (59%)
  waiting for transfers between devices  321 us (25%)
  local copies, waits for them, and re-layouts  160 us (13%)
  other arithmetic  18.8 us (1%)
    ppermute x108, starting transfers between devices, shifted(): return lax.ppermute(block, axis, route)  742 us
    ppermute x108, waiting for transfers between devices, shifted(): return lax.ppermute(block, axis, route)  321 us
    unnamed x127, local copies, waits for them, and re-layouts  81.1 us
  transfers between devices with their start and end apart: 108, of which 64 were waited for; matrix products, arithmetic and copies ran while one was open for 10% of the time, Pallas kernels for 0%

commit v1 on v0

v1 whole, which is shorter than its diff:
```python
import jax
import jax.numpy as jnp
from jax import lax
from jax.experimental import pallas as pl
from jax.experimental.pallas import tpu as pltpu
from jax.sharding import PartitionSpec as P

IB = 90
JB = 60
SLOTS = 10
COURANT = 0.2
GROUP = 8
FAR = 3
ROWS = 112
LANES = 128
EAST_LANE = 64
MESH = pl.DeviceIdType.MESH


def padded(parts, lane_parts):
    rows = jnp.concatenate(parts, axis=0)
    return jnp.pad(rows, ((0, ROWS - rows.shape[0]), (0, lane_parts - rows.shape[1])))


def edge_packs(tracers, velocity, kmt):
    def rows_at(near, far):
        def cut(field, row):
            piece = field[..., row * IB : (row + 1) * IB]
            return piece.reshape(-1, IB)

        return padded(
            [cut(tracers, near), cut(tracers, far), cut(velocity[:, 2:4], near), cut(kmt, near)], LANES
        )

    def columns_at(near, far):
        def cut(field, column):
            piece = field.reshape(field.shape[:-1] + (JB, IB))[..., column]
            return piece.reshape(-1, JB)

        return padded(
            [cut(tracers, near), cut(tracers, far), cut(velocity[:, 0:2], near), cut(kmt, near)], EAST_LANE
        )

    south = rows_at(0, 1)
    north = rows_at(JB - 1, JB - 2)
    sides = jnp.concatenate([columns_at(0, 1), columns_at(IB - 1, IB - 2)], axis=1)
    return jnp.stack([south, north, sides])


def link_table(me, total, block_owner, neighbours, fold_partner):
    slots = (me - GROUP // 2) * SLOTS + jnp.arange(GROUP * SLOTS, dtype=jnp.int32)
    slots = jnp.mod(slots, total * SLOTS)
    hit = slots[:, None] == block_owner[None, :]
    links = jnp.concatenate([neighbours, fold_partner[:, None]], axis=1)
    picked = jnp.sum(jnp.where(hit[:, :, None], links[None] + 1, 0), axis=1) - 1
    ids = jnp.arange(block_owner.shape[0], dtype=jnp.int32)
    same = picked[:, :, None] == ids
    codes = jnp.sum(jnp.where(same, block_owner + 1, 0), axis=2) - 1
    away = jnp.mod(codes // SLOTS - me + GROUP * FAR, total)
    usable = (codes >= 0) & (away % GROUP == 0) & (away >= 0) & (away <= 2 * GROUP * FAR)
    source = jnp.where(usable, away // GROUP * SLOTS + codes % SLOTS, -1)
    live = jnp.any(hit, axis=1)
    return source, live


def pick(hot, packed):
    count = packed.shape[0]
    lanes = packed.shape[-1]

    def one(start, chans):
        rows = packed[:, start : start + SLOTS * chans].reshape(count * SLOTS, chans, lanes)
        out = jnp.einsum("xy,ycl->xcl", hot, rows, precision=lax.Precision.HIGHEST)
        return out.reshape(GROUP, SLOTS * chans, lanes)

    return jnp.concatenate([one(0, 4), one(40, 4), one(80, 2), one(100, 1)], axis=1)


def choose(source, window):
    hot = (source[:, :, None] == jnp.arange((2 * FAR + 1) * SLOTS)).astype(jnp.float32)
    south_edge, north_edge, sides = window[:, 0], window[:, 1], window[:, 2]
    south = pick(hot[:, 2], north_edge)
    north = pick(hot[:, 3], south_edge)
    mirrored = pick(hot[:, 4], north_edge)[:, :, IB - 1 :: -1]
    sign = jnp.where((jnp.arange(110) >= 80) & (jnp.arange(110) < 100), -1.0, 1.0)
    mirrored = mirrored * sign[:, None]
    north = north + jnp.pad(mirrored, ((0, 0), (0, 0), (0, LANES - IB)))
    west = pick(hot[:, 0], sides[:, :, EAST_LANE:])
    east = pick(hot[:, 1], sides[:, :, :EAST_LANE])
    out = jnp.stack([south, north, jnp.concatenate([west, east], axis=2)], axis=1)
    return jnp.pad(out, ((0, 0), (0, 0), (0, ROWS - 110), (0, 0)))


def coordinates(index, total):
    index = lax.rem(index + total, total)
    return (index // 4, lax.rem(index, 4))


def greet(offsets, me, total):
    barrier = pltpu.get_barrier_semaphore()
    for offset in offsets:
        pl.semaphore_signal(barrier, inc=1, device_id=coordinates(me + offset, total), device_id_type=MESH)
    pl.semaphore_wait(barrier, len(offsets))


def far_kernel(total, pack_ref, out_ref, send_sem, recv_sem, own_sem):
    me = lax.axis_index("blk") * 4 + lax.axis_index("sub")
    steps = [e for e in range(-FAR, FAR + 1) if e != 0]
    own = pltpu.make_async_copy(pack_ref, out_ref.at[FAR], own_sem)
    own.start()
    greet([GROUP * e for e in steps], me, total)
    copies = []
    for e in steps:
        copy = pltpu.make_async_remote_copy(
            src_ref=pack_ref,
            dst_ref=out_ref.at[FAR - e],
            send_sem=send_sem.at[FAR - e],
            recv_sem=recv_sem.at[FAR - e],
            device_id=coordinates(me + GROUP * e, total),
            device_id_type=MESH,
        )
        copy.start()
        copies.append(copy)
    own.wait()
    for copy in copies:
        copy.wait()


def near_kernel(total, message_ref, out_ref, send_sem, recv_sem, own_sem):
    me = lax.axis_index("blk") * 4 + lax.axis_index("sub")
    half = GROUP // 2
    own = pltpu.make_async_copy(message_ref.at[half], out_ref.at[half], own_sem)
    own.start()
    greet([c for c in range(-half, half + 1) if c != 0], me, total)
    copies = []
    for c in range(-half, half):
        if c == 0:
            continue
        copy = pltpu.make_async_remote_copy(
            src_ref=message_ref.at[c + half],
            dst_ref=out_ref.at[c + half],
            send_sem=send_sem.at[c + half],
            recv_sem=recv_sem.at[c + half],
            device_id=coordinates(me + c, total),
            device_id_type=MESH,
        )
        copy.start()
        copies.append(copy)
    own.wait()
    for copy in copies:
        copy.wait()


def exchange(kernel, data, count, ident, total):
    return pl.pallas_call(
        lambda *refs: kernel(total, *refs),
        out_shape=jax.ShapeDtypeStruct((count,) + data.shape[-3:], jnp.float32),
        in_specs=[pl.BlockSpec(memory_space=pl.ANY)],
        out_specs=pl.BlockSpec(memory_space=pl.ANY),
        scratch_shapes=[
            pltpu.SemaphoreType.DMA((count,)),
            pltpu.SemaphoreType.DMA((count,)),
            pltpu.SemaphoreType.DMA,
        ],
        compiler_params=pltpu.CompilerParams(collective_id=ident, has_side_effects=True),
    )(data)


def finish(tracers, velocity, kappa, kmt, halos, live):
    def rows_of(index, start, chans, lanes):
        piece = halos[index, start : start + SLOTS * chans, lanes]
        return piece.reshape(SLOTS, chans, -1)

    def grid(field):
        return field.reshape(SLOTS, -1, JB, IB)

    row = slice(0, IB)
    west = slice(0, JB)
    east = slice(EAST_LANE, EAST_LANE + JB)
    stack = jnp.stack

    def both(index, lanes, start, chans, order, axis):
        near = rows_of(index, start, chans, lanes)
        if order is None:
            return jnp.expand_dims(near, axis)
        far = rows_of(index, 40, chans, lanes)
        return stack([far, near] if order else [near, far], axis=axis)

    state, speed = grid(tracers), grid(velocity)
    depth = grid(kmt)
    ext_x = jnp.concatenate([both(2, west, 0, 4, True, 3), state, both(2, east, 0, 4, False, 3)], axis=3)
    ext_y = jnp.concatenate([both(0, row, 0, 4, True, 2), state, both(1, row, 0, 4, False, 2)], axis=2)
    u = jnp.concatenate([both(2, west, 80, 2, None, 3), speed[:, :2], both(2, east, 80, 2, None, 3)], axis=3)
    v = jnp.concatenate([both(0, row, 80, 2, None, 2), speed[:, 2:], both(1, row, 80, 2, None, 2)], axis=2)
    depth_x = jnp.concatenate([both(2, west, 100, 1, None, 3), depth, both(2, east, 100, 1, None, 3)], axis=3)
    depth_y = jnp.concatenate([both(0, row, 100, 1, None, 2), depth, both(1, row, 100, 1, None, 2)], axis=2)
    levels = jnp.arange(2, dtype=jnp.float32).reshape(1, 2, 1, 1)
    wet_x = jnp.clip(depth_x - levels, 0.0, 1.0)
    wet_y = jnp.clip(depth_y - levels, 0.0, 1.0)
    wet = jnp.clip(depth - levels, 0.0, 1.0)
    face_x = 0.5 * (u[..., :-1] + u[..., 1:]) * wet_x[..., :-1] * wet_x[..., 1:]
    face_y = 0.5 * (v[:, :, :-1] + v[:, :, 1:]) * wet_y[:, :, :-1] * wet_y[:, :, 1:]
    coupling = kappa.reshape(SLOTS, JB, IB) * wet[:, 0] * wet[:, 1]

    def flux(velocity_face, far_a, a, b, far_b):
        speed_face = velocity_face[:, None]
        centered = (7.0 * (a + b) - (far_a + far_b)) / 12.0
        upwind = (far_b - 3.0 * b + 3.0 * a - far_a) / 12.0
        return speed_face * centered + jnp.abs(speed_face) * upwind

    x = ext_x.reshape(SLOTS, 2, 2, JB, IB + 4)
    y = ext_y.reshape(SLOTS, 2, 2, JB + 4, IB)
    n = IB + 1
    flux_x = flux(face_x, x[..., :n], x[..., 1 : n + 1], x[..., 2 : n + 2], x[..., 3:])
    n = JB + 1
    flux_y = flux(face_y, y[:, :, :, :n], y[:, :, :, 1 : n + 1], y[:, :, :, 2 : n + 2], y[:, :, :, 3:])
    divergence = flux_x[..., 1:] - flux_x[..., :-1] + (flux_y[:, :, :, 1:] - flux_y[:, :, :, :-1])
    explicit = state.reshape(SLOTS, 2, 2, JB, IB) - COURANT * wet[:, None] * divergence
    c = coupling[:, None]
    first = explicit[:, :, 0] / (1.0 + c)
    ratio = c / (1.0 + c)
    lower = (explicit[:, :, 1] + c * first) / (1.0 + c - c * ratio)
    upper = first + ratio * lower
    result = stack([upper, lower], axis=2).reshape(SLOTS, 4, JB * IB)
    return jnp.where(live[:, None, None], result, 0.0)


def per_device(tracers, velocity, kappa, kmt, block_owner, neighbours, fold_partner):
    total = lax.axis_size("blk") * lax.axis_size("sub")
    me = lax.axis_index("blk") * 4 + lax.axis_index("sub")
    packs = edge_packs(tracers, velocity, kmt)
    window = exchange(far_kernel, packs, 2 * FAR + 1, 0, total)
    source, live = link_table(me, total, block_owner, neighbours, fold_partner)
    messages = choose(source, window)
    arrived = exchange(near_kernel, messages, GROUP, 1, total)
    halos = jnp.sum(arrived, axis=0)
    half = GROUP // 2 * SLOTS
    return finish(tracers, velocity, kappa, kmt, halos, live[half : half + SLOTS])


def solution(mesh):
    placed = (
        P(("blk", "sub"), None, None),
        P(("blk", "sub"), None, None),
        P(("blk", "sub"), None),
        P(("blk", "sub"), None),
        P(),
        P(),
        P(),
    )
    return jax.shard_map(
        per_device,
        mesh=mesh,
        in_specs=placed,
        out_specs=P(("blk", "sub"), None, None),
        check_vma=False,
    )
```

time: 1260 us -> 111 us (0.09); the launches traced: 1240 us -> 110 us
  starting transfers between devices: 742 us -> 0 us
  waiting for transfers between devices: 321 us -> 0 us
  local copies, waits for them, and re-layouts: 160 us -> 37.6 us
  Pallas kernels: 0 us -> 44.3 us
    ppermute x108 -> x0, starting transfers between devices: 742 us -> none  [shifted(): return lax.ppermute(block, axis, route)]
    ppermute x108 -> x0, waiting for transfers between devices: 321 us -> none  [shifted(): return lax.ppermute(block, axis, route)]
    unnamed x127 -> x26, local copies, waits for them, and re-layouts: 81.1 us -> 2.59 us
    pallas_call x0 -> x2, Pallas kernels: none -> 44.3 us  [exchange(): pl.pallas_call(lambda *refs: kernel(total, *refs), out_shape=jax.ShapeDty...]
    scatter x1 -> x0, local copies, waits for them, and re-layouts: 16.2 us -> none  [per_device(): slot_block = jnp.full((slot_total,), -1, jnp.int32).at[block_owner].set(j...]
    another operation x13 -> x16, local copies, waits for them, and re-layouts: 19.1 us -> 5.69 us  [the longest x10 3.42 us: both(): return jnp.expand_dims(near, axis)]
  transfers between devices with their start and end apart: 108 -> 0, of which waited for: 64 -> 0; matrix products, arithmetic and copies ran while one was open for 10% -> 0% of each run, Pallas kernels for 0% -> 0%
where the time goes in v1:
time: 111 us; the launch traced here: 110 us
  Pallas kernels  44.3 us (40%)
  local copies, waits for them, and re-layouts  37.6 us (34%)
  other arithmetic  22.3 us (20%)
  matrix products  4.96 us (4%)
    pallas_call x2, Pallas kernels, exchange(): pl.pallas_call(lambda *refs: kernel(total, *refs), out_shape=jax.ShapeDty...  44.3 us
    add x2, other arithmetic, flux(): return speed_face * centered + jnp.abs(speed_face) * upwind  7.31 us
    concatenate x4, local copies, waits for them, and re-layouts, finish(): jnp.concatenate([both(2, west, 0, 4, True, 3), state, both(2, east, 0, 4,...  6.37 us
    reshape x2, local copies, waits for them, and re-layouts, cut(): piece = field.reshape(field.shape[:-1] + (JB, IB))[..., column]  4.54 us
    mul x4, other arithmetic, flux(): return speed_face * centered + jnp.abs(speed_face) * upwind  4.06 us
    reshape x2, local copies, waits for them, and re-layouts, grid(): return field.reshape(SLOTS, -1, JB, IB)  3.89 us
    dot_general x14, matrix products, one(): out = jnp.einsum('xy,ycl->xcl', hot, rows, precision=lax.Precision.HIGHEST)  3.8 us
    another operation x10, local copies, waits for them, and re-layouts, both(): return jnp.expand_dims(near, axis)  3.42 us

profile of v1, /device:TPU:1, one launch (start us, length us, event | category | flops | bytes accessed | tf_op | source)
XLA Modules:
  0.0 110.0 jit_solution(18089970637721616095)
XLA Ops:
  0.0 3.4 %reshape.355 = f32[10,4,60,90]{3,2,1,0:T(8,128)S(1)} reshape(f32[10,4,5400]{2,1,0:T(4,128)} %param.7) | data formatting | bytes 1728000 | tf_op jit(solution)/shard_map/reshape | solution.py:37
  3.4 2.5 %slice_reduce_fusion.3 = (f32[10,4,60]{2,1,0:T(4,128)S(1)}, f32[10,4,60]{2,1,0:T(4,128)S(1)}, f32[10,4,60]{2,1,0:T(4,128)S(1)}, f32[10,4,60]{2,1,0:T(4,128)S(1)}) fusion(f32[10,4,60,90]{3,2,1,0:T(8,128)S(1)} %reshape.355), kind=kLoop, calls=%fused_computation.22 | loop fusion | bytes 76800 | tf_op jit(solution)/shard_map/slice | solution.py:37
  5.9 0.5 sub.111
  7.2 0.4 slice-done
  7.6 1.1 %reshape.356 = f32[10,2,60,90]{3,2,1,0:T(8,128)S(1)} reshape(f32[10,2,5400]{2,1,0:T(2,128)S(1)} %slice-done) | data formatting | bytes 864000 | tf_op jit(solution)/shard_map/reshape | solution.py:37
  8.8 0.6 slice_reduce_fusion.5
  9.7 0.3 copy-done.6
  10.1 0.7 pad_maximum_fusion.16.refs_0_
  10.8 22.3 %shard_map.73 = f32[7,3,112,128]{3,2,1,0:T(8,128)} custom-call(f32[3,112,128]{2,1,0:T(8,128)} %pad_maximum_fusion.16.refs_0_), custom_call_target="tpu_custom_call" | custom-call | tf_op jit(solution)/shard_map/pallas_call | solution.py:154
  33.2 1.3 %slice_bitcast_fusion.2 = (f32[7,112,128]{2,1,0:T(8,128)S(1)}, f32[7,112,128]{2,1,0:T(8,128)S(1)}, f32[7,112,128]{2,1,0:T(8,128)S(1)}) fusion(f32[7,3,112,128]{3,2,1,0:T(8,128)} %shard_map.73), kind=kLoop, calls=%fused_computation.62 | loop fusion | bytes 2408448 | tf_op jit(solution)/shard_map/squeeze | solution.py:80
  34.8 0.3 select_reduce_fusion.1
  35.2 0.4 select_reduce_fusion
  36.1 0.3 fusion.19
  36.4 0.3 fusion.15
  37.5 0.3 fusion.17
  37.9 0.3 fusion.13
  38.6 0.8 rev.3
  40.0 0.3 fusion.11
  40.3 0.3 fusion.9
  40.6 0.7 copy.185
  41.7 1.0 fusion.6
  43.3 0.8 fusion.29
  47.1 1.0 maximum_bitcast_fusion.1
  48.1 1.2 %select_maximum_fusion.refs_0_ = f32[8,3,112,128]{3,2,1,0:T(8,128)} fusion(f32[8,1,110,128]{3,2,1,0:T(8,128)S(1)} %maximum_bitcast_fusion.1, f32[8,1,110,128]{3,2,1,0:T(8,128)S(1)} %fusion.6, f32[8,1,110,128]{3,2,1,0:T(8,128)S(1)} %maximum_bitcast_fusion), kind=kLoop, calls=%fused_computation.3 | loop fusion | flops 2064384 | bytes 2727936 | tf_op jit(solution)/shard_map/stack | solution.py:89
  49.3 21.9 %shard_map.74 = f32[8,3,112,128]{3,2,1,0:T(8,128)} custom-call(f32[8,3,112,128]{3,2,1,0:T(8,128)} %select_maximum_fusion.refs_0_), custom_call_target="tpu_custom_call" | custom-call | tf_op jit(solution)/shard_map/pallas_call | solution.py:154
  71.3 1.5 %reduce_sum.29 = f32[3,112,128]{2,1,0:T(8,128)S(1)} reduce(f32[8,3,112,128]{3,2,1,0:T(8,128)} %shard_map.74, f32[]{:T(128)} %constant.101.clone.1), dimensions={0}, to_apply=%region_3.4 | reduce | flops 301056 | bytes 1548292 | tf_op jit(solution)/shard_map/reduce_sum | solution.py:235
  73.3 0.5 reshape.389
  74.2 1.4 %broadcast_in_dim_reshape_squeeze.32 = f32[10,2,60,1]{3,2,1,0:T(8,128)} reshape(f32[1,20,60]{2,1,0:T(8,128)S(1)} %get-tuple-element.50) | data formatting | bytes 9600 | tf_op jit(solution)/shard_map/broadcast_in_dim;reshape;squeeze | solution.py:184
  75.6 1.4 %broadcast_in_dim_reshape_squeeze.33 = f32[10,2,60,1]{3,2,1,0:T(8,128)} reshape(f32[1,20,60]{2,1,0:T(8,128)S(1)} %get-tuple-element.51) | data formatting | bytes 9600 | tf_op jit(solution)/shard_map/broadcast_in_dim;reshape;squeeze | solution.py:184
  77.1 3.4 %reshape.388 = f32[10,4,60,90]{3,2,1,0:T(8,128)S(1)} reshape(f32[10,4,5400]{2,1,0:T(4,128)} %param.8) | data formatting | bytes 1728000 | tf_op jit(solution)/shard_map/reshape | solution.py:174
  80.5 0.9 fusion.84
  81.4 0.3 copy-done.4
  82.0 1.5 %broadcast_multiply_fusion.1 = (f32[10,2,60,91]{3,2,1,0:T(8,128)}, f32[10,2,60,91]{3,2,1,0:T(8,128)S(1)}) fusion(f32[10,2,60,92]{3,2,1,0:T(8,128)S(1)} %subtract_clamp_fusion.1, f32[10,2,60,1]{3,2,1,0:T(8,128)S(1)} %copy-done.5, f32[10,2,60,90]{3,2,1,0:T(8,128)S(1)} %get-tuple-element.19, f32[10,2,60,1]{3,2,1,0:T(8,128)S(1)} %copy-done.4), kind=kLoop, calls=%fused_computation.69 | loop fusion | flops 764400 | bytes 2188800 | tf_op jit(solution)/shard_map/mul | solution.py:208
  83.4 0.9 abs_multiply_fusion.1
  84.5 1.6 %copy.212 = f32[10,2,2,60,1]{4,3,2,1,0:T(8,128)} copy(f32[10,2,2,60,1]{3,2,1,0,4:T(2,128)S(1)} %bitcast.193) | data formatting | bytes 19200 | tf_op jit(solution)/shard_map/concatenate | solution.py:190
  86.1 1.6 %copy.213 = f32[10,2,2,60,1]{4,3,2,1,0:T(8,128)} copy(f32[10,2,2,60,1]{3,2,1,0,4:T(2,128)S(1)} %bitcast.192) | data formatting | bytes 19200 | tf_op jit(solution)/shard_map/concatenate | solution.py:190
  87.7 1.6 %copy.214 = f32[10,2,2,60,1]{4,3,2,1,0:T(8,128)} copy(f32[10,2,2,60,1]{3,2,1,0,4:T(2,128)S(1)} %bitcast.191) | data formatting | bytes 19200 | tf_op jit(solution)/shard_map/concatenate | solution.py:190
  89.2 1.6 %copy.217 = f32[10,2,2,60,1]{4,3,2,1,0:T(8,128)} copy(f32[10,2,2,60,1]{3,2,1,0,4:T(2,128)S(1)} %bitcast.190) | data formatting | bytes 19200 | tf_op jit(solution)/shard_map/concatenate | solution.py:190
  90.8 2.2 %reshape_reshape.3 = f32[10,2,2,60,90]{4,3,2,1,0:T(8,128)S(1)} reshape(f32[10,4,5400]{2,1,0:T(4,128)S(1)} %copy-done.3) | data formatting | bytes 1728000 | tf_op jit(solution)/shard_map/reshape;reshape | solution.py:217
  93.1 6.2 %multiply_add_fusion.1 = f32[10,2,2,60,91]{4,3,2,1,0:T(8,128)S(1)} fusion(f32[10,2,2,60,90]{4,3,2,1,0:T(8,128)S(1)} %reshape_reshape.3, f32[10,2,2,60,1]{4,3,2,1,0:T(8,128)} %copy.212, f32[10,2,2,60,1]{4,3,2,1,0:T(8,128)} %copy.214, f32[10,2,2,60,1]{4,3,2,1,0:T(8,128)} %copy.217, f32[10,2,2,60,1]{4,3,2,1,0:T(8,128)} %copy.213, ...), kind=kLoop, calls=%fused_computation.29 | loop fusion | flops 3931200 | bytes 2649600 | tf_op jit(solution)/shard_map/add | solution.py:208
  99.5 1.6 %broadcast_multiply_fusion = (f32[10,2,61,90]{3,2,1,0:T(8,128)S(1)}, f32[10,2,61,90]{3,2,1,0:T(8,128)S(1)}) fusion(f32[10,2,62,90]{3,2,1,0:T(8,128)S(1)} %subtract_clamp_fusion, f32[10,2,1,90]{3,2,1,0:T(1,128)S(1)} %broadcast_in_dim_reshape_squeeze.29, f32[10,2,60,90]{3,2,1,0:T(8,128)} %get-tuple-element.20, ...), kind=kLoop, calls=%fused_computation.68 | loop fusion | flops 768600 | bytes 2203200 | tf_op jit(solution)/shard_map/mul | solution.py:208
  101.2 1.1 multiply_add_fusion
  102.5 1.8 %fusion.2 = f32[10,2,2,60,90]{4,3,2,1,0:T(8,128)} fusion(f32[10,2,2,60,90]{4,3,2,1,0:T(8,128)S(1)} %reshape_reshape.3, f32[10,2,2,61,90]{4,3,2,1,0:T(8,128)S(1)} %multiply_add_fusion, f32[10,2,2,60,91]{4,3,2,1,0:T(8,128)S(1)} %multiply_add_fusion.1, f32[10,2,60,90]{3,2,0,1:T(8,128)S(1)} %get-tuple-element.46), kind=kLoop, calls=%fused_computation.9 | loop fusion | flops 1080000 | bytes 5616000 | tf_op jit(solution)/shard_map/sub | solution.py:217
  104.3 1.5 %reshape.390 = f32[10,1,60,90]{3,2,0,1:T(8,128)S(1)} reshape(f32[10,5400]{1,0:T(8,128)} %param.9) | data formatting | bytes 432000 | tf_op jit(solution)/shard_map/reshape | solution.py:202
  105.9 1.1 %copy-done.2 = f32[10,2,2,60,90]{4,3,2,1,0:T(8,128)S(1)} copy-done((f32[10,2,2,60,90]{4,3,2,1,0:T(8,128)S(1)}, f32[10,2,2,60,90]{4,3,2,1,0:T(8,128)}, u32[]{:S(2)}) %copy-start.2) | copy-done | bytes 864024
  107.1 0.3 multiply_add_fusion.2
  107.6 1.2 %reshape.391 = f32[10,4,5400]{2,1,0:T(4,128)S(1)} reshape(f32[10,2,2,60,90]{4,3,2,1,0:T(8,128)S(1)} %pad_maximum_fusion.12) | data formatting | bytes 1728000 | tf_op jit(solution)/shard_map/reshape | solution.py:223
  108.9 1.2 %broadcast_select_fusion = f32[10,4,5400]{2,1,0:T(4,128)} fusion(f32[10,4,5400]{2,1,0:T(4,128)S(1)} %reshape.391, pred[10]{0:T(512)(128)(4,1)S(1)} %slice.270), kind=kLoop, calls=%fused_computation.59 | loop fusion | flops 216000 | bytes 1728010 | tf_op jit(solution)/shard_map/jit(_where)/select_n | solution.py:224
  (135 shorter events, 9.5 us)
Async XLA Ops:
  3.4 2.5 %copy-start.7 = (f32[10,5400]{1,0:T(8,128)S(1)}, f32[10,5400]{1,0:T(8,128)}, u32[]{:S(2)}) copy-start(f32[10,5400]{1,0:T(8,128)} %param.10) | copy-start | bytes 648004
  6.4 0.7 copy-start
  6.5 1.1 %slice-start = ((f32[10,4,5400]{2,1,0:T(4,128)}), f32[10,2,5400]{2,1,0:T(2,128)S(1)}, s32[]{:S(2)}) async-start(f32[10,4,5400]{2,1,0:T(4,128)} %param.8), calls=%async_computation | async-start | bytes 880640 | tf_op jit(solution)/shard_map/slice | solution.py:41
  7.6 2.0 %copy-start.3 = (f32[10,4,5400]{2,1,0:T(4,128)S(1)}, f32[10,4,5400]{2,1,0:T(4,128)}, u32[]{:S(2)}) copy-start(f32[10,4,5400]{2,1,0:T(4,128)} %param.7) | copy-start | bytes 2592004
  8.7 1.2 %copy-start.6 = (f32[10,4,5400]{2,1,0:T(4,128)S(1)}, f32[10,4,5400]{2,1,0:T(4,128)}, u32[]{:S(2)}) copy-start(f32[10,4,5400]{2,1,0:T(4,128)} %param.8) | copy-start | bytes 2592004
  33.1 1.4 %copy-start.9 = (s32[1280]{0:T(1024)S(1)}, s32[1280]{0:T(1024)}, u32[]{:S(2)}) copy-start(s32[1280]{0:T(1024)} %param.11) | copy-start | bytes 15364
  33.1 1.7 %copy-start.11 = (s32[1280]{0:T(1024)S(1)}, s32[1280]{0:T(1024)}, u32[]{:S(2)}) copy-start(s32[1280]{0:T(1024)} %param.13) | copy-start | bytes 15364
  33.2 1.7 %copy-start.10 = (s32[1280,4]{0,1:T(4,128)S(1)}, s32[1280,4]{0,1:T(4,128)}, u32[]{:S(2)}) copy-start(s32[1280,4]{0,1:T(4,128)} %param.12) | copy-start | bytes 61444
  71.3 2.0 %copy-start.8 = (f32[10,5400]{1,0:T(8,128)S(1)}, f32[10,5400]{1,0:T(8,128)}, u32[]{:S(2)}) copy-start(f32[10,5400]{1,0:T(8,128)} %param.10) | copy-start | bytes 648004
  80.5 1.3 %copy-start.4 = (f32[10,2,60,1]{3,2,1,0:T(8,128)S(1)}, f32[10,2,60,1]{3,2,1,0:T(8,128)}, u32[]{:S(2)}) copy-start(f32[10,2,60,1]{3,2,1,0:T(8,128)} %broadcast_in_dim_reshape_squeeze.32) | copy-start | bytes 14404
  80.5 1.5 %copy-start.5 = (f32[10,2,60,1]{3,2,1,0:T(8,128)S(1)}, f32[10,2,60,1]{3,2,1,0:T(8,128)}, u32[]{:S(2)}) copy-start(f32[10,2,60,1]{3,2,1,0:T(8,128)} %broadcast_in_dim_reshape_squeeze.33) | copy-start | bytes 14404
  101.2 1.1 copy-start.1
  105.7 1.3 %copy-start.2 = (f32[10,2,2,60,90]{4,3,2,1,0:T(8,128)S(1)}, f32[10,2,2,60,90]{4,3,2,1,0:T(8,128)}, u32[]{:S(2)}) copy-start(f32[10,2,2,60,90]{4,3,2,1,0:T(8,128)} %fusion.2) | copy-start | bytes 2592004

commit v2 on v0

v2 whole, which is shorter than its diff:
```python
import jax
import jax.numpy as jnp
from jax import lax
from jax.experimental import pallas as pl
from jax.experimental.pallas import tpu as pltpu
from jax.sharding import PartitionSpec as P

IB = 90
JB = 60
CELLS = IB * JB
SLOTS = 10
PAIRS = SLOTS // 2
DEVICES = 256
COURANT = 0.2
GROUP = 8
HALF = GROUP // 2
FAR = 3
LANES = 128
TILES = 43
FRAME = 47
SIDE = 64
PACK = SLOTS + 1
OWN_UP = FAR * PACK
OWN_DOWN = OWN_UP + PACK
EXTRA = OWN_DOWN + (FAR + 1) * PACK
EMPTY = EXTRA + 2 * PACK
WINDOW = EMPTY + 2
WANT = 2 * SLOTS + 2
FOLD_REACH = 14
MESH = pl.DeviceIdType.MESH
COLUMNS = ("south", "north", "earlier", "later", "west", "east", "send_later", "send_earlier", "next", "previous", "fold", "live", "up")
AT = {name: number for number, name in enumerate(COLUMNS)}


def position():
    return lax.axis_index("blk") * 4 + lax.axis_index("sub")


def lanes_at(tile):
    return pl.ds(tile * LANES, LANES)


def iotas():
    return (
        lax.broadcasted_iota(jnp.int32, (8, LANES), 0),
        lax.broadcasted_iota(jnp.int32, (8, LANES), 1),
    )


def take(packed, index):
    return jnp.take_along_axis(packed, index, axis=1, mode="promise_in_bounds")


def row(value, number):
    return jnp.broadcast_to(value[number : number + 1], (8, LANES))


def table_kernel(owner_ref, near_ref, fold_ref, out_ref):
    me = position()
    rows = GROUP * SLOTS
    blocks = owner_ref.shape[1]
    number = lax.broadcasted_iota(jnp.int32, (rows, 1), 0).astype(jnp.float32)
    which = jnp.floor((number + 0.5) * (1.0 / SLOTS))
    slot = number - which * SLOTS
    offset = which - HALF
    device = offset + jnp.float32(1) * me
    device = jnp.where(device < 0, device + DEVICES, device)
    device = jnp.where(device >= DEVICES, device - DEVICES, device)
    code = device * SLOTS + slot
    owner = owner_ref[...].astype(jnp.float32)
    hit = owner == code
    ids = lax.broadcasted_iota(jnp.int32, (1, blocks), 1).astype(jnp.float32)

    def total(mask, value):
        return jnp.sum(jnp.where(mask, value, 0.0), axis=1, keepdims=True)

    own_count = total((owner >= device * SLOTS) & (owner < device * SLOTS + SLOTS), 1.0)
    before_count = total((owner >= device * SLOTS - SLOTS) & (owner < device * SLOTS), 1.0)
    live = total(hit, 1.0)
    links = []
    for k in range(5):
        link = near_ref[k : k + 1, :] if k < 4 else fold_ref[...]
        block = total(hit, link.astype(jnp.float32) + 1.0) - 1.0
        links.append(total(block == ids, owner + 1.0) - 1.0)

    def where_is(other):
        source = jnp.floor((other + 0.5) * (1.0 / SLOTS))
        apart = source - device
        eight = apart + offset
        hop = jnp.floor((eight + 0.5) * (1.0 / GROUP))
        there = (other >= 0) & (hop * GROUP == eight)
        return there, source, other - source * SLOTS, apart, hop

    vote = jnp.where(links[3] >= 0, jnp.where(links[3] > code, 1.0, -1.0), 0.0)
    vote = vote - jnp.where(links[2] >= 0, jnp.where(links[2] > code, 1.0, -1.0), 0.0)
    up = jnp.sum(vote, axis=0, keepdims=True) >= 0

    def straight(other, own_if_up, own_if_down):
        there, _, place, apart, hop = where_is(other)
        index = jnp.where(
            apart < 0,
            (hop + FAR) * PACK,
            jnp.where(apart > 0, OWN_DOWN + hop * PACK, jnp.where(up, own_if_up, own_if_down)),
        )
        return jnp.where(there, index + place, float(EMPTY))

    south = straight(links[2], float(OWN_UP), float(OWN_DOWN))
    north = straight(links[3], float(OWN_DOWN), float(OWN_UP))
    there, _, place, apart, hop = where_is(links[4])
    folded_up = jnp.where(
        apart < 0, (hop + FAR) * PACK, jnp.where(hop > 0, EXTRA + (hop - 1) * PACK, float(OWN_UP))
    )
    folded_down = jnp.where(
        apart > 0, OWN_DOWN + hop * PACK, jnp.where(hop < 0, EXTRA + (-hop - 1) * PACK, float(OWN_DOWN))
    )
    folded = jnp.where(up, folded_up, folded_down) + place
    north = jnp.where(there, folded, north)
    sides = []
    columns = {"earlier": 0.0, "later": 0.0, "send_later": 0.0, "send_earlier": 0.0, "next": 0.0, "previous": 0.0}
    for side in range(2):
        other = links[side]
        there, source, place, apart, hop = where_is(other)
        linked = other >= 0
        after = linked & (slot == own_count - 1.0) & (other == device * SLOTS + SLOTS)
        before = linked & (slot == 0) & (apart == -1) & (place + 1.0 == before_count)
        earlier = linked & (apart < 0) & ~before
        later = linked & (apart > 0) & ~after
        mine = slot * 2.0 + (side + 1.0)
        columns["earlier"] += jnp.where(earlier & there, (hop + FAR) * PACK + SLOTS - EMPTY, 0.0)
        columns["later"] += jnp.where(later & there, OWN_DOWN + hop * PACK + SLOTS - EMPTY, 0.0)
        columns["send_later"] += jnp.where(later, mine, 0.0)
        columns["send_earlier"] += jnp.where(earlier, mine, 0.0)
        columns["next"] += jnp.where(after, mine, 0.0)
        columns["previous"] += jnp.where(before, mine, 0.0)
        index = jnp.where(linked & (apart == 0), place * 2.0 + (1.0 - side), 24.0)
        index = jnp.where(before, 20.0, jnp.where(after, 21.0, index))
        index = jnp.where(earlier, 22.0, jnp.where(later, 23.0, index))
        sides.append(index)
    columns.update(
        south=south, north=north, west=sides[0], east=sides[1], live=live,
        fold=jnp.where(links[4] >= 0, 1.0, 0.0), up=jnp.where(up, 1.0, 0.0),
    )
    lane = lax.broadcasted_iota(jnp.int32, (rows, LANES), 1)
    result = jnp.zeros((rows, LANES), jnp.float32)
    for name, at in AT.items():
        result = jnp.where(lane == at, columns[name], result)
    out_ref[...] = result.astype(jnp.int32)


def link_table(block_owner, neighbours, fold_partner):
    return pl.pallas_call(
        table_kernel,
        out_shape=jax.ShapeDtypeStruct((GROUP * SLOTS, LANES), jnp.int32),
        compiler_params=pltpu.CompilerParams(vmem_limit_bytes=20 << 20),
        name="table",
    )(block_owner[None], neighbours.T, fold_partner[None])


def own_row(table_ref, slot, name):
    return table_ref[HALF * SLOTS + slot, AT[name]]


def load4(ref, half, t):
    if t < TILES - 1:
        return ref[half, :, lanes_at(t)]
    width = CELLS - t * LANES
    return jnp.pad(ref[half, :, pl.ds(t * LANES, width)], ((0, 0), (0, LANES - width)))


def load_rows(ref, t):
    if t < TILES - 1:
        return ref[:, lanes_at(t)]
    width = CELLS - t * LANES
    return jnp.pad(ref[:, pl.ds(t * LANES, width)], ((0, 0), (0, LANES - width)))


def line(tiles, start, lane):
    first = start // LANES
    r = start % LANES
    if r == 0:
        return tiles(first)
    amount = LANES - r
    return jnp.where(lane < amount, pltpu.roll(tiles(first), amount, 1), pltpu.roll(tiles(first + 1), amount, 1))


ROW_STARTS = (0, IB, (JB - 1) * IB, (JB - 2) * IB)


def pack_kernel(table_ref, tracers_ref, velocity_ref, kmt_ref, up_ref, down_ref, next_ref, sides_ref, depth_rows):
    pair = pl.program_id(0)
    sub, lane = iotas()
    column = lane % SIDE
    base_near = column * IB + jnp.where(lane >= SIDE, IB - 1, 0)
    base_far = column * IB + jnp.where(lane >= SIDE, IB - 2, 1)
    near_tile, near_at = base_near // LANES, base_near % LANES
    far_tile, far_at = base_far // LANES, base_far % LANES

    @pl.when(pair == 0)
    def _():
        lane10 = lane[0:1]
        near = jnp.zeros((16, LANES), jnp.float32)
        index16 = jnp.concatenate([near_at, near_at], axis=0)
        tile16 = jnp.concatenate([near_tile, near_tile], axis=0)

        def padded(t):
            return jnp.pad(load_rows(kmt_ref, t), ((0, 6), (0, 0)))

        for t in range(TILES):
            near = jnp.where(tile16 == t, take(padded(t), index16), near)
        south = padded(0)
        north = line(padded, (JB - 1) * IB, lane10)
        for q in range(SLOTS):
            depth_rows[0, q] = row(south, q)
            depth_rows[1, q] = row(north, q)
            depth_rows[2, q] = row(near, q)

    flag = own_row(table_ref, 0, "up") > 0
    aux_at = lane
    for s in range(8):
        move = {6: 28, 7: 14}.get(s, 90 if s % 2 == 0 else 52)
        aux_at = jnp.where((sub == s) & (lane >= IB), lane - move, aux_at)
    lane4 = lane[0:4]
    for half in range(2):
        q = 2 * pair + half

        def tracer(t):
            return load4(tracers_ref, half, t)

        def speed(t):
            return load4(velocity_ref, half, t)

        packets = []
        for kind, (near, far) in enumerate(((0, 1), (JB - 1, JB - 2))):
            body = jnp.concatenate([line(tracer, near * IB, lane4), line(tracer, far * IB, lane4)], axis=0)
            v = line(speed, near * IB, lane4)
            v0, v1 = row(v, 2), row(v, 3)
            joint = jnp.where(lane >= 76, v0, pltpu.roll(v1, LANES - 14, 1))
            aux = jnp.where(sub == 6, joint, depth_rows[kind, q])
            aux = jnp.where(sub < 2, v0, jnp.where(sub < 4, v1, aux))
            packets.append(jnp.where(lane < IB, body, take(aux, aux_at)))
        up_ref[q] = jnp.where(flag, packets[1], packets[0])
        down_ref[q] = jnp.where(flag, packets[0], packets[1])

    near = far = drift = jnp.zeros((8, LANES), jnp.float32)
    for t in range(TILES):
        x = jnp.concatenate([load4(tracers_ref, 0, t), load4(tracers_ref, 1, t)], axis=0)
        v = jnp.concatenate([load4(velocity_ref, 0, t), load4(velocity_ref, 1, t)], axis=0)
        near = jnp.where(near_tile == t, take(x, near_at), near)
        far = jnp.where(far_tile == t, take(x, far_at), far)
        drift = jnp.where(near_tile == t, take(v, near_at), drift)
    for half in range(2):
        q = 2 * pair + half
        if half == 0:
            body = jnp.where(sub < 4, near, pltpu.roll(far, 4, 0))
            aux = drift
        else:
            body = jnp.where(sub < 4, pltpu.roll(near, 4, 0), far)
            aux = pltpu.roll(drift, 4, 0)
        aux = jnp.where(sub == 2, depth_rows[2, q], aux)
        sides_ref[2 * q] = jnp.where(lane < SIDE, body, pltpu.roll(aux, SIDE, 1))
        sides_ref[2 * q + 1] = jnp.where(lane < SIDE, pltpu.roll(body, SIDE, 1), aux)

    @pl.when(pair == PAIRS - 1)
    def _():
        sides_ref[2 * SLOTS] = jnp.zeros((8, LANES), jnp.float32)

        def chosen(name):
            value = own_row(table_ref, 0, name)
            for q in range(1, SLOTS):
                value = value + own_row(table_ref, q, name)
            return sides_ref[jnp.where(value > 0, value - 1, 2 * SLOTS)]

        up_ref[SLOTS] = chosen("send_later")
        down_ref[SLOTS] = chosen("send_earlier")
        next_ref[0] = chosen("next")
        next_ref[1] = chosen("previous")


def packet_shape(*lead):
    return jax.ShapeDtypeStruct(lead + (8, LANES), jnp.float32)


def edge_packs(table, tracers, velocity, kmt):
    field = pl.BlockSpec((2, 4, CELLS), lambda p: (p, 0, 0))

    def whole(count):
        return pl.BlockSpec((count, 8, LANES), lambda p: (0, 0, 0))

    return pl.pallas_call(
        pack_kernel,
        grid=(PAIRS,),
        out_shape=[packet_shape(PACK), packet_shape(PACK), packet_shape(2), packet_shape(2 * SLOTS + 1)],
        in_specs=[
            pl.BlockSpec(memory_space=pltpu.SMEM),
            field,
            field,
            pl.BlockSpec((SLOTS, CELLS), lambda p: (0, 0)),
        ],
        out_specs=[whole(PACK), whole(PACK), whole(2), whole(2 * SLOTS + 1)],
        scratch_shapes=[pltpu.VMEM((3, SLOTS, 8, LANES), jnp.float32)],
        compiler_params=pltpu.CompilerParams(vmem_limit_bytes=20 << 20),
        name="pack",
    )(table, tracers, velocity, kmt)


def choose_kernel(table_ref, window_ref, out_ref):
    for c in range(GROUP):
        earlier = later = EMPTY
        for q in range(SLOTS):
            r = c * SLOTS + q
            out_ref[c, q] = window_ref[table_ref[r, AT["south"]]]
            out_ref[c, SLOTS + q] = window_ref[table_ref[r, AT["north"]]]
            earlier = earlier + table_ref[r, AT["earlier"]]
            later = later + table_ref[r, AT["later"]]
        out_ref[c, 2 * SLOTS] = window_ref[earlier]
        out_ref[c, 2 * SLOTS + 1] = window_ref[later]


def choose(table, window):
    vmem = pl.BlockSpec(memory_space=pltpu.VMEM)
    return pl.pallas_call(
        choose_kernel,
        out_shape=packet_shape(GROUP, WANT),
        in_specs=[pl.BlockSpec(memory_space=pltpu.SMEM), vmem],
        out_specs=vmem,
        compiler_params=pltpu.CompilerParams(vmem_limit_bytes=20 << 20),
        name="choose",
    )(table, window)


def coordinates(index):
    index = lax.rem(index + DEVICES, DEVICES)
    return (index // 4, lax.rem(index, 4))


def greet(offsets, me):
    barrier = pltpu.get_barrier_semaphore()
    for offset in offsets:
        pl.semaphore_signal(barrier, inc=1, device_id=coordinates(me + offset), device_id_type=MESH)
    pl.semaphore_wait(barrier, len(offsets))


FAR_SENDS = (
    [("up", GROUP * k, (FAR - k) * PACK) for k in range(1, FAR + 1)]
    + [("down", -GROUP * k, OWN_DOWN + k * PACK) for k in range(1, FAR + 1)]
    + [("next", 1, 0), ("next", -1, 1)]
)


def far_kernel(up_ref, down_ref, next_ref, window_ref, beside_ref, send_sem, recv_sem, extra_send, extra_recv):
    me = position()
    greet([offset for _, offset, _ in FAR_SENDS], me)
    copies = []
    for number, (kind, offset, place) in enumerate(FAR_SENDS):
        if kind == "next":
            source, target = next_ref.at[place], beside_ref.at[place]
        else:
            source = up_ref if kind == "up" else down_ref
            target = window_ref.at[pl.ds(place, PACK)]
        copy = pltpu.make_async_remote_copy(
            src_ref=source,
            dst_ref=target,
            send_sem=send_sem.at[number],
            recv_sem=recv_sem.at[number],
            device_id=coordinates(me + offset),
            device_id_type=MESH,
        )
        copy.start()
        copies.append(copy)

    def fold_copy(k, downwards):
        return pltpu.make_async_remote_copy(
            src_ref=up_ref if downwards else down_ref,
            dst_ref=window_ref.at[pl.ds(EXTRA + (k - 1) * PACK, PACK)],
            send_sem=extra_send.at[k - 1],
            recv_sem=extra_recv.at[k - 1],
            device_id=coordinates(me - GROUP * k if downwards else me + GROUP * k),
            device_id_type=MESH,
        )

    high, low = DEVICES - FOLD_REACH, FOLD_REACH
    for k in (1, 2):
        @pl.when(me >= high)
        def _():
            fold_copy(k, True).start()

        @pl.when(me < low)
        def _():
            fold_copy(k, False).start()

    window_ref[pl.ds(OWN_UP, PACK)] = up_ref[...]
    window_ref[pl.ds(OWN_DOWN, PACK)] = down_ref[...]
    window_ref[pl.ds(EMPTY, 2)] = jnp.zeros((2, 8, LANES), jnp.float32)
    for copy in copies:
        copy.wait()
    for k in (1, 2):
        @pl.when(me >= high)
        def _():
            fold_copy(k, True).wait_send()

        @pl.when(me < low)
        def _():
            fold_copy(k, False).wait_send()

        @pl.when((me + GROUP * k >= high) & (me + GROUP * k < DEVICES))
        def _():
            fold_copy(k, True).wait_recv()

        @pl.when((me - GROUP * k >= 0) & (me - GROUP * k < low))
        def _():
            fold_copy(k, False).wait_recv()


def far_exchange(up, down, beside):
    vmem = pl.BlockSpec(memory_space=pltpu.VMEM)
    return pl.pallas_call(
        far_kernel,
        out_shape=[packet_shape(WINDOW), packet_shape(2)],
        in_specs=[vmem] * 3,
        out_specs=[vmem] * 2,
        scratch_shapes=[
            pltpu.SemaphoreType.DMA((len(FAR_SENDS),)),
            pltpu.SemaphoreType.DMA((len(FAR_SENDS),)),
            pltpu.SemaphoreType.DMA((2,)),
            pltpu.SemaphoreType.DMA((2,)),
        ],
        compiler_params=pltpu.CompilerParams(
            collective_id=0, has_side_effects=True, vmem_limit_bytes=20 << 20
        ),
        name="far",
    )(up, down, beside)


def near_kernel(message_ref, out_ref, send_sem, recv_sem):
    me = position()
    greet([c for c in range(-HALF, HALF + 1) if c != 0], me)
    copies = []
    for c in range(-HALF, HALF):
        if c == 0:
            continue
        copy = pltpu.make_async_remote_copy(
            src_ref=message_ref.at[c + HALF],
            dst_ref=out_ref.at[c + HALF],
            send_sem=send_sem.at[c + HALF],
            recv_sem=recv_sem.at[c + HALF],
            device_id=coordinates(me + c),
            device_id_type=MESH,
        )
        copy.start()
        copies.append(copy)
    out_ref[HALF] = message_ref[HALF]
    for copy in copies:
        copy.wait()


def near_exchange(messages):
    vmem = pl.BlockSpec(memory_space=pltpu.VMEM)
    return pl.pallas_call(
        near_kernel,
        out_shape=packet_shape(GROUP, WANT),
        in_specs=[vmem],
        out_specs=vmem,
        scratch_shapes=[pltpu.SemaphoreType.DMA((GROUP,)), pltpu.SemaphoreType.DMA((GROUP,))],
        compiler_params=pltpu.CompilerParams(
            collective_id=1, has_side_effects=True, vmem_limit_bytes=20 << 20
        ),
        name="near",
    )(messages)


def finish_kernel(table_ref, tracers_ref, velocity_ref, kappa_ref, kmt_ref, arrived_ref, sides_ref, beside_ref, out_ref,
                  halo, around, place, spot, xs, us, vs, all_ds, all_ks):
    pair = pl.program_id(0)
    sub, lane = iotas()
    upper = sub < 4

    def spread(ref, p, t):
        width = min(LANES, CELLS - t * LANES)
        value = ref[2 * p : 2 * p + 2, pl.ds(t * LANES, width)]
        if width < LANES:
            value = jnp.pad(value, ((0, 0), (0, LANES - width)))
        return jnp.where(
            sub < 4, jnp.broadcast_to(value[0:1], (8, LANES)), jnp.broadcast_to(value[1:2], (8, LANES))
        )

    @pl.when(pair == 0)
    def _():
        for number in range(WANT):
            total = arrived_ref[0, number]
            for source in range(1, GROUP):
                total = total + arrived_ref[source, number]
            halo[number] = total
        for number in range(2 * SLOTS):
            around[number] = sides_ref[number]
        around[2 * SLOTS] = beside_ref[0]
        around[2 * SLOTS + 1] = beside_ref[1]
        around[2 * SLOTS + 2] = halo[2 * SLOTS]
        around[2 * SLOTS + 3] = halo[2 * SLOTS + 1]
        around[2 * SLOTS + 4] = jnp.zeros((8, LANES), jnp.float32)
        for t in range(TILES):
            flat = lane + t * LANES
            j = ((flat.astype(jnp.float32) + 0.5) * (1.0 / IB)).astype(jnp.int32)
            i = flat - j * IB
            place[:, lanes_at(t)] = i
            spot[:, lanes_at(t)] = j + jnp.where(i >= IB // 2, SIDE, 0)
            for p in range(PAIRS):
                all_ds[p, :, lanes_at(t + 2)] = spread(kmt_ref, p, t)
                all_ks[p, :, lanes_at(t)] = spread(kappa_ref, p, t)

    ds, ks = all_ds.at[pair], all_ks.at[pair]
    lower_half = sub % 4 < 2
    for t in range(TILES):
        xs[:, lanes_at(t + 2)] = jnp.concatenate([load4(tracers_ref, 0, t), load4(tracers_ref, 1, t)], axis=0)
        speed = jnp.concatenate([load4(velocity_ref, 0, t), load4(velocity_ref, 1, t)], axis=0)
        us[:, lanes_at(t + 2)] = jnp.where(lower_half, speed, pltpu.roll(speed, 2, 0))
        vs[:, lanes_at(t + 2)] = jnp.where(lower_half, pltpu.roll(speed, 6, 0), speed)

    def frame(ref, south_near, south_far, north_near, north_far):
        if south_far is not None:
            ref[:, lanes_at(0)] = pltpu.roll(south_far, 76, 1)
            ref[:, lanes_at(1)] = jnp.where(lane < 38, pltpu.roll(south_far, 76, 1), pltpu.roll(south_near, 38, 1))
            far = pltpu.roll(north_far, 114, 1)
            ref[:, lanes_at(45)] = far
        else:
            ref[:, lanes_at(1)] = pltpu.roll(south_near, 38, 1)
            far = pltpu.roll(north_near, 24, 1)
        tail = ref[:, lanes_at(44)]
        ref[:, lanes_at(44)] = jnp.where(lane < 24, tail, jnp.where(lane < 114, pltpu.roll(north_near, 24, 1), far))

    odd = sub % 2 == 1

    def paired(first, second):
        return jnp.where(upper, first, second)

    def across(first, second):
        near = jnp.where(upper, first, pltpu.roll(second, 4, 0))
        return near, jnp.where(upper, pltpu.roll(first, 4, 0), second)

    def unpack(packet):
        a, b = pltpu.roll(packet, 38, 1), pltpu.roll(packet, 76, 1)
        c, d = pltpu.roll(packet, 100, 1), pltpu.roll(packet, 114, 1)

        def joined(first, second, third):
            return jnp.where(lane < 38, first, jnp.where(lane < 76, second, third))

        speed = jnp.where(odd, joined(row(a, 2), row(b, 3), row(d, 6)), joined(row(a, 0), row(b, 1), row(c, 6)))
        return speed, joined(row(a, 4), row(b, 5), row(d, 7))

    def rows_from(first, second):
        near, far = across(first, second)
        (speed_a, depth_a), (speed_b, depth_b) = unpack(first), unpack(second)
        return near, far, paired(speed_a, speed_b), paired(depth_a, depth_b)

    slots = (2 * pair, 2 * pair + 1)
    south = rows_from(halo[slots[0]], halo[slots[1]])
    north = rows_from(halo[SLOTS + slots[0]], halo[SLOTS + slots[1]])
    folded = paired(*(own_row(table_ref, q, "fold") for q in slots)) > 0
    back = jnp.where(lane < IB, IB - 1 - lane, lane)
    north = [
        jnp.where(folded, sign * take(value, back), value) for value, sign in zip(north, (1.0, 1.0, -1.0, 1.0))
    ]
    frame(xs, south[0], south[1], north[0], north[1])
    frame(vs, south[2], None, north[2], None)
    frame(ds, south[3], None, north[3], None)
    bodies, speeds, depths = [], [], []
    for q in slots:
        west, east = (around[own_row(table_ref, q, name)] for name in ("west", "east"))
        bodies.append(jnp.where(lane < SIDE, west, pltpu.roll(east, SIDE, 1)))
        aux = jnp.where(lane < SIDE, pltpu.roll(west, SIDE, 1), east)
        speeds.append(jnp.where(odd, row(aux, 1), row(aux, 0)))
        depths.append(row(aux, 2))
    side_near, side_far = across(*bodies)
    side_speed, side_depth = paired(*speeds), paired(*depths)
    level = (sub % 2).astype(jnp.float32)
    keep = paired(*(own_row(table_ref, q, "live") for q in slots)) > 0
    turned = {}

    def tile_of(ref, tile):
        key = (id(ref), tile, 0)
        if key not in turned:
            turned[key] = ref[:, lanes_at(tile)]
        return turned[key]

    def turn(ref, tile, r):
        key = (id(ref), tile, r)
        if key not in turned:
            turned[key] = pltpu.roll(tile_of(ref, tile), LANES - r, 1)
        return turned[key]

    def shift(ref, t, s):
        tile = t + 2 + s // LANES
        r = s % LANES
        return jnp.where(lane < LANES - r, turn(ref, tile, r), turn(ref, tile + 1, r))

    def flux(w, far_a, a, b, far_b):
        return jnp.maximum(w, 0.0) * (5.0 * a + 2.0 * b - far_a) + jnp.minimum(w, 0.0) * (2.0 * a + 5.0 * b - far_b)

    def wetness(d):
        return jnp.clip(d - level, 0.0, 1.0)

    def swap(z):
        return jnp.where(odd, pltpu.roll(z, 1, 0), pltpu.roll(z, 7, 0))

    for t in range(TILES):
        for key in [k for k in turned if k[1] < t]:
            del turned[key]
        i, index = place[:, lanes_at(t)], spot[:, lanes_at(t)]
        first, last = i == 0, i == IB - 1
        near, far = take(side_near, index), take(side_far, index)
        x = tile_of(xs, t + 2)
        west = jnp.where(first, near, shift(xs, t, -1))
        west_far = jnp.where(first, far, jnp.where(i == 1, near, shift(xs, t, -2)))
        east = jnp.where(last, near, shift(xs, t, 1))
        east_far = jnp.where(last, far, jnp.where(i == IB - 2, near, shift(xs, t, 2)))
        u = tile_of(us, t + 2)
        side_u = take(side_speed, index)
        u_west = jnp.where(first, side_u, shift(us, t, -1))
        u_east = jnp.where(last, side_u, shift(us, t, 1))
        wet = wetness(tile_of(ds, t + 2))
        side_d = take(side_depth, index)
        wet_west = wetness(jnp.where(first, side_d, shift(ds, t, -1)))
        wet_east = wetness(jnp.where(last, side_d, shift(ds, t, 1)))
        wet_south = wetness(shift(ds, t, -IB))
        wet_north = wetness(shift(ds, t, IB))
        v = tile_of(vs, t + 2)
        x_south, x_south_far = shift(xs, t, -IB), shift(xs, t, -2 * IB)
        x_north, x_north_far = shift(xs, t, IB), shift(xs, t, 2 * IB)
        flux_east = flux((u + u_east) * (wet * wet_east), west, x, east, east_far)
        flux_west = flux((u_west + u) * (wet_west * wet), west_far, west, x, east)
        flux_north = flux((v + shift(vs, t, IB)) * (wet * wet_north), x_south, x, x_north, x_north_far)
        flux_south = flux((shift(vs, t, -IB) + v) * (wet_south * wet), x_south_far, x_south, x, x_north)
        divergence = flux_east - flux_west + (flux_north - flux_south)
        explicit = x - (wet * (COURANT / 12.0)) * divergence
        coupling = ks[:, lanes_at(t)] * wet * swap(wet)
        share = coupling / (1.0 + 2.0 * coupling)
        result = explicit + share * (swap(explicit) - explicit)
        result = jnp.where(keep, result, 0.0)
        width = min(LANES, CELLS - t * LANES)
        out_ref[0, :, pl.ds(t * LANES, width)] = result[0:4, :width]
        out_ref[1, :, pl.ds(t * LANES, width)] = result[4:8, :width]


def finish(table, tracers, velocity, kappa, kmt, arrived, sides, beside):
    field = pl.BlockSpec((2, 4, CELLS), lambda p: (p, 0, 0))
    column = pl.BlockSpec((SLOTS, CELLS), lambda p: (0, 0))

    def whole(*lead):
        return pl.BlockSpec(lead + (8, LANES), lambda p: (0,) * (len(lead) + 2))

    wide = pltpu.VMEM((8, FRAME * LANES), jnp.float32)
    return pl.pallas_call(
        finish_kernel,
        grid=(PAIRS,),
        out_shape=jax.ShapeDtypeStruct((SLOTS, 4, CELLS), jnp.float32),
        in_specs=[
            pl.BlockSpec(memory_space=pltpu.SMEM),
            field,
            field,
            column,
            column,
            whole(GROUP, WANT),
            whole(2 * SLOTS + 1),
            whole(2),
        ],
        out_specs=field,
        scratch_shapes=[
            pltpu.VMEM((WANT, 8, LANES), jnp.float32),
            pltpu.VMEM((2 * SLOTS + 5, 8, LANES), jnp.float32),
            pltpu.VMEM((8, TILES * LANES), jnp.int32),
            pltpu.VMEM((8, TILES * LANES), jnp.int32),
            wide,
            wide,
            wide,
            pltpu.VMEM((PAIRS, 8, FRAME * LANES), jnp.float32),
            pltpu.VMEM((PAIRS, 8, TILES * LANES), jnp.float32),
        ],
        compiler_params=pltpu.CompilerParams(vmem_limit_bytes=40 << 20),
        name="advance",
    )(table, tracers, velocity, kappa, kmt, arrived, sides, beside)


def per_device(tracers, velocity, kappa, kmt, block_owner, neighbours, fold_partner):
    table = link_table(block_owner, neighbours, fold_partner)
    up, down, beside, sides = edge_packs(table, tracers, velocity, kmt)
    window, beside = far_exchange(up, down, beside)
    arrived = near_exchange(choose(table, window))
    return finish(table, tracers, velocity, kappa, kmt, arrived, sides, beside)


def solution(mesh):
    placed = (
        P(("blk", "sub"), None, None),
        P(("blk", "sub"), None, None),
        P(("blk", "sub"), None),
        P(("blk", "sub"), None),
        P(),
        P(),
        P(),
    )
    return jax.shard_map(
        per_device,
        mesh=mesh,
        in_specs=placed,
        out_specs=P(("blk", "sub"), None, None),
        check_vma=False,
    )
```

time: 1260 us -> 48.5 us (0.04); the launches traced: 1240 us -> 48.2 us
  starting transfers between devices: 742 us -> 0 us
  waiting for transfers between devices: 321 us -> 0 us
  local copies, waits for them, and re-layouts: 160 us -> 4.74 us
  Pallas kernels: 0 us -> 43.4 us
  other arithmetic: 18.8 us -> 0 us
    ppermute x108 -> x0, starting transfers between devices: 742 us -> none  [shifted(): return lax.ppermute(block, axis, route)]
    ppermute x108 -> x0, waiting for transfers between devices: 321 us -> none  [shifted(): return lax.ppermute(block, axis, route)]
    unnamed x127 -> x16, local copies, waits for them, and re-layouts: 81.1 us -> 3.34 us
    pallas_call x0 -> x6, Pallas kernels: none -> 43.4 us  [the longest x1 15.4 us: far_exchange(): pl.pallas_call(far_kernel, out_shape=[packet_shape(WINDOW), packet_shape(...]
    another operation x13 -> x0, local copies, waits for them, and re-layouts: 19.1 us -> none  [the longest x2 7.12 us: extend(): west_halo = sources[:, 0, :, strip:2 * strip].reshape(count, chans, rows, 2)]
    slice x14 -> x0, local copies, waits for them, and re-layouts: 17.9 us -> none  [the longest x3 8.84 us: edge_pack(): west_edge = block_field[:, :, :, 0:2].reshape(count, chans, rows * 2)]
    scatter x1 -> x0, local copies, waits for them, and re-layouts: 16.2 us -> none  [per_device(): slot_block = jnp.full((slot_total,), -1, jnp.int32).at[block_owner].set(j...]
  transfers between devices with their start and end apart: 108 -> 0, of which waited for: 64 -> 0; matrix products, arithmetic and copies ran while one was open for 10% -> 0% of each run, Pallas kernels for 0% -> 0%
where the time goes in v2:
time: 48.5 us; the launch traced here: 48.2 us
  Pallas kernels  43.4 us (89%)
  local copies, waits for them, and re-layouts  4.74 us (10%)
    pallas_call x1, Pallas kernels, far_exchange(): pl.pallas_call(far_kernel, out_shape=[packet_shape(WINDOW), packet_shape(...  15.4 us
    pallas_call x1, Pallas kernels, near_exchange(): pl.pallas_call(near_kernel, out_shape=packet_shape(GROUP, WANT), in_specs...  13 us
    pallas_call x1, Pallas kernels, finish(): pl.pallas_call(finish_kernel, grid=(PAIRS,), out_shape=jax.ShapeDtypeStru...  8.84 us
    pallas_call x1, Pallas kernels, edge_packs(): pl.pallas_call(pack_kernel, grid=(PAIRS,), out_shape=[packet_shape(PACK),...  3.59 us
    unnamed x16, local copies, waits for them, and re-layouts  3.34 us
    pallas_call x1, Pallas kernels, choose(): pl.pallas_call(choose_kernel, out_shape=packet_shape(GROUP, WANT), in_spe...  1.43 us
    pallas_call x1, Pallas kernels, link_table(): pl.pallas_call(table_kernel, out_shape=jax.ShapeDtypeStruct((GROUP * SLOT...  1.05 us

profile of v2, /device:TPU:1, one launch (start us, length us, event | category | flops | bytes accessed | tf_op | source)
XLA Modules:
  0.0 48.2 jit_solution(8029459186515937716)
XLA Ops:
  0.0 0.0 copy-start.7
  0.0 0.7 %broadcast_in_dim.6.owner_ref = s32[1,1280]{1,0:T(1,128)S(1)} reshape(s32[1280]{0:T(1024)} %param.11) | data formatting | bytes 10240 | tf_op jit(solution)/shard_map/broadcast_in_dim | solution.py:156
  0.7 0.7 %broadcast_in_dim.7.fold_ref = s32[1,1280]{1,0:T(1,128)S(1)} reshape(s32[1280]{0:T(1024)} %param.13) | data formatting | bytes 10240 | tf_op jit(solution)/shard_map/broadcast_in_dim | solution.py:156
  1.4 0.0 copy-done.7
  1.4 1.0 %table.1.table_ref = s32[80,128]{1,0:T(8,128)S(1)} custom-call(s32[1,1280]{1,0:T(1,128)S(1)} %broadcast_in_dim.6.owner_ref, s32[4,1280]{1,0:T(4,128)S(1)} %bitcast.1, s32[1,1280]{1,0:T(1,128)S(1)} %broadcast_in_dim.7.fold_ref), custom_call_target="tpu_custom_call" | custom-call | tf_op jit(solution)/shard_map/table/pallas_call | solution.py:151
  2.5 0.0 copy-start
  2.5 1.2 %copy-done = f32[10,4,5400]{2,1,0:T(4,128)S(1)} copy-done((f32[10,4,5400]{2,1,0:T(4,128)S(1)}, f32[10,4,5400]{2,1,0:T(4,128)}, u32[]{:S(2)}) %copy-start) | copy-done | bytes 864024
  3.6 0.0 copy-start.2
  3.6 1.2 %copy-done.2 = f32[10,4,5400]{2,1,0:T(4,128)S(1)} copy-done((f32[10,4,5400]{2,1,0:T(4,128)S(1)}, f32[10,4,5400]{2,1,0:T(4,128)}, u32[]{:S(2)}) %copy-start.2) | copy-done | bytes 864024
  4.8 0.0 copy-start.4
  4.8 1.0 %copy-done.4 = f32[10,5400]{1,0:T(8,128)S(1)} copy-done((f32[10,5400]{1,0:T(8,128)S(1)}, f32[10,5400]{1,0:T(8,128)}, u32[]{:S(2)}) %copy-start.4) | copy-done | bytes 216024
  5.8 3.6 %pack.1 = (f32[11,8,128]{2,1,0:T(8,128)S(1)}, f32[11,8,128]{2,1,0:T(8,128)S(1)}, f32[2,8,128]{2,1,0:T(8,128)S(1)}, f32[21,8,128]{2,1,0:T(8,128)S(1)}) custom-call(s32[80,128]{1,0:T(8,128)S(1)} %table.1.table_ref, f32[10,4,5400]{2,1,0:T(4,128)S(1)} %copy-done, f32[10,4,5400]{2,1,0:T(4,128)S(1)} %copy-done.2, f32[10,5400]{1,0:T(8,128)S(1)} %copy-done.4), custom_call_target="tpu_custom_call" | custom-call | tf_op jit(solution)/shard_map/pack/pallas_call | solution.py:289
  9.4 15.4 %far.1 = (f32[112,8,128]{2,1,0:T(8,128)S(1)}, f32[2,8,128]{2,1,0:T(8,128)S(1)}) custom-call(f32[11,8,128]{2,1,0:T(8,128)S(1)} %get-tuple-element.11.up_ref, f32[11,8,128]{2,1,0:T(8,128)S(1)} %get-tuple-element.12.down_ref, f32[2,8,128]{2,1,0:T(8,128)S(1)} %get-tuple-element.13.next_ref), custom_call_target="tpu_custom_call" | custom-call | tf_op jit(solution)/shard_map/far/pallas_call | solution.py:416
  24.8 0.0 copy-start.3
  24.8 0.0 copy-start.6
  24.8 1.4 %choose.1.message_ref = f32[8,22,8,128]{3,2,1,0:T(8,128)S(1)} custom-call(s32[80,128]{1,0:T(8,128)S(1)} %table.1.table_ref, f32[112,8,128]{2,1,0:T(8,128)S(1)} %get-tuple-element.14.window_ref), custom_call_target="tpu_custom_call" | custom-call | tf_op jit(solution)/shard_map/choose/pallas_call | solution.py:321
  26.3 0.0 copy-start.1
  26.3 0.0 copy-start.5
  26.3 13.0 %near.1.arrived_ref = f32[8,22,8,128]{3,2,1,0:T(8,128)S(1)} custom-call(f32[8,22,8,128]{3,2,1,0:T(8,128)S(1)} %choose.1.message_ref), custom_call_target="tpu_custom_call" | custom-call | tf_op jit(solution)/shard_map/near/pallas_call | solution.py:458
  39.3 0.0 copy-done.3
  39.4 0.0 copy-done.6
  39.4 0.0 copy-done.1
  39.4 0.0 copy-done.5
  39.4 8.8 %advance.1 = f32[10,4,5400]{2,1,0:T(4,128)} custom-call(s32[80,128]{1,0:T(8,128)S(1)} %table.1.table_ref, f32[10,4,5400]{2,1,0:T(4,128)S(1)} %copy-done.1, f32[10,4,5400]{2,1,0:T(4,128)S(1)} %copy-done.3, f32[10,5400]{1,0:T(8,128)S(1)} %copy-done.6, f32[10,5400]{1,0:T(8,128)S(1)} %copy-done.5, f32[8,22,8,128]{3,2,1,0:T(8,128)S(1)} %near.1.arrived_ref, ...), custom_call_target="tpu_custom_call" | custom-call | tf_op jit(solution)/shard_map/advance/pallas_call | solution.py:651
Async XLA Ops:
  0.0 1.4 %copy-start.7 = (s32[1280,4]{0,1:T(4,128)S(1)}, s32[1280,4]{0,1:T(4,128)}, u32[]{:S(2)}) copy-start(s32[1280,4]{0,1:T(4,128)} %param.12) | copy-start | bytes 61444
  2.5 1.2 %copy-start = (f32[10,4,5400]{2,1,0:T(4,128)S(1)}, f32[10,4,5400]{2,1,0:T(4,128)}, u32[]{:S(2)}) copy-start(f32[10,4,5400]{2,1,0:T(4,128)} %tracers_ref.3) | copy-start | bytes 2592004
  3.6 1.2 %copy-start.2 = (f32[10,4,5400]{2,1,0:T(4,128)S(1)}, f32[10,4,5400]{2,1,0:T(4,128)}, u32[]{:S(2)}) copy-start(f32[10,4,5400]{2,1,0:T(4,128)} %velocity_ref.3) | copy-start | bytes 2592004
  4.8 1.0 %copy-start.4 = (f32[10,5400]{1,0:T(8,128)S(1)}, f32[10,5400]{1,0:T(8,128)}, u32[]{:S(2)}) copy-start(f32[10,5400]{1,0:T(8,128)} %kmt_ref.3) | copy-start | bytes 648004
  24.8 14.5 %copy-start.3 = (f32[10,4,5400]{2,1,0:T(4,128)S(1)}, f32[10,4,5400]{2,1,0:T(4,128)}, u32[]{:S(2)}) copy-start(f32[10,4,5400]{2,1,0:T(4,128)} %velocity_ref.3) | copy-start | bytes 2592004
  24.8 14.5 %copy-start.6 = (f32[10,5400]{1,0:T(8,128)S(1)}, f32[10,5400]{1,0:T(8,128)}, u32[]{:S(2)}) copy-start(f32[10,5400]{1,0:T(8,128)} %kappa_ref.1) | copy-start | bytes 648004
  26.3 13.1 %copy-start.1 = (f32[10,4,5400]{2,1,0:T(4,128)S(1)}, f32[10,4,5400]{2,1,0:T(4,128)}, u32[]{:S(2)}) copy-start(f32[10,4,5400]{2,1,0:T(4,128)} %tracers_ref.3) | copy-start | bytes 2592004
  26.3 13.1 %copy-start.5 = (f32[10,5400]{1,0:T(8,128)S(1)}, f32[10,5400]{1,0:T(8,128)}, u32[]{:S(2)}) copy-start(f32[10,5400]{1,0:T(8,128)} %kmt_ref.3) | copy-start | bytes 648004

commit v3 on v0

v3 whole, which is shorter than its diff:
```python
import jax
import jax.numpy as jnp
from jax import lax
from jax.experimental import pallas as pl
from jax.experimental.pallas import tpu as pltpu
from jax.sharding import PartitionSpec as P

IB = 90
JB = 60
CELLS = IB * JB
SLOTS = 10
PAIRS = SLOTS // 2
DEVICES = 256
COURANT = 0.2
STRIDE = 4
HOPS = 7
LANES = 128
TILES = 43
FRAME = 47
SIDE = 64
PACK = SLOTS + 1
OWN_DOWN = HOPS * PACK
EXTRA = OWN_DOWN + STRIDE * PACK
EXTRAS = 3
EMPTY = EXTRA + EXTRAS * PACK
WINDOW = EMPTY + 1
WANT = 2 * SLOTS + 2
TARGETS = STRIDE + HOPS
TABLE_ROWS = 112
EARLY = 2
BIG = 63 << 20
FOLD_REACH = 14
MESH = pl.DeviceIdType.MESH
COLUMNS = ("behind", "ahead", "extra", "earlier", "later", "west", "east", "send_later", "send_earlier", "next", "previous", "fold", "live", "up")
AT = {name: number for number, name in enumerate(COLUMNS)}


def position():
    return lax.axis_index("blk") * 4 + lax.axis_index("sub")


def lanes_at(tile):
    return pl.ds(tile * LANES, LANES)


def iotas():
    return (
        lax.broadcasted_iota(jnp.int32, (8, LANES), 0),
        lax.broadcasted_iota(jnp.int32, (8, LANES), 1),
    )


def take(packed, index):
    return jnp.take_along_axis(packed, index, axis=1, mode="promise_in_bounds")


def row(value, number):
    return jnp.broadcast_to(value[number : number + 1], (8, LANES))


def table_of(owner_ref, near_ref, fold_ref):
    me = position()
    rows = TABLE_ROWS
    strips = owner_ref.shape[0]
    number = lax.broadcasted_iota(jnp.int32, (rows, 1), 0).astype(jnp.float32)
    which = jnp.floor((number + 0.5) * (1.0 / SLOTS))
    slot = number - which * SLOTS
    onward = which < STRIDE
    hops = jnp.where(onward, which, which - STRIDE)
    device = jnp.where(onward, hops, -STRIDE * hops) + jnp.float32(1) * me
    device = jnp.where(device < 0, device + DEVICES, device)
    device = jnp.where(device >= DEVICES, device - DEVICES, device)
    code = device * SLOTS + slot
    wide = lax.broadcasted_iota(jnp.int32, (1, LANES), 1).astype(jnp.float32)

    def total(pieces):
        acc = jnp.zeros((rows, LANES), jnp.float32)
        for mask, value in pieces:
            acc = acc + jnp.where(mask, value, 0.0)
        return jnp.sum(acc, axis=1, keepdims=True)

    owners = [owner_ref[t : t + 1, :].astype(jnp.float32) for t in range(strips)]
    hits = [owner == code for owner in owners]
    first = device * SLOTS
    own_count = total([((owner >= first) & (owner < first + SLOTS), 1.0) for owner in owners])
    before_count = total([((owner >= first - SLOTS) & (owner < first), 1.0) for owner in owners])
    live = total([(hit, 1.0) for hit in hits])
    links = []
    for k in range(5):
        if k < 4:
            link = [near_ref[k : k + 1, lanes_at(t)].astype(jnp.float32) for t in range(strips)]
        else:
            link = [fold_ref[t : t + 1, :].astype(jnp.float32) for t in range(strips)]
        block = total([(hit, piece + 1.0) for hit, piece in zip(hits, link)]) - 1.0
        links.append(total([(block == wide + t * LANES, owner + 1.0) for t, owner in enumerate(owners)]) - 1.0)

    def where_is(other):
        source = jnp.floor((other + 0.5) * (1.0 / SLOTS))
        apart = source - device
        distance = jnp.abs(apart)
        far = jnp.floor((distance + 0.5) * (1.0 / STRIDE))
        rest = distance - far * STRIDE
        from_behind = (other >= 0) & (apart <= 0) & onward & (rest == hops)
        from_ahead = (other >= 0) & (apart >= 0) & ~onward & (far == hops)
        return source, other - source * SLOTS, apart, far, rest, from_behind, from_ahead

    vote = jnp.where(links[3] >= 0, jnp.where(links[3] > code, 1.0, -1.0), 0.0)
    vote = vote - jnp.where(links[2] >= 0, jnp.where(links[2] > code, 1.0, -1.0), 0.0)
    up = jnp.sum(vote, axis=0, keepdims=True) >= 0
    empty = float(EMPTY)
    _, place, _, far, _, from_behind, _ = where_is(jnp.where(up, links[2], links[3]))
    behind = jnp.where(from_behind, far * PACK + place, empty)
    _, place, _, _, rest, _, from_ahead = where_is(jnp.where(up, links[3], links[2]))
    ahead = jnp.where(from_ahead, OWN_DOWN + rest * PACK + place, empty)
    _, place, apart, far, rest, from_behind, from_ahead = where_is(links[4])
    against = jnp.where(rest > 0, EXTRA + (rest - 1.0) * PACK, 0.0) + place
    ahead = jnp.where(up & from_ahead, against, ahead)
    against = jnp.where(far > 0, EXTRA + (far - 1.0) * PACK, float(OWN_DOWN)) + place
    behind = jnp.where(~up & from_behind, against, behind)
    extra = jnp.where(up & from_behind & (apart < 0), far * PACK + place, empty)
    extra = jnp.where(~up & from_ahead & (apart > 0), OWN_DOWN + rest * PACK + place, extra)
    sides = []
    columns = {"earlier": 0.0, "later": 0.0, "send_later": 0.0, "send_earlier": 0.0, "next": 0.0, "previous": 0.0}
    for side in range(2):
        other = links[side]
        source, place, apart, far, rest, from_behind, from_ahead = where_is(other)
        linked = other >= 0
        after = linked & (slot == own_count - 1.0) & (other == device * SLOTS + SLOTS)
        before = linked & (slot == 0) & (apart == -1) & (place + 1.0 == before_count)
        earlier = linked & (apart < 0) & ~before
        later = linked & (apart > 0) & ~after
        mine = slot * 2.0 + (side + 1.0)
        columns["earlier"] += jnp.where(earlier & from_behind, far * PACK + SLOTS - EMPTY, 0.0)
        columns["later"] += jnp.where(later & from_ahead, OWN_DOWN + rest * PACK + SLOTS - EMPTY, 0.0)
        columns["send_later"] += jnp.where(later, mine, 0.0)
        columns["send_earlier"] += jnp.where(earlier, mine, 0.0)
        columns["next"] += jnp.where(after, mine, 0.0)
        columns["previous"] += jnp.where(before, mine, 0.0)
        index = jnp.where(linked & (apart == 0), place * 2.0 + (1.0 - side), 24.0)
        index = jnp.where(before, 20.0, jnp.where(after, 21.0, index))
        index = jnp.where(earlier, 22.0, jnp.where(later, 23.0, index))
        sides.append(index)
    columns.update(
        behind=behind, ahead=ahead, extra=extra, west=sides[0], east=sides[1], live=live,
        fold=jnp.where(links[4] >= 0, 1.0, 0.0), up=jnp.where(up, 1.0, 0.0),
    )
    lane = lax.broadcasted_iota(jnp.int32, (rows, LANES), 1)
    result = jnp.zeros((rows, LANES), jnp.float32)
    for name, at in AT.items():
        result = jnp.where(lane == at, columns[name], result)
    own = number < SLOTS
    chosen = {
        name: jnp.sum(jnp.where(own, columns[name], 0.0), axis=0, keepdims=True)
        for name in ("send_later", "send_earlier", "next", "previous")
    }
    return result.astype(jnp.int32), up, chosen


def own_row(table_ref, slot, name):
    return table_ref[slot, AT[name]]


def load4(ref, half, t):
    if t < TILES - 1:
        return ref[half, :, lanes_at(t)]
    width = CELLS - t * LANES
    return jnp.pad(ref[half, :, pl.ds(t * LANES, width)], ((0, 0), (0, LANES - width)))


def load_rows(ref, t):
    if t < TILES - 1:
        return ref[:, lanes_at(t)]
    width = CELLS - t * LANES
    return jnp.pad(ref[:, pl.ds(t * LANES, width)], ((0, 0), (0, LANES - width)))


def line(tiles, start, lane):
    first = start // LANES
    r = start % LANES
    if r == 0:
        return tiles(first)
    amount = LANES - r
    return jnp.where(lane < amount, pltpu.roll(tiles(first), amount, 1), pltpu.roll(tiles(first + 1), amount, 1))


ROW_STARTS = (0, IB, (JB - 1) * IB, (JB - 2) * IB)


def front_kernel(owner_hbm, near_hbm, fold_hbm, tracers_hbm, velocity_hbm, kmt_hbm, table_ref, up_ref, down_ref, next_ref,
                 sides_ref, tracers_all, velocity_all, kmt_ref, depth_rows, sems,
                 owner_ref, near_ref, fold_ref, list_sems):
    lists = [
        pltpu.make_async_copy(source, target, list_sems.at[number])
        for number, (source, target) in enumerate(
            ((owner_hbm, owner_ref), (near_hbm, near_ref), (fold_hbm, fold_ref))
        )
    ]
    for copy in lists:
        copy.start()

    def fetch(pair):
        part = pl.ds(2 * pair, 2)
        return (
            pltpu.make_async_copy(tracers_hbm.at[part], tracers_all.at[part], sems.at[0, pair]),
            pltpu.make_async_copy(velocity_hbm.at[part], velocity_all.at[part], sems.at[1, pair]),
        )

    kmt_copy = pltpu.make_async_copy(kmt_hbm, kmt_ref, sems.at[0, PAIRS])
    kmt_copy.start()
    for pair in range(PAIRS):
        for copy in fetch(pair):
            copy.start()
    for copy in lists:
        copy.wait()
    table, up, chosen = table_of(owner_ref, near_ref, fold_ref)
    table_ref[...] = table
    sub, lane = iotas()
    flag = jnp.broadcast_to(up, (8, LANES))
    column = lane % SIDE
    base_near = column * IB + jnp.where(lane >= SIDE, IB - 1, 0)
    base_far = column * IB + jnp.where(lane >= SIDE, IB - 2, 1)
    near_tile, near_at = base_near // LANES, base_near % LANES
    far_tile, far_at = base_far // LANES, base_far % LANES
    kmt_copy.wait()
    near = jnp.zeros((16, LANES), jnp.float32)
    index16 = jnp.concatenate([near_at, near_at], axis=0)
    tile16 = jnp.concatenate([near_tile, near_tile], axis=0)

    def padded(t):
        return jnp.pad(load_rows(kmt_ref, t), ((0, 6), (0, 0)))

    for t in range(TILES):
        near = jnp.where(tile16 == t, take(padded(t), index16), near)
    south = padded(0)
    north = line(padded, (JB - 1) * IB, lane[0:1])
    for q in range(SLOTS):
        depth_rows[0, q] = row(south, q)
        depth_rows[1, q] = row(north, q)
        depth_rows[2, q] = row(near, q)
    aux_at = lane
    for s in range(8):
        move = {6: 28, 7: 14}.get(s, 90 if s % 2 == 0 else 52)
        aux_at = jnp.where((sub == s) & (lane >= IB), lane - move, aux_at)
    lane4 = lane[0:4]

    def one_pair(pair, carry):
        for copy in fetch(pair):
            copy.wait()
        tracers_ref, velocity_ref = tracers_all.at[pl.ds(2 * pair, 2)], velocity_all.at[pl.ds(2 * pair, 2)]
        for half in range(2):
            q = 2 * pair + half

            def tracer(t):
                return load4(tracers_ref, half, t)

            def speed(t):
                return load4(velocity_ref, half, t)

            packets = []
            for kind, (near, far) in enumerate(((0, 1), (JB - 1, JB - 2))):
                body = jnp.concatenate([line(tracer, near * IB, lane4), line(tracer, far * IB, lane4)], axis=0)
                v = line(speed, near * IB, lane4)
                v0, v1 = row(v, 2), row(v, 3)
                joint = jnp.where(lane >= 76, v0, pltpu.roll(v1, LANES - 14, 1))
                aux = jnp.where(sub == 6, joint, depth_rows[kind, q])
                aux = jnp.where(sub < 2, v0, jnp.where(sub < 4, v1, aux))
                packets.append(jnp.where(lane < IB, body, take(aux, aux_at)))
            up_ref[q] = jnp.where(flag, packets[1], packets[0])
            down_ref[q] = jnp.where(flag, packets[0], packets[1])
        near = far = drift = jnp.zeros((8, LANES), jnp.float32)
        for t in range(TILES):
            x = jnp.concatenate([load4(tracers_ref, 0, t), load4(tracers_ref, 1, t)], axis=0)
            v = jnp.concatenate([load4(velocity_ref, 0, t), load4(velocity_ref, 1, t)], axis=0)
            near = jnp.where(near_tile == t, take(x, near_at), near)
            far = jnp.where(far_tile == t, take(x, far_at), far)
            drift = jnp.where(near_tile == t, take(v, near_at), drift)
        for half in range(2):
            q = 2 * pair + half
            if half == 0:
                body = jnp.where(sub < 4, near, pltpu.roll(far, 4, 0))
                aux = drift
            else:
                body = jnp.where(sub < 4, pltpu.roll(near, 4, 0), far)
                aux = pltpu.roll(drift, 4, 0)
            aux = jnp.where(sub == 2, depth_rows[2, q], aux)
            sides_ref[2 * q] = jnp.where(lane < SIDE, body, pltpu.roll(aux, SIDE, 1))
            sides_ref[2 * q + 1] = jnp.where(lane < SIDE, pltpu.roll(body, SIDE, 1), aux)
        return carry

    lax.fori_loop(0, PAIRS, one_pair, 0)
    outputs = {"send_later": (up_ref, SLOTS), "send_earlier": (down_ref, SLOTS), "next": (next_ref, 0), "previous": (next_ref, 1)}
    for name, (ref, at) in outputs.items():
        which = jnp.broadcast_to(chosen[name], (8, LANES))
        packet = jnp.zeros((8, LANES), jnp.float32)
        for number in range(2 * SLOTS):
            packet = jnp.where(which == number + 1.0, sides_ref[number], packet)
        ref[at] = packet


def packet_shape(*lead):
    return jax.ShapeDtypeStruct(lead + (8, LANES), jnp.float32)


def front(block_owner, neighbours, fold_partner, tracers, velocity, kmt):
    vmem = pl.BlockSpec(memory_space=pltpu.VMEM)
    anywhere = pl.BlockSpec(memory_space=pltpu.HBM)
    return pl.pallas_call(
        front_kernel,
        out_shape=[
            jax.ShapeDtypeStruct((TABLE_ROWS, LANES), jnp.int32),
            packet_shape(PACK),
            packet_shape(PACK),
            packet_shape(2),
            packet_shape(2 * SLOTS),
        ],
        in_specs=[anywhere] * 6,
        out_specs=[vmem] * 5,
        scratch_shapes=[
            pltpu.VMEM((SLOTS, 4, CELLS), jnp.float32),
            pltpu.VMEM((SLOTS, 4, CELLS), jnp.float32),
            pltpu.VMEM((SLOTS, CELLS), jnp.float32),
            pltpu.VMEM((3, SLOTS, 8, LANES), jnp.float32),
            pltpu.SemaphoreType.DMA((2, PAIRS + 1)),
            pltpu.VMEM((SLOTS, LANES), jnp.int32),
            pltpu.VMEM((4, SLOTS * LANES), jnp.int32),
            pltpu.VMEM((SLOTS, LANES), jnp.int32),
            pltpu.SemaphoreType.DMA((3,)),
        ],
        compiler_params=pltpu.CompilerParams(vmem_limit_bytes=BIG),
        name="front",
    )(block_owner.reshape(-1, LANES), neighbours.T, fold_partner.reshape(-1, LANES), tracers, velocity, kmt)


def coordinates(index):
    index = lax.rem(index + DEVICES, DEVICES)
    return (index // 4, lax.rem(index, 4))


PARTNERS = [sign * step for step in [1, 2, 3] + [STRIDE * a for a in range(1, HOPS)] for sign in (1, -1)]
HIGH, LOW = DEVICES - FOLD_REACH, FOLD_REACH


def exchange_kernel(table_ref, up_ref, down_ref, next_ref, tracers_hbm, velocity_hbm, kappa_hbm, kmt_hbm, halo_ref, beside_ref,
                    partial_ref, edges_ref, rows_ref, spot_ref, kind_ref, window, message, extra_message, arrived,
                    extra_arrived, send_sem, recv_sem, extra_send, extra_recv, later_send, later_recv, last_send, last_recv,
                    tracers_all, velocity_all, kappa_ref, kmt_ref, xs, us, vs, all_ds, all_ks, ws, gs, place_ref, load_sem):
    me = position()
    loads = [
        pltpu.make_async_copy(source, target, load_sem.at[number])
        for number, (source, target) in enumerate(
            ((kmt_hbm, kmt_ref), (kappa_hbm, kappa_ref), (tracers_hbm, tracers_all), (velocity_hbm, velocity_all))
        )
    ]
    for copy in loads:
        copy.start()
    barrier = pltpu.get_barrier_semaphore()
    for offset in PARTNERS:
        pl.semaphore_signal(barrier, inc=1, device_id=coordinates(me + offset), device_id_type=MESH)
    pl.semaphore_wait(barrier, len(PARTNERS))

    def remote(source, target, sends, recvs, number, offset):
        return pltpu.make_async_remote_copy(
            src_ref=source,
            dst_ref=target,
            send_sem=sends.at[number],
            recv_sem=recvs.at[number],
            device_id=coordinates(me + offset),
            device_id_type=MESH,
        )

    plan = []
    for a in range(HOPS - 1, 0, -1):
        plan.append((up_ref, window.at[pl.ds(a * PACK, PACK)], STRIDE * a))
        if a < STRIDE:
            plan.append((down_ref, window.at[pl.ds(OWN_DOWN + a * PACK, PACK)], -a))
    plan.append((next_ref.at[0], beside_ref.at[0], 1))
    plan.append((next_ref.at[1], beside_ref.at[1], -1))
    copies = [
        remote(source, target, send_sem, recv_sem, number, offset)
        for number, (source, target, offset) in enumerate(plan)
    ]
    for copy in copies:
        copy.start()

    def fold_copy(k, downwards):
        target = window.at[pl.ds(EXTRA + (k - 1) * PACK, PACK)]
        if downwards:
            return remote(up_ref, target, extra_send, extra_recv, k - 1, -k)
        return remote(down_ref, target, extra_send, extra_recv, k - 1, STRIDE * k)

    for k in range(1, EXTRAS + 1):
        @pl.when(me >= HIGH)
        def _():
            fold_copy(k, True).start()

        @pl.when(me < LOW)
        def _():
            fold_copy(k, False).start()

        from_high = (me + k >= HIGH) & (me + k < DEVICES)
        from_low = (me - STRIDE * k >= 0) & (me - STRIDE * k < LOW)

        @pl.when(jnp.logical_not(from_high | from_low))
        def _():
            window[pl.ds(EXTRA + (k - 1) * PACK, PACK)] = jnp.zeros((PACK, 8, LANES), jnp.float32)

    window[pl.ds(0, PACK)] = up_ref[...]
    window[pl.ds(OWN_DOWN, PACK)] = down_ref[...]
    window[EMPTY] = jnp.zeros((8, LANES), jnp.float32)
    loads[0].wait()
    loads[1].wait()
    prepare(kappa_ref, kmt_ref, xs, us, vs, all_ds, all_ks, place_ref, spot_ref, kind_ref)
    loads[2].wait()
    loads[3].wait()

    def one_pair(pair, carry):
        part = pl.ds(2 * pair, 2)
        interior(
            tracers_all.at[part], velocity_all.at[part], xs, us, vs, all_ds.at[pair], all_ks.at[pair], ws, gs,
            place_ref, partial_ref.at[pair], edges_ref.at[pair], rows_ref.at[pair],
        )
        return carry

    lax.fori_loop(0, EARLY, one_pair, 0)
    for copy in copies:
        copy.wait()
    for k in range(1, EXTRAS + 1):
        @pl.when(me >= HIGH)
        def _():
            fold_copy(k, True).wait_send()

        @pl.when(me < LOW)
        def _():
            fold_copy(k, False).wait_send()

        @pl.when((me + k >= HIGH) & (me + k < DEVICES))
        def _():
            fold_copy(k, True).wait_recv()

        @pl.when((me - STRIDE * k >= 0) & (me - STRIDE * k < LOW))
        def _():
            fold_copy(k, False).wait_recv()

    def fill(number, halo_name, wrap_name):
        wrap = EMPTY
        for q in range(SLOTS):
            r = number * SLOTS + q
            message[number, q] = window[table_ref[r, AT[halo_name]]]
            wrap = wrap + table_ref[r, AT[wrap_name]]
        message[number, SLOTS] = window[wrap]

    later = []
    for number in [STRIDE + a for a in range(HOPS - 1, 0, -1)] + [1, 2, 3]:
        onward = number < STRIDE
        fill(number, *(("behind", "earlier") if onward else ("ahead", "later")))
        offset = number if onward else -STRIDE * (number - STRIDE)
        copy = remote(message.at[number], arrived.at[number], later_send, later_recv, number, offset)
        copy.start()
        later.append(copy)

    def last_copy(k, onward):
        offset = k if onward else -STRIDE * k
        return remote(extra_message.at[k], extra_arrived.at[k], last_send, last_recv, k, offset)

    def to_high(k):
        return (me + k >= HIGH) & (me + k < DEVICES)

    def to_low(k):
        return (me - STRIDE * k >= 0) & (me - STRIDE * k < LOW)

    for k in range(STRIDE):
        for goes, number in ((to_high(k), k), (to_low(k), STRIDE + k)):
            @pl.when(goes)
            def _():
                for q in range(SLOTS):
                    extra_message[k, q] = window[table_ref[number * SLOTS + q, AT["extra"]]]
                if k > 0:
                    last_copy(k, number < STRIDE).start()

    fill(0, "behind", "earlier")
    fill(STRIDE, "ahead", "later")
    lax.fori_loop(EARLY, PAIRS, one_pair, 0)
    for copy in later:
        copy.wait()
    flag = own_row(table_ref, 0, "up") > 0
    for q in range(PACK):
        behind = message[0, q]
        for number in range(1, STRIDE):
            behind = behind + arrived[number, q]
        ahead = message[STRIDE, q]
        for number in range(STRIDE + 1, TARGETS):
            ahead = ahead + arrived[number, q]
        if q < SLOTS:
            halo_ref[q] = jnp.where(flag, behind, ahead)
            halo_ref[SLOTS + q] = jnp.where(flag, ahead, behind)
        else:
            halo_ref[2 * SLOTS] = behind
            halo_ref[2 * SLOTS + 1] = ahead
    for k in range(1, STRIDE):
        for goes, onward in ((to_high(k), True), (to_low(k), False)):
            @pl.when(goes)
            def _():
                last_copy(k, onward).wait_send()

        for comes, onward in ((me >= HIGH, True), (me < LOW, False)):
            @pl.when(comes)
            def _():
                last_copy(k, onward).wait_recv()

    @pl.when((me >= HIGH) | (me < LOW))
    def _():
        for q in range(SLOTS):
            value = extra_message[0, q]
            for k in range(1, STRIDE):
                value = value + extra_arrived[k, q]
            halo_ref[SLOTS + q] = halo_ref[SLOTS + q] + value


def exchange(table, up, down, beside, tracers, velocity, kappa, kmt):
    vmem = pl.BlockSpec(memory_space=pltpu.VMEM)
    anywhere = pl.BlockSpec(memory_space=pltpu.HBM)

    def packets(*lead):
        return pltpu.VMEM(lead + (8, LANES), jnp.float32)

    def tiles(*lead):
        return pltpu.VMEM(lead[:-1] + (8, lead[-1] * LANES), jnp.float32)

    def sems(count):
        return [pltpu.SemaphoreType.DMA((count,))] * 2

    cells = jax.ShapeDtypeStruct((8, TILES * LANES), jnp.int32)
    return pl.pallas_call(
        exchange_kernel,
        out_shape=[
            packet_shape(WANT),
            packet_shape(2),
            jax.ShapeDtypeStruct((PAIRS, 8, TILES * LANES), jnp.float32),
            packet_shape(PAIRS, 8),
            packet_shape(PAIRS, 16),
            cells,
            cells,
        ],
        in_specs=[pl.BlockSpec(memory_space=pltpu.SMEM)] + [vmem] * 3 + [anywhere] * 4,
        out_specs=[vmem] * 7,
        scratch_shapes=[
            packets(WINDOW),
            packets(TARGETS, PACK),
            packets(STRIDE, SLOTS),
            packets(TARGETS, PACK),
            packets(STRIDE, SLOTS),
            *sems(HOPS - 1 + EXTRAS + 2),
            *sems(EXTRAS),
            *sems(TARGETS),
            *sems(STRIDE),
            pltpu.VMEM((SLOTS, 4, CELLS), jnp.float32),
            pltpu.VMEM((SLOTS, 4, CELLS), jnp.float32),
            pltpu.VMEM((SLOTS, CELLS), jnp.float32),
            pltpu.VMEM((SLOTS, CELLS), jnp.float32),
            tiles(FRAME),
            tiles(FRAME),
            tiles(FRAME),
            tiles(PAIRS, FRAME),
            tiles(PAIRS, TILES),
            tiles(TILES),
            tiles(TILES),
            pltpu.VMEM((8, TILES * LANES), jnp.int32),
            pltpu.SemaphoreType.DMA((4,)),
        ],
        compiler_params=pltpu.CompilerParams(collective_id=0, has_side_effects=True, vmem_limit_bytes=BIG),
        name="exchange",
    )(table, up, down, beside, tracers, velocity, kappa, kmt)


def flux(w, far_a, a, b, far_b):
    return jnp.maximum(w, 0.0) * (5.0 * a + 2.0 * b - far_a) + jnp.minimum(w, 0.0) * (2.0 * a + 5.0 * b - far_b)


def wetness(d):
    sub, _ = iotas()
    return jnp.clip(d - (sub % 2).astype(jnp.float32), 0.0, 1.0)


def swap(z):
    sub, _ = iotas()
    return jnp.where(sub % 2 == 1, pltpu.roll(z, 1, 0), pltpu.roll(z, 7, 0))


def prepare(kappa_ref, kmt_ref, xs, us, vs, all_ds, all_ks, place_ref, spot_ref, kind_ref):
    sub, lane = iotas()
    zero = jnp.zeros((8, LANES), jnp.float32)
    for t in (0, 1, 45, 46):
        for ref in (xs, us, vs):
            ref[:, lanes_at(t)] = zero
        for p in range(PAIRS):
            all_ds[p, :, lanes_at(t)] = zero

    def one_tile(t, rows_kappa, rows_kmt):
        flat = lane + t * LANES
        j = ((flat.astype(jnp.float32) + 0.5) * (1.0 / IB)).astype(jnp.int32)
        i = flat - j * IB
        place_ref[:, lanes_at(t)] = i
        spot_ref[:, lanes_at(t)] = j + jnp.where(i >= IB // 2, SIDE, 0)
        kind_ref[:, lanes_at(t)] = jnp.where(
            (i == 0) | (i == IB - 1), 1, jnp.where((i == 1) | (i == IB - 2), 2, 0)
        )
        for p in range(PAIRS):
            for rows, ref, at in ((rows_kmt, all_ds, t + 2), (rows_kappa, all_ks, t)):
                ref[p, :, lanes_at(at)] = jnp.where(sub < 4, row(rows, 2 * p), row(rows, 2 * p + 1))

    for t in range(TILES):
        one_tile(t, load_rows(kappa_ref, t), load_rows(kmt_ref, t))


def interior(tracers_ref, velocity_ref, xs, us, vs, ds, ks, ws, gs, place_ref, partial_ref, edges_ref, rows_ref):
    sub, lane = iotas()
    lower_half = sub % 4 < 2
    column = lane % SIDE
    base_near = column * IB + jnp.where(lane >= SIDE, IB - 1, 0)
    base_far = column * IB + jnp.where(lane >= SIDE, IB - 2, 1)
    bases = (base_near // LANES, base_near % LANES), (base_far // LANES, base_far % LANES)
    for t in range(TILES):
        xs[:, lanes_at(t + 2)] = jnp.concatenate([load4(tracers_ref, 0, t), load4(tracers_ref, 1, t)], axis=0)
        speed = jnp.concatenate([load4(velocity_ref, 0, t), load4(velocity_ref, 1, t)], axis=0)
        us[:, lanes_at(t + 2)] = jnp.where(lower_half, speed, pltpu.roll(speed, 2, 0))
        vs[:, lanes_at(t + 2)] = jnp.where(lower_half, pltpu.roll(speed, 6, 0), speed)
    turned = {}

    def tile_of(name, ref, tile):
        if (name, tile, 0) not in turned:
            turned[name, tile, 0] = ref[:, lanes_at(tile)]
        return turned[name, tile, 0]

    def turn(name, ref, tile, r):
        if (name, tile, r) not in turned:
            turned[name, tile, r] = pltpu.roll(tile_of(name, ref, tile), LANES - r, 1)
        return turned[name, tile, r]

    def shift(name, ref, t, s):
        tile = t + 2 + s // LANES
        r = s % LANES
        return jnp.where(lane < LANES - r, turn(name, ref, tile, r), turn(name, ref, tile + 1, r))

    edges = [jnp.zeros((8, LANES), jnp.float32)] * 8
    for t in range(TILES):
        for key in [k for k in turned if k[1] < t]:
            del turned[key]
        i = place_ref[:, lanes_at(t)]
        x, u, v = (tile_of(name, ref, t + 2) for name, ref in (("x", xs), ("u", us), ("v", vs)))
        wet = wetness(tile_of("d", ds, t + 2))
        west = jnp.where(i == 0, 0.0, shift("x", xs, t, -1))
        west_far = jnp.where(i <= 1, 0.0, shift("x", xs, t, -2))
        east = jnp.where(i == IB - 1, 0.0, shift("x", xs, t, 1))
        east_far = jnp.where(i >= IB - 2, 0.0, shift("x", xs, t, 2))
        wet_west = jnp.where(i == 0, 0.0, wetness(shift("d", ds, t, -1)))
        wet_east = jnp.where(i == IB - 1, 0.0, wetness(shift("d", ds, t, 1)))
        wet_south = wetness(shift("d", ds, t, -IB))
        wet_north = wetness(shift("d", ds, t, IB))
        south, south_far = shift("x", xs, t, -IB), shift("x", xs, t, -2 * IB)
        north, north_far = shift("x", xs, t, IB), shift("x", xs, t, 2 * IB)
        flux_east = flux((u + shift("u", us, t, 1)) * (wet * wet_east), west, x, east, east_far)
        flux_west = flux((shift("u", us, t, -1) + u) * (wet_west * wet), west_far, west, x, east)
        flux_north = flux((v + shift("v", vs, t, IB)) * (wet * wet_north), south, x, north, north_far)
        flux_south = flux((shift("v", vs, t, -IB) + v) * (wet_south * wet), south_far, south, x, north)
        divergence = flux_east - flux_west + (flux_north - flux_south)
        explicit = x - (wet * (COURANT / 12.0)) * divergence
        coupling = ks[:, lanes_at(t)] * wet * swap(wet)
        share = coupling / (1.0 + 2.0 * coupling)
        partial_ref[:, lanes_at(t)] = explicit + share * (swap(explicit) - explicit)
        ws[:, lanes_at(t)] = wet
        gs[:, lanes_at(t)] = share
        for k, (tile, at) in enumerate(bases):
            here = tile == t
            for n, value in enumerate((x, u, wet, share)):
                edges[2 * n + k] = jnp.where(here, take(value, at), edges[2 * n + k])
    for n in range(8):
        edges_ref[n] = edges[n]
    for k, number in enumerate((0, 1, JB - 1, JB - 2)):
        for n, (ref, offset) in enumerate(((xs, 2), (vs, 2), (ws, 0), (gs, 0))):
            rows_ref[4 * k + n] = line(lambda t: ref[:, lanes_at(t + offset)], number * IB, lane)


def finish_kernel(table_ref, halo, sides_ref, beside_ref, partial_ref, edges_ref, rows_ref, spot_ref, kind_ref, out_hbm,
                  around, out_ref, sems):
    for number in range(2 * SLOTS):
        around[number] = sides_ref[number]
    around[2 * SLOTS] = beside_ref[0]
    around[2 * SLOTS + 1] = beside_ref[1]
    around[2 * SLOTS + 2] = halo[2 * SLOTS]
    around[2 * SLOTS + 3] = halo[2 * SLOTS + 1]
    around[2 * SLOTS + 4] = jnp.zeros((8, LANES), jnp.float32)

    def store(pair):
        part = pl.ds(2 * pair, 2)
        return pltpu.make_async_copy(out_ref.at[part], out_hbm.at[part], sems.at[pair])

    def one_pair(pair, carry):
        finish_pair(
            pair, table_ref, halo, around, partial_ref.at[pair], edges_ref.at[pair], rows_ref.at[pair], spot_ref, kind_ref,
            out_ref.at[pl.ds(2 * pair, 2)],
        )
        store(pair).start()
        return carry

    lax.fori_loop(0, PAIRS, one_pair, 0)
    for pair in range(PAIRS):
        store(pair).wait()


def finish_pair(pair, table_ref, halo, around, partial_ref, edges_ref, rows_ref, spot_ref, kind_ref, out_ref):
    sub, lane = iotas()
    upper = sub < 4
    odd = sub % 2 == 1

    def paired(first, second):
        return jnp.where(upper, first, second)

    def across(first, second):
        near = jnp.where(upper, first, pltpu.roll(second, 4, 0))
        return near, jnp.where(upper, pltpu.roll(first, 4, 0), second)

    def unpack(packet):
        a, b = pltpu.roll(packet, 38, 1), pltpu.roll(packet, 76, 1)
        c, d = pltpu.roll(packet, 100, 1), pltpu.roll(packet, 114, 1)

        def joined(first, second, third):
            return jnp.where(lane < 38, first, jnp.where(lane < 76, second, third))

        speed = jnp.where(odd, joined(row(a, 2), row(b, 3), row(d, 6)), joined(row(a, 0), row(b, 1), row(c, 6)))
        return speed, joined(row(a, 4), row(b, 5), row(d, 7))

    def rows_from(first, second):
        near, far = across(first, second)
        (speed_a, depth_a), (speed_b, depth_b) = unpack(first), unpack(second)
        return near, far, paired(speed_a, speed_b), paired(depth_a, depth_b)

    slots = (2 * pair, 2 * pair + 1)
    south = rows_from(halo[slots[0]], halo[slots[1]])
    north = rows_from(halo[SLOTS + slots[0]], halo[SLOTS + slots[1]])
    folded = paired(*(own_row(table_ref, q, "fold") for q in slots)) > 0
    back = jnp.where(lane < IB, IB - 1 - lane, lane)
    north = [
        jnp.where(folded, sign * take(value, back), value) for value, sign in zip(north, (1.0, 1.0, -1.0, 1.0))
    ]
    bodies, speeds, depths = [], [], []
    for q in slots:
        west, east = (around[own_row(table_ref, q, name)] for name in ("west", "east"))
        bodies.append(jnp.where(lane < SIDE, west, pltpu.roll(east, SIDE, 1)))
        aux = jnp.where(lane < SIDE, pltpu.roll(west, SIDE, 1), east)
        speeds.append(jnp.where(odd, row(aux, 1), row(aux, 0)))
        depths.append(row(aux, 2))
    side_near, side_far = across(*bodies)
    side_speed, side_depth = paired(*speeds), paired(*depths)
    keep = paired(*(own_row(table_ref, q, "live") for q in slots)) > 0

    def boundary(sign, halo_near, halo_far, halo_speed, halo_depth, own):
        (x_near, x_far), (speed_near, speed_far), (wet_near, wet_far), (share_near, share_far) = own
        outer = sign * (halo_speed + speed_near) * (wetness(halo_depth) * wet_near)
        inner = sign * (speed_near + speed_far) * (wet_near * wet_far)
        lost = jnp.minimum(inner, 0.0) * halo_near
        near = -(COURANT / 12.0) * wet_near * (flux(outer, x_far, x_near, halo_near, halo_far) + lost)
        far = (COURANT / 12.0) * wet_far * lost
        return near + share_near * (swap(near) - near), far + share_far * (swap(far) - far)

    edges = [edges_ref[n] for n in range(8)]
    rows = [rows_ref[n] for n in range(16)]
    side_sign = jnp.where(lane < SIDE, -1.0, 1.0)
    side = boundary(side_sign, side_near, side_far, side_speed, side_depth, [edges[2 * n : 2 * n + 2] for n in range(4)])
    add_south = boundary(-1.0, *south, list(zip(rows[0:4], rows[4:8])))
    add_north = boundary(1.0, *north, list(zip(rows[8:12], rows[12:16])))
    pieces = {}
    for start, value in zip((0, IB, (JB - 1) * IB, (JB - 2) * IB), (*add_south, *add_north)):
        first, at = start // LANES, start % LANES
        moved = pltpu.roll(value, at, 1) if at else value
        pieces.setdefault(first, []).append((moved, (lane >= at) & (lane < at + IB)))
        if at + IB > LANES:
            pieces.setdefault(first + 1, []).append((moved, lane < at + IB - LANES))
    for t in range(TILES):
        kind, index = kind_ref[:, lanes_at(t)], spot_ref[:, lanes_at(t)]
        value = partial_ref[:, lanes_at(t)]
        value = value + jnp.where(kind == 1, take(side[0], index), jnp.where(kind == 2, take(side[1], index), 0.0))
        for moved, mask in pieces.get(t, []):
            value = value + jnp.where(mask, moved, 0.0)
        value = jnp.where(keep, value, 0.0)
        width = min(LANES, CELLS - t * LANES)
        out_ref[0, :, pl.ds(t * LANES, width)] = value[0:4, :width]
        out_ref[1, :, pl.ds(t * LANES, width)] = value[4:8, :width]


def finish(table, halo, sides, beside, partial, edges, rows, spot, kind):
    vmem = pl.BlockSpec(memory_space=pltpu.VMEM)
    return pl.pallas_call(
        finish_kernel,
        out_shape=jax.ShapeDtypeStruct((SLOTS, 4, CELLS), jnp.float32),
        in_specs=[pl.BlockSpec(memory_space=pltpu.SMEM)] + [vmem] * 8,
        out_specs=pl.BlockSpec(memory_space=pltpu.HBM),
        scratch_shapes=[
            pltpu.VMEM((2 * SLOTS + 5, 8, LANES), jnp.float32),
            pltpu.VMEM((SLOTS, 4, CELLS), jnp.float32),
            pltpu.SemaphoreType.DMA((PAIRS,)),
        ],
        compiler_params=pltpu.CompilerParams(vmem_limit_bytes=BIG),
        name="final",
    )(table, halo, sides, beside, partial, edges, rows, spot, kind)


def per_device(tracers, velocity, kappa, kmt, block_owner, neighbours, fold_partner):
    table, up, down, beside, sides = front(block_owner, neighbours, fold_partner, tracers, velocity, kmt)
    halo, beside, *work = exchange(table, up, down, beside, tracers, velocity, kappa, kmt)
    return finish(table, halo, sides, beside, *work)


def solution(mesh):
    placed = (
        P(("blk", "sub"), None, None),
        P(("blk", "sub"), None, None),
        P(("blk", "sub"), None),
        P(("blk", "sub"), None),
        P(),
        P(),
        P(),
    )
    return jax.shard_map(
        per_device,
        mesh=mesh,
        in_specs=placed,
        out_specs=P(("blk", "sub"), None, None),
        check_vma=False,
    )
```

time: 1260 us -> 40.3 us (0.03); the launches traced: 1240 us -> 40.1 us
  starting transfers between devices: 742 us -> 0 us
  waiting for transfers between devices: 321 us -> 0 us
  local copies, waits for them, and re-layouts: 160 us -> 0 us
  Pallas kernels: 0 us -> 40 us
  other arithmetic: 18.8 us -> 0 us
    ppermute x108 -> x0, starting transfers between devices: 742 us -> none  [shifted(): return lax.ppermute(block, axis, route)]
    ppermute x108 -> x0, waiting for transfers between devices: 321 us -> none  [shifted(): return lax.ppermute(block, axis, route)]
    unnamed x127 -> x0, local copies, waits for them, and re-layouts: 81.1 us -> none
    pallas_call x0 -> x3, Pallas kernels: none -> 40 us  [the longest x1 29.5 us: exchange(): pl.pallas_call(exchange_kernel, out_shape=[packet_shape(WANT), packet_sha...]
    another operation x13 -> x0, local copies, waits for them, and re-layouts: 19.1 us -> none  [the longest x2 7.12 us: extend(): west_halo = sources[:, 0, :, strip:2 * strip].reshape(count, chans, rows, 2)]
    slice x14 -> x0, local copies, waits for them, and re-layouts: 17.9 us -> none  [the longest x3 8.84 us: edge_pack(): west_edge = block_field[:, :, :, 0:2].reshape(count, chans, rows * 2)]
    scatter x1 -> x0, local copies, waits for them, and re-layouts: 16.2 us -> none  [per_device(): slot_block = jnp.full((slot_total,), -1, jnp.int32).at[block_owner].set(j...]
  transfers between devices with their start and end apart: 108 -> 0, of which waited for: 64 -> 0; matrix products, arithmetic and copies ran while one was open for 10% -> 0% of each run, Pallas kernels for 0% -> 0%
where the time goes in v3:
time: 40.3 us; the launch traced here: 40.1 us
  Pallas kernels  40 us (99%)
    pallas_call x1, Pallas kernels, exchange(): pl.pallas_call(exchange_kernel, out_shape=[packet_shape(WANT), packet_sha...  29.5 us
    pallas_call x1, Pallas kernels, front(): pl.pallas_call(front_kernel, out_shape=[jax.ShapeDtypeStruct((TABLE_ROWS,...  6.06 us
    pallas_call x1, Pallas kernels, finish(): pl.pallas_call(finish_kernel, out_shape=jax.ShapeDtypeStruct((SLOTS, 4, C...  4.46 us

profile of v3, /device:TPU:1, one launch (start us, length us, event | category | flops | bytes accessed | tf_op | source)
XLA Modules:
  0.0 40.1 jit_solution(13006197535128927502)
XLA Ops:
  0.0 6.1 %front.1 = (s32[112,128]{1,0:T(8,128)}, f32[11,8,128]{2,1,0:T(8,128)}, f32[11,8,128]{2,1,0:T(8,128)}, f32[2,8,128]{2,1,0:T(8,128)}, f32[20,8,128]{2,1,0:T(8,128)}) custom-call(s32[10,128]{1,0:T(8,128)} %bitcast.4, s32[4,1280]{1,0:T(4,128)} %bitcast.3, s32[10,128]{1,0:T(8,128)} %bitcast.5, f32[10,4,5400]{2,1,0:T(4,128)} %tracers_hbm.3, ...), custom_call_target="tpu_custom_call" | custom-call | tf_op jit(solution)/shard_map/front/pallas_call | solution.py:307
  6.1 29.5 %exchange.1 = (f32[22,8,128]{2,1,0:T(8,128)}, f32[2,8,128]{2,1,0:T(8,128)}, f32[5,8,5504]{2,1,0:T(8,128)}, f32[5,8,8,128]{3,2,1,0:T(8,128)}, f32[5,16,8,128]{3,2...) custom-call(s32[112,128]{1,0:T(8,128)} %get-tuple-element.17.table_ref, f32[11,8,128]{2,1,0:T(8,128)} %get-tuple-element.18.up_ref, ...), custom_call_target="tpu_custom_call" | custom-call | tf_op jit(solution)/shard_map/exchange/pallas_call | solution.py:533
  35.6 4.5 %final.1 = f32[10,4,5400]{2,1,0:T(4,128)} custom-call(s32[112,128]{1,0:T(8,128)} %get-tuple-element.17.table_ref, f32[22,8,128]{2,1,0:T(8,128)} %get-tuple-element.21.halo, f32[20,8,128]{2,1,0:T(8,128)} %get-tuple-element.22.sides_ref, f32[2,8,128]{2,1,0:T(8,128)} %get-tuple-element.23.beside_ref, f32[5,8,5504]{2,1,0:T(8,128)} %get-tuple-element.24.partial_ref, ...), custom_call_target="tpu_custom_call" | custom-call | tf_op jit(solution)/shard_map/final/pallas_call | solution.py:792

commit v4 on v3

--- a/solution.py
+++ b/solution.py
@@ -28,6 +28,7 @@
 TARGETS = STRIDE + HOPS
 TABLE_ROWS = 112
 EARLY = 2
+EDGES = 24
 BIG = 63 << 20
 FOLD_REACH = 14
 MESH = pl.DeviceIdType.MESH
@@ -139,11 +140,13 @@
         index = jnp.where(linked & (apart == 0), place * 2.0 + (1.0 - side), 24.0)
         index = jnp.where(before, 20.0, jnp.where(after, 21.0, index))
         index = jnp.where(earlier, 22.0, jnp.where(later, 23.0, index))
-        sides.append(index)
+        sides.append(jnp.clip(index, 0.0, 24.0))
     columns.update(
         behind=behind, ahead=ahead, extra=extra, west=sides[0], east=sides[1], live=live,
         fold=jnp.where(links[4] >= 0, 1.0, 0.0), up=jnp.where(up, 1.0, 0.0),
     )
+    for name in ("behind", "ahead", "extra"):
+        columns[name] = jnp.clip(columns[name], 0.0, empty)
     lane = lax.broadcasted_iota(jnp.int32, (rows, LANES), 1)
     result = jnp.zeros((rows, LANES), jnp.float32)
     for name, at in AT.items():
@@ -186,34 +189,7 @@
 ROW_STARTS = (0, IB, (JB - 1) * IB, (JB - 2) * IB)
 
 
-def front_kernel(owner_hbm, near_hbm, fold_hbm, tracers_hbm, velocity_hbm, kmt_hbm, table_ref, up_ref, down_ref, next_ref,
-                 sides_ref, tracers_all, velocity_all, kmt_ref, depth_rows, sems,
-                 owner_ref, near_ref, fold_ref, list_sems):
-    lists = [
-        pltpu.make_async_copy(source, target, list_sems.at[number])
-        for number, (source, target) in enumerate(
-            ((owner_hbm, owner_ref), (near_hbm, near_ref), (fold_hbm, fold_ref))
-        )
-    ]
-    for copy in lists:
-        copy.start()
-
-    def fetch(pair):
-        part = pl.ds(2 * pair, 2)
-        return (
-            pltpu.make_async_copy(tracers_hbm.at[part], tracers_all.at[part], sems.at[0, pair]),
-            pltpu.make_async_copy(velocity_hbm.at[part], velocity_all.at[part], sems.at[1, pair]),
-        )
-
-    kmt_copy = pltpu.make_async_copy(kmt_hbm, kmt_ref, sems.at[0, PAIRS])
-    kmt_copy.start()
-    for pair in range(PAIRS):
-        for copy in fetch(pair):
-            copy.start()
-    for copy in lists:
-        copy.wait()
-    table, up, chosen = table_of(owner_ref, near_ref, fold_ref)
-    table_ref[...] = table
+def pack_edges(fetch, loads, up, chosen, tracers_all, velocity_all, kmt_ref, up_ref, down_ref, next_ref, sides_ref, depth_rows):
     sub, lane = iotas()
     flag = jnp.broadcast_to(up, (8, LANES))
     column = lane % SIDE
@@ -221,7 +197,7 @@
     base_far = column * IB + jnp.where(lane >= SIDE, IB - 2, 1)
     near_tile, near_at = base_near // LANES, base_near % LANES
     far_tile, far_at = base_far // LANES, base_far % LANES
-    kmt_copy.wait()
+    loads["kmt"].wait()
     near = jnp.zeros((16, LANES), jnp.float32)
     index16 = jnp.concatenate([near_at, near_at], axis=0)
     tile16 = jnp.concatenate([near_tile, near_tile], axis=0)
@@ -301,36 +277,6 @@
     return jax.ShapeDtypeStruct(lead + (8, LANES), jnp.float32)
 
 
-def front(block_owner, neighbours, fold_partner, tracers, velocity, kmt):
-    vmem = pl.BlockSpec(memory_space=pltpu.VMEM)
-    anywhere = pl.BlockSpec(memory_space=pltpu.HBM)
-    return pl.pallas_call(
-        front_kernel,
-        out_shape=[
-            jax.ShapeDtypeStruct((TABLE_ROWS, LANES), jnp.int32),
-            packet_shape(PACK),
-            packet_shape(PACK),
-            packet_shape(2),
-            packet_shape(2 * SLOTS),
-        ],
-        in_specs=[anywhere] * 6,
-        out_specs=[vmem] * 5,
-        scratch_shapes=[
-            pltpu.VMEM((SLOTS, 4, CELLS), jnp.float32),
-            pltpu.VMEM((SLOTS, 4, CELLS), jnp.float32),
-            pltpu.VMEM((SLOTS, CELLS), jnp.float32),
-            pltpu.VMEM((3, SLOTS, 8, LANES), jnp.float32),
-            pltpu.SemaphoreType.DMA((2, PAIRS + 1)),
-            pltpu.VMEM((SLOTS, LANES), jnp.int32),
-            pltpu.VMEM((4, SLOTS * LANES), jnp.int32),
-            pltpu.VMEM((SLOTS, LANES), jnp.int32),
-            pltpu.SemaphoreType.DMA((3,)),
-        ],
-        compiler_params=pltpu.CompilerParams(vmem_limit_bytes=BIG),
-        name="front",
-    )(block_owner.reshape(-1, LANES), neighbours.T, fold_partner.reshape(-1, LANES), tracers, velocity, kmt)
-
-
 def coordinates(index):
     index = lax.rem(index + DEVICES, DEVICES)
     return (index // 4, lax.rem(index, 4))
@@ -340,22 +286,50 @@
 HIGH, LOW = DEVICES - FOLD_REACH, FOLD_REACH
 
 
-def exchange_kernel(table_ref, up_ref, down_ref, next_ref, tracers_hbm, velocity_hbm, kappa_hbm, kmt_hbm, halo_ref, beside_ref,
-                    partial_ref, edges_ref, rows_ref, spot_ref, kind_ref, window, message, extra_message, arrived,
-                    extra_arrived, send_sem, recv_sem, extra_send, extra_recv, later_send, later_recv, last_send, last_recv,
-                    tracers_all, velocity_all, kappa_ref, kmt_ref, xs, us, vs, all_ds, all_ks, ws, gs, place_ref, load_sem):
+def exchange_kernel(owner_hbm, near_hbm, fold_hbm, tracers_hbm, velocity_hbm, kappa_hbm, kmt_hbm, table_out, halo_ref,
+                    beside_ref, sides_ref, partial_hbm, edges_hbm, up_ref, down_ref, next_ref, window, message,
+                    extra_message, arrived, extra_arrived, send_sem, recv_sem, extra_send, extra_recv, later_send, later_recv,
+                    last_send, last_recv, owner_ref, near_ref, fold_ref, tracers_all, velocity_all, kappa_ref, kmt_ref,
+                    depth_rows, table_ref, xs, us, vs, all_ds, all_ks, ws, gs, place_ref, partial_all, edges_all, load_sem,
+                    pair_sem, out_sem):
     me = position()
-    loads = [
-        pltpu.make_async_copy(source, target, load_sem.at[number])
-        for number, (source, target) in enumerate(
-            ((kmt_hbm, kmt_ref), (kappa_hbm, kappa_ref), (tracers_hbm, tracers_all), (velocity_hbm, velocity_all))
-        )
-    ]
-    for copy in loads:
-        copy.start()
     barrier = pltpu.get_barrier_semaphore()
     for offset in PARTNERS:
         pl.semaphore_signal(barrier, inc=1, device_id=coordinates(me + offset), device_id_type=MESH)
+    sources = {
+        "owner": (owner_hbm, owner_ref),
+        "near": (near_hbm, near_ref),
+        "fold": (fold_hbm, fold_ref),
+        "kmt": (kmt_hbm, kmt_ref),
+        "kappa": (kappa_hbm, kappa_ref),
+    }
+    loads = {
+        name: pltpu.make_async_copy(source, target, load_sem.at[number])
+        for number, (name, (source, target)) in enumerate(sources.items())
+    }
+
+    def fetch(pair):
+        part = pl.ds(2 * pair, 2)
+        return (
+            pltpu.make_async_copy(tracers_hbm.at[part], tracers_all.at[part], pair_sem.at[0, pair]),
+            pltpu.make_async_copy(velocity_hbm.at[part], velocity_all.at[part], pair_sem.at[1, pair]),
+        )
+
+    for name in ("owner", "near", "fold", "kmt"):
+        loads[name].start()
+    for pair in range(PAIRS):
+        for copy in fetch(pair):
+            copy.start()
+    loads["kappa"].start()
+    for name in ("owner", "near", "fold"):
+        loads[name].wait()
+    table, up, chosen = table_of(owner_ref, near_ref, fold_ref)
+    table_out[...] = table
+    table_copy = pltpu.make_async_copy(table_out, table_ref, load_sem.at[len(sources)])
+    table_copy.start()
+    pack_edges(
+        fetch, loads, up, chosen, tracers_all, velocity_all, kmt_ref, up_ref, down_ref, next_ref, sides_ref, depth_rows
+    )
     pl.semaphore_wait(barrier, len(PARTNERS))
 
     def remote(source, target, sends, recvs, number, offset):
@@ -407,20 +381,26 @@
     window[pl.ds(0, PACK)] = up_ref[...]
     window[pl.ds(OWN_DOWN, PACK)] = down_ref[...]
     window[EMPTY] = jnp.zeros((8, LANES), jnp.float32)
-    loads[0].wait()
-    loads[1].wait()
-    prepare(kappa_ref, kmt_ref, xs, us, vs, all_ds, all_ks, place_ref, spot_ref, kind_ref)
-    loads[2].wait()
-    loads[3].wait()
+    loads["kappa"].wait()
+    prepare(kappa_ref, kmt_ref, xs, us, vs, all_ds, all_ks, place_ref)
+
+    def save(pair):
+        return (
+            pltpu.make_async_copy(partial_all.at[pair], partial_hbm.at[pair], out_sem.at[0, pair]),
+            pltpu.make_async_copy(edges_all.at[pair], edges_hbm.at[pair], out_sem.at[1, pair]),
+        )
 
     def one_pair(pair, carry):
         part = pl.ds(2 * pair, 2)
         interior(
             tracers_all.at[part], velocity_all.at[part], xs, us, vs, all_ds.at[pair], all_ks.at[pair], ws, gs,
-            place_ref, partial_ref.at[pair], edges_ref.at[pair], rows_ref.at[pair],
+            place_ref, partial_all.at[pair], edges_all.at[pair],
         )
+        for copy in save(pair):
+            copy.start()
         return carry
 
+    table_copy.wait()
     lax.fori_loop(0, EARLY, one_pair, 0)
     for copy in copies:
         copy.wait()
@@ -441,13 +421,16 @@
         def _():
             fold_copy(k, False).wait_recv()
 
+    def picked(index):
+        return window[jnp.minimum(jnp.maximum(index, 0), EMPTY)]
+
     def fill(number, halo_name, wrap_name):
         wrap = EMPTY
         for q in range(SLOTS):
             r = number * SLOTS + q
-            message[number, q] = window[table_ref[r, AT[halo_name]]]
+            message[number, q] = picked(table_ref[r, AT[halo_name]])
             wrap = wrap + table_ref[r, AT[wrap_name]]
-        message[number, SLOTS] = window[wrap]
+        message[number, SLOTS] = picked(wrap)
 
     later = []
     for number in [STRIDE + a for a in range(HOPS - 1, 0, -1)] + [1, 2, 3]:
@@ -473,7 +456,7 @@
             @pl.when(goes)
             def _():
                 for q in range(SLOTS):
-                    extra_message[k, q] = window[table_ref[number * SLOTS + q, AT["extra"]]]
+                    extra_message[k, q] = picked(table_ref[number * SLOTS + q, AT["extra"]])
                 if k > 0:
                     last_copy(k, number < STRIDE).start()
 
@@ -496,6 +479,9 @@
         else:
             halo_ref[2 * SLOTS] = behind
             halo_ref[2 * SLOTS + 1] = ahead
+    for pair in range(PAIRS):
+        for copy in save(pair):
+            copy.wait()
     for k in range(1, STRIDE):
         for goes, onward in ((to_high(k), True), (to_low(k), False)):
             @pl.when(goes)
@@ -516,7 +502,7 @@
             halo_ref[SLOTS + q] = halo_ref[SLOTS + q] + value
 
 
-def exchange(table, up, down, beside, tracers, velocity, kappa, kmt):
+def exchange(block_owner, neighbours, fold_partner, tracers, velocity, kappa, kmt):
     vmem = pl.BlockSpec(memory_space=pltpu.VMEM)
     anywhere = pl.BlockSpec(memory_space=pltpu.HBM)
 
@@ -529,21 +515,22 @@
     def sems(count):
         return [pltpu.SemaphoreType.DMA((count,))] * 2
 
-    cells = jax.ShapeDtypeStruct((8, TILES * LANES), jnp.int32)
     return pl.pallas_call(
         exchange_kernel,
         out_shape=[
+            jax.ShapeDtypeStruct((TABLE_ROWS, LANES), jnp.int32),
             packet_shape(WANT),
             packet_shape(2),
+            packet_shape(2 * SLOTS),
             jax.ShapeDtypeStruct((PAIRS, 8, TILES * LANES), jnp.float32),
-            packet_shape(PAIRS, 8),
-            packet_shape(PAIRS, 16),
-            cells,
-            cells,
+            packet_shape(PAIRS, EDGES),
         ],
-        in_specs=[pl.BlockSpec(memory_space=pltpu.SMEM)] + [vmem] * 3 + [anywhere] * 4,
-        out_specs=[vmem] * 7,
+        in_specs=[anywhere] * 7,
+        out_specs=[vmem] * 4 + [anywhere] * 2,
         scratch_shapes=[
+            packets(PACK),
+            packets(PACK),
+            packets(2),
             packets(WINDOW),
             packets(TARGETS, PACK),
             packets(STRIDE, SLOTS),
@@ -553,10 +540,15 @@
             *sems(EXTRAS),
             *sems(TARGETS),
             *sems(STRIDE),
+            pltpu.VMEM((SLOTS, LANES), jnp.int32),
+            pltpu.VMEM((4, SLOTS * LANES), jnp.int32),
+            pltpu.VMEM((SLOTS, LANES), jnp.int32),
             pltpu.VMEM((SLOTS, 4, CELLS), jnp.float32),
             pltpu.VMEM((SLOTS, 4, CELLS), jnp.float32),
             pltpu.VMEM((SLOTS, CELLS), jnp.float32),
             pltpu.VMEM((SLOTS, CELLS), jnp.float32),
+            packets(3, SLOTS),
+            pltpu.SMEM((TABLE_ROWS, LANES), jnp.int32),
             tiles(FRAME),
             tiles(FRAME),
             tiles(FRAME),
@@ -565,11 +557,15 @@
             tiles(TILES),
             tiles(TILES),
             pltpu.VMEM((8, TILES * LANES), jnp.int32),
-            pltpu.SemaphoreType.DMA((4,)),
+            tiles(PAIRS, TILES),
+            packets(PAIRS, EDGES),
+            pltpu.SemaphoreType.DMA((6,)),
+            pltpu.SemaphoreType.DMA((2, PAIRS)),
+            pltpu.SemaphoreType.DMA((2, PAIRS)),
         ],
         compiler_params=pltpu.CompilerParams(collective_id=0, has_side_effects=True, vmem_limit_bytes=BIG),
         name="exchange",
-    )(table, up, down, beside, tracers, velocity, kappa, kmt)
+    )(block_owner.reshape(-1, LANES), neighbours.T, fold_partner.reshape(-1, LANES), tracers, velocity, kappa, kmt)
 
 
 def flux(w, far_a, a, b, far_b):
@@ -586,7 +582,13 @@
     return jnp.where(sub % 2 == 1, pltpu.roll(z, 1, 0), pltpu.roll(z, 7, 0))
 
 
-def prepare(kappa_ref, kmt_ref, xs, us, vs, all_ds, all_ks, place_ref, spot_ref, kind_ref):
+def place_of(t, lane):
+    flat = lane + t * LANES
+    j = ((flat.astype(jnp.float32) + 0.5) * (1.0 / IB)).astype(jnp.int32)
+    return j, flat - j * IB
+
+
+def prepare(kappa_ref, kmt_ref, xs, us, vs, all_ds, all_ks, place_ref):
     sub, lane = iotas()
     zero = jnp.zeros((8, LANES), jnp.float32)
     for t in (0, 1, 45, 46):
@@ -596,14 +598,7 @@
             all_ds[p, :, lanes_at(t)] = zero
 
     def one_tile(t, rows_kappa, rows_kmt):
-        flat = lane + t * LANES
-        j = ((flat.astype(jnp.float32) + 0.5) * (1.0 / IB)).astype(jnp.int32)
-        i = flat - j * IB
-        place_ref[:, lanes_at(t)] = i
-        spot_ref[:, lanes_at(t)] = j + jnp.where(i >= IB // 2, SIDE, 0)
-        kind_ref[:, lanes_at(t)] = jnp.where(
-            (i == 0) | (i == IB - 1), 1, jnp.where((i == 1) | (i == IB - 2), 2, 0)
-        )
+        place_ref[:, lanes_at(t)] = place_of(t, lane)[1]
         for p in range(PAIRS):
             for rows, ref, at in ((rows_kmt, all_ds, t + 2), (rows_kappa, all_ks, t)):
                 ref[p, :, lanes_at(at)] = jnp.where(sub < 4, row(rows, 2 * p), row(rows, 2 * p + 1))
@@ -612,7 +607,7 @@
         one_tile(t, load_rows(kappa_ref, t), load_rows(kmt_ref, t))
 
 
-def interior(tracers_ref, velocity_ref, xs, us, vs, ds, ks, ws, gs, place_ref, partial_ref, edges_ref, rows_ref):
+def interior(tracers_ref, velocity_ref, xs, us, vs, ds, ks, ws, gs, place_ref, partial_ref, edges_ref):
     sub, lane = iotas()
     lower_half = sub % 4 < 2
     column = lane % SIDE
@@ -677,11 +672,27 @@
         edges_ref[n] = edges[n]
     for k, number in enumerate((0, 1, JB - 1, JB - 2)):
         for n, (ref, offset) in enumerate(((xs, 2), (vs, 2), (ws, 0), (gs, 0))):
-            rows_ref[4 * k + n] = line(lambda t: ref[:, lanes_at(t + offset)], number * IB, lane)
-
-
-def finish_kernel(table_ref, halo, sides_ref, beside_ref, partial_ref, edges_ref, rows_ref, spot_ref, kind_ref, out_hbm,
-                  around, out_ref, sems):
+            edges_ref[8 + 4 * k + n] = line(lambda t: ref[:, lanes_at(t + offset)], number * IB, lane)
+
+
+def finish_kernel(table_ref, halo, sides_ref, beside_ref, partial_hbm, edges_hbm, out_hbm, around, partial_all, edges_all,
+                  spot_ref, kind_ref, out_ref, load_sem, sems):
+    def load(pair):
+        return (
+            pltpu.make_async_copy(partial_hbm.at[pair], partial_all.at[pair], load_sem.at[0, pair]),
+            pltpu.make_async_copy(edges_hbm.at[pair], edges_all.at[pair], load_sem.at[1, pair]),
+        )
+
+    for pair in range(PAIRS):
+        for copy in load(pair):
+            copy.start()
+    sub, lane = iotas()
+    for t in range(TILES):
+        j, i = place_of(t, lane)
+        spot_ref[:, lanes_at(t)] = j + jnp.where(i >= IB // 2, SIDE, 0)
+        kind_ref[:, lanes_at(t)] = jnp.where(
+            (i == 0) | (i == IB - 1), 1, jnp.where((i == 1) | (i == IB - 2), 2, 0)
+        )
     for number in range(2 * SLOTS):
         around[number] = sides_ref[number]
     around[2 * SLOTS] = beside_ref[0]
@@ -695,8 +706,10 @@
         return pltpu.make_async_copy(out_ref.at[part], out_hbm.at[part], sems.at[pair])
 
     def one_pair(pair, carry):
+        for copy in load(pair):
+            copy.wait()
         finish_pair(
-            pair, table_ref, halo, around, partial_ref.at[pair], edges_ref.at[pair], rows_ref.at[pair], spot_ref, kind_ref,
+            pair, table_ref, halo, around, partial_all.at[pair], edges_all.at[pair], spot_ref, kind_ref,
             out_ref.at[pl.ds(2 * pair, 2)],
         )
         store(pair).start()
@@ -707,7 +720,7 @@
         store(pair).wait()
 
 
-def finish_pair(pair, table_ref, halo, around, partial_ref, edges_ref, rows_ref, spot_ref, kind_ref, out_ref):
+def finish_pair(pair, table_ref, halo, around, partial_ref, edges_ref, spot_ref, kind_ref, out_ref):
     sub, lane = iotas()
     upper = sub < 4
     odd = sub % 2 == 1
@@ -763,7 +776,7 @@
         return near + share_near * (swap(near) - near), far + share_far * (swap(far) - far)
 
     edges = [edges_ref[n] for n in range(8)]
-    rows = [rows_ref[n] for n in range(16)]
+    rows = [edges_ref[8 + n] for n in range(16)]
     side_sign = jnp.where(lane < SIDE, -1.0, 1.0)
     side = boundary(side_sign, side_near, side_far, side_speed, side_depth, [edges[2 * n : 2 * n + 2] for n in range(4)])
     add_south = boundary(-1.0, *south, list(zip(rows[0:4], rows[4:8])))
@@ -787,27 +800,31 @@
         out_ref[1, :, pl.ds(t * LANES, width)] = value[4:8, :width]
 
 
-def finish(table, halo, sides, beside, partial, edges, rows, spot, kind):
+def finish(table, halo, beside, sides, partial, edges):
     vmem = pl.BlockSpec(memory_space=pltpu.VMEM)
+    anywhere = pl.BlockSpec(memory_space=pltpu.HBM)
     return pl.pallas_call(
         finish_kernel,
         out_shape=jax.ShapeDtypeStruct((SLOTS, 4, CELLS), jnp.float32),
-        in_specs=[pl.BlockSpec(memory_space=pltpu.SMEM)] + [vmem] * 8,
-        out_specs=pl.BlockSpec(memory_space=pltpu.HBM),
+        in_specs=[pl.BlockSpec(memory_space=pltpu.SMEM)] + [vmem] * 3 + [anywhere] * 2,
+        out_specs=anywhere,
         scratch_shapes=[
             pltpu.VMEM((2 * SLOTS + 5, 8, LANES), jnp.float32),
+            pltpu.VMEM((PAIRS, 8, TILES * LANES), jnp.float32),
+            pltpu.VMEM((PAIRS, EDGES, 8, LANES), jnp.float32),
+            pltpu.VMEM((8, TILES * LANES), jnp.int32),
+            pltpu.VMEM((8, TILES * LANES), jnp.int32),
             pltpu.VMEM((SLOTS, 4, CELLS), jnp.float32),
+            pltpu.SemaphoreType.DMA((2, PAIRS)),
             pltpu.SemaphoreType.DMA((PAIRS,)),
         ],
         compiler_params=pltpu.CompilerParams(vmem_limit_bytes=BIG),
         name="final",
-    )(table, halo, sides, beside, partial, edges, rows, spot, kind)
+    )(table, halo, sides, beside, partial, edges)
 
 
 def per_device(tracers, velocity, kappa, kmt, block_owner, neighbours, fold_partner):
-    table, up, down, beside, sides = front(block_owner, neighbours, fold_partner, tracers, velocity, kmt)
-    halo, beside, *work = exchange(table, up, down, beside, tracers, velocity, kappa, kmt)
-    return finish(table, halo, sides, beside, *work)
+    return finish(*exchange(block_owner, neighbours, fold_partner, tracers, velocity, kappa, kmt))
 
 
 def solution(mesh):

time: 40.3 us -> 34.7 us (0.86)
  Pallas kernels: 40 us -> 34.5 us
    pallas_call x2 -> x1, Pallas kernels: 35.6 us -> 29 us  [exchange(): pl.pallas_call(exchange_kernel, out_shape=[jax.ShapeDtypeStruct((TABLE_RO...]
    pallas_call x1, Pallas kernels: 4.46 us -> 5.52 us  [finish(): pl.pallas_call(finish_kernel, out_shape=jax.ShapeDtypeStruct((SLOTS, 4, C...]
where the time goes in v4:
time: 34.7 us; the launch traced here: 34.5 us
  Pallas kernels  34.5 us (99%)
    pallas_call x1, Pallas kernels, exchange(): pl.pallas_call(exchange_kernel, out_shape=[jax.ShapeDtypeStruct((TABLE_RO...  29 us
    pallas_call x1, Pallas kernels, finish(): pl.pallas_call(finish_kernel, out_shape=jax.ShapeDtypeStruct((SLOTS, 4, C...  5.52 us

profile of v4, /device:TPU:1, one launch (start us, length us, event | category | flops | bytes accessed | tf_op | source)
XLA Modules:
  0.0 34.5 jit_solution(10542053534647355943)
XLA Ops:
  0.0 29.0 %exchange.1 = (s32[112,128]{1,0:T(8,128)}, f32[22,8,128]{2,1,0:T(8,128)}, f32[2,8,128]{2,1,0:T(8,128)}, f32[20,8,128]{2,1,0:T(8,128)}, f32[5,8,5504]{2,1,0:T(8,128)}, /*index=5*/f32[5,24,8,128]{3,2,1,0:T(8,128)}) custom-call(s32[10,128]{1,0:T(8,128)} %bitcast.4, s32[4,1280]{1,0:T(4,128)} %bitcast.3, s32[10,128]{1,0:T(8,128)} %bitcast.5, ...), custom_call_target="tpu_custom_call" | custom-call | tf_op jit(solution)/shard_map/exchange/pallas_call | solution.py:518
  29.0 5.5 %final.1 = f32[10,4,5400]{2,1,0:T(4,128)} custom-call(s32[112,128]{1,0:T(8,128)} %get-tuple-element.11.table_ref, f32[22,8,128]{2,1,0:T(8,128)} %get-tuple-element.12.halo, f32[20,8,128]{2,1,0:T(8,128)} %get-tuple-element.13.sides_ref, f32[2,8,128]{2,1,0:T(8,128)} %get-tuple-element.14.beside_ref, f32[5,8,5504]{2,1,0:T(8,128)} %get-tuple-element.15.partial_hbm, ...), custom_call_target="tpu_custom_call" | custom-call | tf_op jit(solution)/shard_map/final/pallas_call | solution.py:806

commit v5 on v4

--- a/solution.py
+++ b/solution.py
@@ -19,15 +19,17 @@
 FRAME = 47
 SIDE = 64
 PACK = SLOTS + 1
+EXTRAS = 3
 OWN_DOWN = HOPS * PACK
-EXTRA = OWN_DOWN + STRIDE * PACK
-EXTRAS = 3
-EMPTY = EXTRA + EXTRAS * PACK
+LOW_EXTRA = OWN_DOWN + PACK
+OWN_UP = STRIDE * PACK
+HIGH_EXTRA = OWN_UP + PACK
+EMPTY = LOW_EXTRA + EXTRAS * PACK
 WINDOW = EMPTY + 1
 WANT = 2 * SLOTS + 2
 TARGETS = STRIDE + HOPS
 TABLE_ROWS = 112
-EARLY = 2
+EARLY = (0, 1, 3)
 EDGES = 24
 BIG = 63 << 20
 FOLD_REACH = 14
@@ -59,9 +61,8 @@
     return jnp.broadcast_to(value[number : number + 1], (8, LANES))
 
 
-def table_of(owner_ref, near_ref, fold_ref):
+def table_of(owner_ref, near_ref, fold_ref, rows):
     me = position()
-    rows = TABLE_ROWS
     strips = owner_ref.shape[0]
     number = lax.broadcasted_iota(jnp.int32, (rows, 1), 0).astype(jnp.float32)
     which = jnp.floor((number + 0.5) * (1.0 / SLOTS))
@@ -107,19 +108,26 @@
 
     vote = jnp.where(links[3] >= 0, jnp.where(links[3] > code, 1.0, -1.0), 0.0)
     vote = vote - jnp.where(links[2] >= 0, jnp.where(links[2] > code, 1.0, -1.0), 0.0)
-    up = jnp.sum(vote, axis=0, keepdims=True) >= 0
+    lean = count = jnp.zeros((1, LANES), jnp.float32)
+    for t, owner in enumerate(owners):
+        top = fold_ref[t : t + 1, :] >= 0
+        lean = lean + jnp.where(top, owner - 0.5 * DEVICES * SLOTS, 0.0)
+        count = count + jnp.where(top, 1.0, 0.0)
+    lean, count = (jnp.sum(value, axis=1, keepdims=True) for value in (lean, count))
+    vote = jnp.sum(vote, axis=0, keepdims=True)
+    up = jnp.where(count > 0, lean, vote) >= 0
     empty = float(EMPTY)
     _, place, _, far, _, from_behind, _ = where_is(jnp.where(up, links[2], links[3]))
     behind = jnp.where(from_behind, far * PACK + place, empty)
     _, place, _, _, rest, _, from_ahead = where_is(jnp.where(up, links[3], links[2]))
-    ahead = jnp.where(from_ahead, OWN_DOWN + rest * PACK + place, empty)
+    ahead = jnp.where(from_ahead, rest * PACK + place, empty)
     _, place, apart, far, rest, from_behind, from_ahead = where_is(links[4])
-    against = jnp.where(rest > 0, EXTRA + (rest - 1.0) * PACK, 0.0) + place
+    against = jnp.where(rest > 0, HIGH_EXTRA + (rest - 1.0) * PACK, float(OWN_UP)) + place
     ahead = jnp.where(up & from_ahead, against, ahead)
-    against = jnp.where(far > 0, EXTRA + (far - 1.0) * PACK, float(OWN_DOWN)) + place
+    against = jnp.where(far > 0, LOW_EXTRA + (far - 1.0) * PACK, float(OWN_DOWN)) + place
     behind = jnp.where(~up & from_behind, against, behind)
     extra = jnp.where(up & from_behind & (apart < 0), far * PACK + place, empty)
-    extra = jnp.where(~up & from_ahead & (apart > 0), OWN_DOWN + rest * PACK + place, extra)
+    extra = jnp.where(~up & from_ahead & (apart > 0), rest * PACK + place, extra)
     sides = []
     columns = {"earlier": 0.0, "later": 0.0, "send_later": 0.0, "send_earlier": 0.0, "next": 0.0, "previous": 0.0}
     for side in range(2):
@@ -132,7 +140,7 @@
         later = linked & (apart > 0) & ~after
         mine = slot * 2.0 + (side + 1.0)
         columns["earlier"] += jnp.where(earlier & from_behind, far * PACK + SLOTS - EMPTY, 0.0)
-        columns["later"] += jnp.where(later & from_ahead, OWN_DOWN + rest * PACK + SLOTS - EMPTY, 0.0)
+        columns["later"] += jnp.where(later & from_ahead, rest * PACK + SLOTS - EMPTY, 0.0)
         columns["send_later"] += jnp.where(later, mine, 0.0)
         columns["send_earlier"] += jnp.where(earlier, mine, 0.0)
         columns["next"] += jnp.where(after, mine, 0.0)
@@ -286,9 +294,9 @@
 HIGH, LOW = DEVICES - FOLD_REACH, FOLD_REACH
 
 
-def exchange_kernel(owner_hbm, near_hbm, fold_hbm, tracers_hbm, velocity_hbm, kappa_hbm, kmt_hbm, table_out, halo_ref,
-                    beside_ref, sides_ref, partial_hbm, edges_hbm, up_ref, down_ref, next_ref, window, message,
-                    extra_message, arrived, extra_arrived, send_sem, recv_sem, extra_send, extra_recv, later_send, later_recv,
+def exchange_kernel(owner_hbm, near_hbm, fold_hbm, tracers_hbm, velocity_hbm, kappa_hbm, kmt_hbm, out_hbm, table_out, halo_ref,
+                    beside_ref, sides_ref, around, spot_ref, kind_ref, out_ref, up_ref, down_ref, next_ref, window, window_ahead, message,
+                    extra_message, arrived, extra_arrived, send_sem, recv_sem, extra_send, extra_recv, low_send, low_recv, later_send, later_recv,
                     last_send, last_recv, owner_ref, near_ref, fold_ref, tracers_all, velocity_all, kappa_ref, kmt_ref,
                     depth_rows, table_ref, xs, us, vs, all_ds, all_ks, ws, gs, place_ref, partial_all, edges_all, load_sem,
                     pair_sem, out_sem):
@@ -323,10 +331,7 @@
     loads["kappa"].start()
     for name in ("owner", "near", "fold"):
         loads[name].wait()
-    table, up, chosen = table_of(owner_ref, near_ref, fold_ref)
-    table_out[...] = table
-    table_copy = pltpu.make_async_copy(table_out, table_ref, load_sem.at[len(sources)])
-    table_copy.start()
+    _, up, chosen = table_of(owner_ref, near_ref, fold_ref, 16)
     pack_edges(
         fetch, loads, up, chosen, tracers_all, velocity_all, kmt_ref, up_ref, down_ref, next_ref, sides_ref, depth_rows
     )
@@ -345,50 +350,63 @@
     plan = []
     for a in range(HOPS - 1, 0, -1):
         plan.append((up_ref, window.at[pl.ds(a * PACK, PACK)], STRIDE * a))
-        if a < STRIDE:
-            plan.append((down_ref, window.at[pl.ds(OWN_DOWN + a * PACK, PACK)], -a))
     plan.append((next_ref.at[0], beside_ref.at[0], 1))
     plan.append((next_ref.at[1], beside_ref.at[1], -1))
+    first_down = len(plan)
+    for a in (2, 1, 3):
+        plan.append((down_ref, window_ahead.at[pl.ds(a * PACK, PACK)], -a))
     copies = [
         remote(source, target, send_sem, recv_sem, number, offset)
         for number, (source, target, offset) in enumerate(plan)
     ]
-    for copy in copies:
-        copy.start()
-
-    def fold_copy(k, downwards):
-        target = window.at[pl.ds(EXTRA + (k - 1) * PACK, PACK)]
-        if downwards:
-            return remote(up_ref, target, extra_send, extra_recv, k - 1, -k)
-        return remote(down_ref, target, extra_send, extra_recv, k - 1, STRIDE * k)
-
+    for number in list(range(first_down, len(plan))) + list(range(first_down)):
+        copies[number].start()
+
+    def high_copy(k):
+        target = window_ahead.at[pl.ds(HIGH_EXTRA + (k - 1) * PACK, PACK)]
+        return remote(up_ref, target, extra_send, extra_recv, k - 1, -k)
+
+    def low_copy(k):
+        target = window.at[pl.ds(LOW_EXTRA + (k - 1) * PACK, PACK)]
+        return remote(down_ref, target, low_send, low_recv, k - 1, STRIDE * k)
+
+    def from_high(k):
+        return (me + k >= HIGH) & (me + k < DEVICES)
+
+    def from_low(k):
+        return (me - STRIDE * k >= 0) & (me - STRIDE * k < LOW)
+
+    nothing = jnp.zeros((PACK, 8, LANES), jnp.float32)
     for k in range(1, EXTRAS + 1):
         @pl.when(me >= HIGH)
         def _():
-            fold_copy(k, True).start()
+            high_copy(k).start()
 
         @pl.when(me < LOW)
         def _():
-            fold_copy(k, False).start()
-
-        from_high = (me + k >= HIGH) & (me + k < DEVICES)
-        from_low = (me - STRIDE * k >= 0) & (me - STRIDE * k < LOW)
-
-        @pl.when(jnp.logical_not(from_high | from_low))
+            low_copy(k).start()
+
+        @pl.when(jnp.logical_not(from_high(k)))
         def _():
-            window[pl.ds(EXTRA + (k - 1) * PACK, PACK)] = jnp.zeros((PACK, 8, LANES), jnp.float32)
+            window_ahead[pl.ds(HIGH_EXTRA + (k - 1) * PACK, PACK)] = nothing
+
+        @pl.when(jnp.logical_not(from_low(k)))
+        def _():
+            window[pl.ds(LOW_EXTRA + (k - 1) * PACK, PACK)] = nothing
 
     window[pl.ds(0, PACK)] = up_ref[...]
     window[pl.ds(OWN_DOWN, PACK)] = down_ref[...]
     window[EMPTY] = jnp.zeros((8, LANES), jnp.float32)
+    window_ahead[pl.ds(0, PACK)] = down_ref[...]
+    window_ahead[pl.ds(OWN_UP, PACK)] = up_ref[...]
+    for number in range(HIGH_EXTRA + EXTRAS * PACK, WINDOW):
+        window_ahead[number] = jnp.zeros((8, LANES), jnp.float32)
+    table, _, _ = table_of(owner_ref, near_ref, fold_ref, TABLE_ROWS)
+    table_out[...] = table
+    table_copy = pltpu.make_async_copy(table_out, table_ref, load_sem.at[len(sources)])
+    table_copy.start()
     loads["kappa"].wait()
-    prepare(kappa_ref, kmt_ref, xs, us, vs, all_ds, all_ks, place_ref)
-
-    def save(pair):
-        return (
-            pltpu.make_async_copy(partial_all.at[pair], partial_hbm.at[pair], out_sem.at[0, pair]),
-            pltpu.make_async_copy(edges_all.at[pair], edges_hbm.at[pair], out_sem.at[1, pair]),
-        )
+    prepare(kappa_ref, kmt_ref, xs, us, vs, all_ds, all_ks, place_ref, spot_ref, kind_ref)
 
     def one_pair(pair, carry):
         part = pl.ds(2 * pair, 2)
@@ -396,35 +414,14 @@
             tracers_all.at[part], velocity_all.at[part], xs, us, vs, all_ds.at[pair], all_ks.at[pair], ws, gs,
             place_ref, partial_all.at[pair], edges_all.at[pair],
         )
-        for copy in save(pair):
-            copy.start()
         return carry
 
-    table_copy.wait()
-    lax.fori_loop(0, EARLY, one_pair, 0)
-    for copy in copies:
-        copy.wait()
-    for k in range(1, EXTRAS + 1):
-        @pl.when(me >= HIGH)
-        def _():
-            fold_copy(k, True).wait_send()
-
-        @pl.when(me < LOW)
-        def _():
-            fold_copy(k, False).wait_send()
-
-        @pl.when((me + k >= HIGH) & (me + k < DEVICES))
-        def _():
-            fold_copy(k, True).wait_recv()
-
-        @pl.when((me - STRIDE * k >= 0) & (me - STRIDE * k < LOW))
-        def _():
-            fold_copy(k, False).wait_recv()
-
-    def picked(index):
-        return window[jnp.minimum(jnp.maximum(index, 0), EMPTY)]
-
     def fill(number, halo_name, wrap_name):
+        ref = window if number < STRIDE else window_ahead
+
+        def picked(index):
+            return ref[jnp.minimum(jnp.maximum(index, 0), EMPTY)]
+
         wrap = EMPTY
         for q in range(SLOTS):
             r = number * SLOTS + q
@@ -433,38 +430,68 @@
         message[number, SLOTS] = picked(wrap)
 
     later = []
-    for number in [STRIDE + a for a in range(HOPS - 1, 0, -1)] + [1, 2, 3]:
-        onward = number < STRIDE
-        fill(number, *(("behind", "earlier") if onward else ("ahead", "later")))
-        offset = number if onward else -STRIDE * (number - STRIDE)
-        copy = remote(message.at[number], arrived.at[number], later_send, later_recv, number, offset)
-        copy.start()
-        later.append(copy)
+
+    def forward(numbers):
+        for number in numbers:
+            onward = number < STRIDE
+            fill(number, *(("behind", "earlier") if onward else ("ahead", "later")))
+            offset = number if onward else -STRIDE * (number - STRIDE)
+            copy = remote(message.at[number], arrived.at[number], later_send, later_recv, number, offset)
+            copy.start()
+            later.append(copy)
+
+    lax.fori_loop(EARLY[0], EARLY[1], one_pair, 0)
+    table_copy.wait()
+    for copy in copies[first_down:]:
+        copy.wait_recv()
+    for k in range(1, EXTRAS + 1):
+        @pl.when(from_high(k))
+        def _():
+            high_copy(k).wait_recv()
+
+    forward([STRIDE + a for a in range(HOPS - 1, 0, -1)])
+    lax.fori_loop(EARLY[1], EARLY[2], one_pair, 0)
+    for copy in copies[:first_down]:
+        copy.wait_recv()
+    for k in range(1, EXTRAS + 1):
+        @pl.when(from_low(k))
+        def _():
+            low_copy(k).wait_recv()
+
+    forward([2, 1, 3])
 
     def last_copy(k, onward):
         offset = k if onward else -STRIDE * k
         return remote(extra_message.at[k], extra_arrived.at[k], last_send, last_recv, k, offset)
 
-    def to_high(k):
-        return (me + k >= HIGH) & (me + k < DEVICES)
-
-    def to_low(k):
-        return (me - STRIDE * k >= 0) & (me - STRIDE * k < LOW)
+    def extra_picked(ref, row_number):
+        return ref[jnp.minimum(jnp.maximum(table_ref[row_number, AT["extra"]], 0), EMPTY)]
 
     for k in range(STRIDE):
-        for goes, number in ((to_high(k), k), (to_low(k), STRIDE + k)):
+        for goes, number, ref in ((from_high(k), k, window), (from_low(k), STRIDE + k, window_ahead)):
             @pl.when(goes)
             def _():
                 for q in range(SLOTS):
-                    extra_message[k, q] = picked(table_ref[number * SLOTS + q, AT["extra"]])
+                    extra_message[k, q] = extra_picked(ref, number * SLOTS + q)
                 if k > 0:
                     last_copy(k, number < STRIDE).start()
 
     fill(0, "behind", "earlier")
     fill(STRIDE, "ahead", "later")
-    lax.fori_loop(EARLY, PAIRS, one_pair, 0)
+    lax.fori_loop(EARLY[2], PAIRS, one_pair, 0)
     for copy in later:
         copy.wait()
+    for copy in copies:
+        copy.wait_send()
+    for k in range(1, EXTRAS + 1):
+        @pl.when(me >= HIGH)
+        def _():
+            high_copy(k).wait_send()
+
+        @pl.when(me < LOW)
+        def _():
+            low_copy(k).wait_send()
+
     flag = own_row(table_ref, 0, "up") > 0
     for q in range(PACK):
         behind = message[0, q]
@@ -479,11 +506,8 @@
         else:
             halo_ref[2 * SLOTS] = behind
             halo_ref[2 * SLOTS + 1] = ahead
-    for pair in range(PAIRS):
-        for copy in save(pair):
-            copy.wait()
     for k in range(1, STRIDE):
-        for goes, onward in ((to_high(k), True), (to_low(k), False)):
+        for goes, onward in ((from_high(k), True), (from_low(k), False)):
             @pl.when(goes)
             def _():
                 last_copy(k, onward).wait_send()
@@ -501,9 +525,11 @@
                 value = value + extra_arrived[k, q]
             halo_ref[SLOTS + q] = halo_ref[SLOTS + q] + value
 
+    finish_all(table_ref, halo_ref, sides_ref, beside_ref, partial_all, edges_all, out_hbm, around, spot_ref, kind_ref, out_ref,
+               out_sem)
+
 
 def exchange(block_owner, neighbours, fold_partner, tracers, velocity, kappa, kmt):
-    vmem = pl.BlockSpec(memory_space=pltpu.VMEM)
     anywhere = pl.BlockSpec(memory_space=pltpu.HBM)
 
     def packets(*lead):
@@ -517,26 +543,29 @@
 
     return pl.pallas_call(
         exchange_kernel,
-        out_shape=[
-            jax.ShapeDtypeStruct((TABLE_ROWS, LANES), jnp.int32),
-            packet_shape(WANT),
-            packet_shape(2),
-            packet_shape(2 * SLOTS),
-            jax.ShapeDtypeStruct((PAIRS, 8, TILES * LANES), jnp.float32),
-            packet_shape(PAIRS, EDGES),
-        ],
+        out_shape=jax.ShapeDtypeStruct((SLOTS, 4, CELLS), jnp.float32),
         in_specs=[anywhere] * 7,
-        out_specs=[vmem] * 4 + [anywhere] * 2,
+        out_specs=anywhere,
         scratch_shapes=[
+            pltpu.VMEM((TABLE_ROWS, LANES), jnp.int32),
+            packets(WANT),
+            packets(2),
+            packets(2 * SLOTS),
+            packets(2 * SLOTS + 5),
+            pltpu.VMEM((8, TILES * LANES), jnp.int32),
+            pltpu.VMEM((8, TILES * LANES), jnp.int32),
+            pltpu.VMEM((SLOTS, 4, CELLS), jnp.float32),
             packets(PACK),
             packets(PACK),
             packets(2),
+            packets(WINDOW),
             packets(WINDOW),
             packets(TARGETS, PACK),
             packets(STRIDE, SLOTS),
             packets(TARGETS, PACK),
             packets(STRIDE, SLOTS),
             *sems(HOPS - 1 + EXTRAS + 2),
+            *sems(EXTRAS),
             *sems(EXTRAS),
             *sems(TARGETS),
             *sems(STRIDE),
@@ -561,7 +590,7 @@
             packets(PAIRS, EDGES),
             pltpu.SemaphoreType.DMA((6,)),
             pltpu.SemaphoreType.DMA((2, PAIRS)),
-            pltpu.SemaphoreType.DMA((2, PAIRS)),
+            pltpu.SemaphoreType.DMA((PAIRS,)),
         ],
         compiler_params=pltpu.CompilerParams(collective_id=0, has_side_effects=True, vmem_limit_bytes=BIG),
         name="exchange",
@@ -588,7 +617,7 @@
     return j, flat - j * IB
 
 
-def prepare(kappa_ref, kmt_ref, xs, us, vs, all_ds, all_ks, place_ref):
+def prepare(kappa_ref, kmt_ref, xs, us, vs, all_ds, all_ks, place_ref, spot_ref, kind_ref):
     sub, lane = iotas()
     zero = jnp.zeros((8, LANES), jnp.float32)
     for t in (0, 1, 45, 46):
@@ -598,7 +627,12 @@
             all_ds[p, :, lanes_at(t)] = zero
 
     def one_tile(t, rows_kappa, rows_kmt):
-        place_ref[:, lanes_at(t)] = place_of(t, lane)[1]
+        j, i = place_of(t, lane)
+        place_ref[:, lanes_at(t)] = i
+        spot_ref[:, lanes_at(t)] = j + jnp.where(i >= IB // 2, SIDE, 0)
+        kind_ref[:, lanes_at(t)] = jnp.where(
+            (i == 0) | (i == IB - 1), 1, jnp.where((i == 1) | (i == IB - 2), 2, 0)
+        )
         for p in range(PAIRS):
             for rows, ref, at in ((rows_kmt, all_ds, t + 2), (rows_kappa, all_ks, t)):
                 ref[p, :, lanes_at(at)] = jnp.where(sub < 4, row(rows, 2 * p), row(rows, 2 * p + 1))
@@ -675,24 +709,8 @@
             edges_ref[8 + 4 * k + n] = line(lambda t: ref[:, lanes_at(t + offset)], number * IB, lane)
 
 
-def finish_kernel(table_ref, halo, sides_ref, beside_ref, partial_hbm, edges_hbm, out_hbm, around, partial_all, edges_all,
-                  spot_ref, kind_ref, out_ref, load_sem, sems):
-    def load(pair):
-        return (
-            pltpu.make_async_copy(partial_hbm.at[pair], partial_all.at[pair], load_sem.at[0, pair]),
-            pltpu.make_async_copy(edges_hbm.at[pair], edges_all.at[pair], load_sem.at[1, pair]),
-        )
-
-    for pair in range(PAIRS):
-        for copy in load(pair):
-            copy.start()
-    sub, lane = iotas()
-    for t in range(TILES):
-        j, i = place_of(t, lane)
-        spot_ref[:, lanes_at(t)] = j + jnp.where(i >= IB // 2, SIDE, 0)
-        kind_ref[:, lanes_at(t)] = jnp.where(
-            (i == 0) | (i == IB - 1), 1, jnp.where((i == 1) | (i == IB - 2), 2, 0)
-        )
+def finish_all(table_ref, halo, sides_ref, beside_ref, partial_all, edges_all, out_hbm, around, spot_ref, kind_ref, out_ref,
+               sems):
     for number in range(2 * SLOTS):
         around[number] = sides_ref[number]
     around[2 * SLOTS] = beside_ref[0]
@@ -706,8 +724,6 @@
         return pltpu.make_async_copy(out_ref.at[part], out_hbm.at[part], sems.at[pair])
 
     def one_pair(pair, carry):
-        for copy in load(pair):
-            copy.wait()
         finish_pair(
             pair, table_ref, halo, around, partial_all.at[pair], edges_all.at[pair], spot_ref, kind_ref,
             out_ref.at[pl.ds(2 * pair, 2)],
@@ -757,7 +773,7 @@
     ]
     bodies, speeds, depths = [], [], []
     for q in slots:
-        west, east = (around[own_row(table_ref, q, name)] for name in ("west", "east"))
+        west, east = (around[jnp.minimum(jnp.maximum(own_row(table_ref, q, name), 0), 2 * SLOTS + 4)] for name in ("west", "east"))
         bodies.append(jnp.where(lane < SIDE, west, pltpu.roll(east, SIDE, 1)))
         aux = jnp.where(lane < SIDE, pltpu.roll(west, SIDE, 1), east)
         speeds.append(jnp.where(odd, row(aux, 1), row(aux, 0)))
@@ -800,31 +816,8 @@
         out_ref[1, :, pl.ds(t * LANES, width)] = value[4:8, :width]
 
 
-def finish(table, halo, beside, sides, partial, edges):
-    vmem = pl.BlockSpec(memory_space=pltpu.VMEM)
-    anywhere = pl.BlockSpec(memory_space=pltpu.HBM)
-    return pl.pallas_call(
-        finish_kernel,
-        out_shape=jax.ShapeDtypeStruct((SLOTS, 4, CELLS), jnp.float32),
-        in_specs=[pl.BlockSpec(memory_space=pltpu.SMEM)] + [vmem] * 3 + [anywhere] * 2,
-        out_specs=anywhere,
-        scratch_shapes=[
-            pltpu.VMEM((2 * SLOTS + 5, 8, LANES), jnp.float32),
-            pltpu.VMEM((PAIRS, 8, TILES * LANES), jnp.float32),
-            pltpu.VMEM((PAIRS, EDGES, 8, LANES), jnp.float32),
-            pltpu.VMEM((8, TILES * LANES), jnp.int32),
-            pltpu.VMEM((8, TILES * LANES), jnp.int32),
-            pltpu.VMEM((SLOTS, 4, CELLS), jnp.float32),
-            pltpu.SemaphoreType.DMA((2, PAIRS)),
-            pltpu.SemaphoreType.DMA((PAIRS,)),
-        ],
-        compiler_params=pltpu.CompilerParams(vmem_limit_bytes=BIG),
-        name="final",
-    )(table, halo, sides, beside, partial, edges)
-
-
 def per_device(tracers, velocity, kappa, kmt, block_owner, neighbours, fold_partner):
-    return finish(*exchange(block_owner, neighbours, fold_partner, tracers, velocity, kappa, kmt))
+    return exchange(block_owner, neighbours, fold_partner, tracers, velocity, kappa, kmt)
 
 
 def solution(mesh):

time: 34.7 us -> 32.1 us (0.925)
  Pallas kernels: 34.5 us -> 29.8 us
  local copies, waits for them, and re-layouts: 0 us -> 2.14 us
    pallas_call x2 -> x1, Pallas kernels: 34.5 us -> 29.8 us  [exchange(): pl.pallas_call(exchange_kernel, out_shape=jax.ShapeDtypeStruct((SLOTS, 4,...]
    unnamed x0 -> x1, local copies, waits for them, and re-layouts: none -> 2.14 us
where the time goes in v5:
time: 32.1 us; the launch traced here: 32 us
  Pallas kernels  29.8 us (93%)
  local copies, waits for them, and re-layouts  2.14 us (7%)
    pallas_call x1, Pallas kernels, exchange(): pl.pallas_call(exchange_kernel, out_shape=jax.ShapeDtypeStruct((SLOTS, 4,...  29.8 us
    unnamed x1, local copies, waits for them, and re-layouts  2.14 us

profile of v5, /device:TPU:1, one launch (start us, length us, event | category | flops | bytes accessed | tf_op | source)
XLA Modules:
  0.0 32.0 jit_solution(5718615637700386912)
XLA Ops:
  0.0 29.8 %exchange.1 = f32[10,4,5400]{2,1,0:T(4,128)} custom-call(s32[10,128]{1,0:T(8,128)} %bitcast.4, s32[4,1280]{1,0:T(4,128)} %bitcast.3, s32[10,128]{1,0:T(8,128)} %bitcast.5, f32[10,4,5400]{2,1,0:T(4,128)} %tracers_hbm.1, f32[10,4,5400]{2,1,0:T(4,128)} %velocity_hbm.1, f32[10,5400]{1,0:T(8,128)} %kappa_hbm.1, f32[10,5400]{1,0:T(8,128)} %kmt_hbm.1), custom_call_target="tpu_custom_call" | custom-call | tf_op jit(solution)/shard_map/exchange/pallas_call | solution.py:544
  29.9 2.1 %copy.9 = f32[10,4,5400]{2,1,0:T(4,128)} copy(f32[10,4,5400]{2,1,0:T(4,128)} %exchange.1) | data formatting | bytes 1728000

commit v6 on v5

--- a/solution.py
+++ b/solution.py
@@ -29,7 +29,7 @@
 WANT = 2 * SLOTS + 2
 TARGETS = STRIDE + HOPS
 TABLE_ROWS = 112
-EARLY = (0, 1, 3)
+EARLY = (0, 2, 4)
 EDGES = 24
 BIG = 63 << 20
 FOLD_REACH = 14
@@ -197,7 +197,7 @@
 ROW_STARTS = (0, IB, (JB - 1) * IB, (JB - 2) * IB)
 
 
-def pack_edges(fetch, loads, up, chosen, tracers_all, velocity_all, kmt_ref, up_ref, down_ref, next_ref, sides_ref, depth_rows):
+def pack_edges(fetch, loads, up, chosen, tracers_all, velocity_all, kmt_ref, up_ref, down_ref, next_ref, sides_ref, depth_rows, edges_all):
     sub, lane = iotas()
     flag = jnp.broadcast_to(up, (8, LANES))
     column = lane % SIDE
@@ -258,6 +258,9 @@
             near = jnp.where(near_tile == t, take(x, near_at), near)
             far = jnp.where(far_tile == t, take(x, far_at), far)
             drift = jnp.where(near_tile == t, take(v, near_at), drift)
+        edges_all[pair, 0] = near
+        edges_all[pair, 1] = far
+        edges_all[pair, 2] = jnp.where(sub % 4 < 2, drift, pltpu.roll(drift, 2, 0))
         for half in range(2):
             q = 2 * pair + half
             if half == 0:
@@ -298,7 +301,7 @@
                     beside_ref, sides_ref, around, spot_ref, kind_ref, out_ref, up_ref, down_ref, next_ref, window, window_ahead, message,
                     extra_message, arrived, extra_arrived, send_sem, recv_sem, extra_send, extra_recv, low_send, low_recv, later_send, later_recv,
                     last_send, last_recv, owner_ref, near_ref, fold_ref, tracers_all, velocity_all, kappa_ref, kmt_ref,
-                    depth_rows, table_ref, xs, us, vs, all_ds, all_ks, ws, gs, place_ref, partial_all, edges_all, load_sem,
+                    depth_rows, table_ref, xs, us, vs, all_ds, all_ks, gs, fe, fn, place_ref, partial_all, edges_all, load_sem,
                     pair_sem, out_sem):
     me = position()
     barrier = pltpu.get_barrier_semaphore()
@@ -333,7 +336,8 @@
         loads[name].wait()
     _, up, chosen = table_of(owner_ref, near_ref, fold_ref, 16)
     pack_edges(
-        fetch, loads, up, chosen, tracers_all, velocity_all, kmt_ref, up_ref, down_ref, next_ref, sides_ref, depth_rows
+        fetch, loads, up, chosen, tracers_all, velocity_all, kmt_ref, up_ref, down_ref, next_ref, sides_ref, depth_rows,
+        edges_all,
     )
     pl.semaphore_wait(barrier, len(PARTNERS))
 
@@ -406,12 +410,12 @@
     table_copy = pltpu.make_async_copy(table_out, table_ref, load_sem.at[len(sources)])
     table_copy.start()
     loads["kappa"].wait()
-    prepare(kappa_ref, kmt_ref, xs, us, vs, all_ds, all_ks, place_ref, spot_ref, kind_ref)
+    prepare(kappa_ref, kmt_ref, xs, us, vs, all_ds, all_ks, fe, fn, place_ref, spot_ref, kind_ref)
 
     def one_pair(pair, carry):
         part = pl.ds(2 * pair, 2)
         interior(
-            tracers_all.at[part], velocity_all.at[part], xs, us, vs, all_ds.at[pair], all_ks.at[pair], ws, gs,
+            tracers_all.at[part], velocity_all.at[part], xs, us, vs, all_ds.at[pair], all_ks.at[pair], gs, fe, fn,
             place_ref, partial_all.at[pair], edges_all.at[pair],
         )
         return carry
@@ -584,7 +588,8 @@
             tiles(PAIRS, FRAME),
             tiles(PAIRS, TILES),
             tiles(TILES),
-            tiles(TILES),
+            tiles(TILES + 1),
+            tiles(TILES + 1),
             pltpu.VMEM((8, TILES * LANES), jnp.int32),
             tiles(PAIRS, TILES),
             packets(PAIRS, EDGES),
@@ -617,9 +622,11 @@
     return j, flat - j * IB
 
 
-def prepare(kappa_ref, kmt_ref, xs, us, vs, all_ds, all_ks, place_ref, spot_ref, kind_ref):
+def prepare(kappa_ref, kmt_ref, xs, us, vs, all_ds, all_ks, fe, fn, place_ref, spot_ref, kind_ref):
     sub, lane = iotas()
     zero = jnp.zeros((8, LANES), jnp.float32)
+    fe[:, lanes_at(0)] = zero
+    fn[:, lanes_at(0)] = zero
     for t in (0, 1, 45, 46):
         for ref in (xs, us, vs):
             ref[:, lanes_at(t)] = zero
@@ -634,14 +641,15 @@
             (i == 0) | (i == IB - 1), 1, jnp.where((i == 1) | (i == IB - 2), 2, 0)
         )
         for p in range(PAIRS):
-            for rows, ref, at in ((rows_kmt, all_ds, t + 2), (rows_kappa, all_ks, t)):
-                ref[p, :, lanes_at(at)] = jnp.where(sub < 4, row(rows, 2 * p), row(rows, 2 * p + 1))
+            depth = jnp.where(sub < 4, row(rows_kmt, 2 * p), row(rows_kmt, 2 * p + 1))
+            all_ds[p, :, lanes_at(t + 2)] = wetness(depth)
+            all_ks[p, :, lanes_at(t)] = jnp.where(sub < 4, row(rows_kappa, 2 * p), row(rows_kappa, 2 * p + 1))
 
     for t in range(TILES):
         one_tile(t, load_rows(kappa_ref, t), load_rows(kmt_ref, t))
 
 
-def interior(tracers_ref, velocity_ref, xs, us, vs, ds, ks, ws, gs, place_ref, partial_ref, edges_ref):
+def interior(tracers_ref, velocity_ref, xs, us, vs, ds, ks, gs, fe, fn, place_ref, partial_ref, edges_ref):
     sub, lane = iotas()
     lower_half = sub % 4 < 2
     column = lane % SIDE
@@ -670,42 +678,54 @@
         r = s % LANES
         return jnp.where(lane < LANES - r, turn(name, ref, tile, r), turn(name, ref, tile + 1, r))
 
-    edges = [jnp.zeros((8, LANES), jnp.float32)] * 8
+    zero = jnp.zeros((8, LANES), jnp.float32)
+    edges = [zero] * 5
     for t in range(TILES):
         for key in [k for k in turned if k[1] < t]:
             del turned[key]
         i = place_ref[:, lanes_at(t)]
-        x, u, v = (tile_of(name, ref, t + 2) for name, ref in (("x", xs), ("u", us), ("v", vs)))
-        wet = wetness(tile_of("d", ds, t + 2))
+        x, u, v, wet = (
+            tile_of(name, ref, t + 2) for name, ref in (("x", xs), ("u", us), ("v", vs), ("d", ds))
+        )
+        last = i == IB - 1
         west = jnp.where(i == 0, 0.0, shift("x", xs, t, -1))
-        west_far = jnp.where(i <= 1, 0.0, shift("x", xs, t, -2))
-        east = jnp.where(i == IB - 1, 0.0, shift("x", xs, t, 1))
+        east = jnp.where(last, 0.0, shift("x", xs, t, 1))
         east_far = jnp.where(i >= IB - 2, 0.0, shift("x", xs, t, 2))
-        wet_west = jnp.where(i == 0, 0.0, wetness(shift("d", ds, t, -1)))
-        wet_east = jnp.where(i == IB - 1, 0.0, wetness(shift("d", ds, t, 1)))
-        wet_south = wetness(shift("d", ds, t, -IB))
-        wet_north = wetness(shift("d", ds, t, IB))
-        south, south_far = shift("x", xs, t, -IB), shift("x", xs, t, -2 * IB)
-        north, north_far = shift("x", xs, t, IB), shift("x", xs, t, 2 * IB)
+        wet_east = jnp.where(last, 0.0, shift("d", ds, t, 1))
+        wet_north = shift("d", ds, t, IB)
+        south, north, north_far = (shift("x", xs, t, s) for s in (-IB, IB, 2 * IB))
         flux_east = flux((u + shift("u", us, t, 1)) * (wet * wet_east), west, x, east, east_far)
-        flux_west = flux((shift("u", us, t, -1) + u) * (wet_west * wet), west_far, west, x, east)
         flux_north = flux((v + shift("v", vs, t, IB)) * (wet * wet_north), south, x, north, north_far)
-        flux_south = flux((shift("v", vs, t, -IB) + v) * (wet_south * wet), south_far, south, x, north)
+        fe[:, lanes_at(t + 1)] = flux_east
+        fn[:, lanes_at(t + 1)] = flux_north
+    back = {}
+
+    def turned_flux(name, ref, tile, amount):
+        if (name, tile) not in back:
+            back[name, tile] = pltpu.roll(ref[:, lanes_at(tile)], amount, 1)
+        return back[name, tile]
+
+    for t in range(TILES):
+        i = place_ref[:, lanes_at(t)]
+        x, u, wet = (ref[:, lanes_at(t + 2)] for ref in (xs, us, ds))
+        flux_east, flux_north = fe[:, lanes_at(t + 1)], fn[:, lanes_at(t + 1)]
+        flux_west = jnp.where(lane < 1, turned_flux("e", fe, t, 1), turned_flux("e", fe, t + 1, 1))
+        flux_west = jnp.where(i == 0, 0.0, flux_west)
+        flux_south = jnp.where(lane < IB, turned_flux("n", fn, t, IB), turned_flux("n", fn, t + 1, IB))
         divergence = flux_east - flux_west + (flux_north - flux_south)
         explicit = x - (wet * (COURANT / 12.0)) * divergence
         coupling = ks[:, lanes_at(t)] * wet * swap(wet)
         share = coupling / (1.0 + 2.0 * coupling)
         partial_ref[:, lanes_at(t)] = explicit + share * (swap(explicit) - explicit)
-        ws[:, lanes_at(t)] = wet
         gs[:, lanes_at(t)] = share
-        for k, (tile, at) in enumerate(bases):
-            here = tile == t
-            for n, value in enumerate((x, u, wet, share)):
-                edges[2 * n + k] = jnp.where(here, take(value, at), edges[2 * n + k])
-    for n in range(8):
-        edges_ref[n] = edges[n]
+        values = ((1, u), (0, wet), (1, wet), (0, share), (1, share))
+        for n, (k, value) in enumerate(values):
+            tile, at = bases[k]
+            edges[n] = jnp.where(tile == t, take(value, at), edges[n])
+    for n in range(5):
+        edges_ref[3 + n] = edges[n]
     for k, number in enumerate((0, 1, JB - 1, JB - 2)):
-        for n, (ref, offset) in enumerate(((xs, 2), (vs, 2), (ws, 0), (gs, 0))):
+        for n, (ref, offset) in enumerate(((xs, 2), (vs, 2), (ds, 2), (gs, 0))):
             edges_ref[8 + 4 * k + n] = line(lambda t: ref[:, lanes_at(t + offset)], number * IB, lane)
 
 

time: 32.1 us -> 31.9 us (level)
  no operation moved by 1% of the time
where the time goes in v6:
time: 31.9 us; the launch traced here: 31.7 us
  Pallas kernels  29.6 us (93%)
  local copies, waits for them, and re-layouts  2.14 us (7%)
    pallas_call x1, Pallas kernels, exchange(): pl.pallas_call(exchange_kernel, out_shape=jax.ShapeDtypeStruct((SLOTS, 4,...  29.6 us
    unnamed x1, local copies, waits for them, and re-layouts  2.14 us

profile of v6, /device:TPU:1, one launch (start us, length us, event | category | flops | bytes accessed | tf_op | source)
XLA Modules:
  0.0 31.7 jit_solution(7750362167615806729)
XLA Ops:
  0.0 29.6 %exchange.1 = f32[10,4,5400]{2,1,0:T(4,128)} custom-call(s32[10,128]{1,0:T(8,128)} %bitcast.4, s32[4,1280]{1,0:T(4,128)} %bitcast.3, s32[10,128]{1,0:T(8,128)} %bitcast.5, f32[10,4,5400]{2,1,0:T(4,128)} %tracers_hbm.1, f32[10,4,5400]{2,1,0:T(4,128)} %velocity_hbm.1, f32[10,5400]{1,0:T(8,128)} %kappa_hbm.1, f32[10,5400]{1,0:T(8,128)} %kmt_hbm.1), custom_call_target="tpu_custom_call" | custom-call | tf_op jit(solution)/shard_map/exchange/pallas_call | solution.py:548
  29.6 2.1 %copy.9 = f32[10,4,5400]{2,1,0:T(4,128)} copy(f32[10,4,5400]{2,1,0:T(4,128)} %exchange.1) | data formatting | bytes 1728000

commit v7 on v6

--- a/solution.py
+++ b/solution.py
@@ -274,7 +274,8 @@
             sides_ref[2 * q + 1] = jnp.where(lane < SIDE, pltpu.roll(body, SIDE, 1), aux)
         return carry
 
-    lax.fori_loop(0, PAIRS, one_pair, 0)
+    for pair in range(PAIRS):
+        one_pair(pair, 0)
     outputs = {"send_later": (up_ref, SLOTS), "send_earlier": (down_ref, SLOTS), "next": (next_ref, 0), "previous": (next_ref, 1)}
     for name, (ref, at) in outputs.items():
         which = jnp.broadcast_to(chosen[name], (8, LANES))

time: 31.9 us -> 31.9 us (level)
  no operation moved by 1% of the time
where the time goes in v7:
time: 31.9 us; the launch traced here: 31.8 us
  Pallas kernels  29.7 us (93%)
  local copies, waits for them, and re-layouts  2.14 us (7%)
    pallas_call x1, Pallas kernels, exchange(): pl.pallas_call(exchange_kernel, out_shape=jax.ShapeDtypeStruct((SLOTS, 4,...  29.7 us
    unnamed x1, local copies, waits for them, and re-layouts  2.14 us

profile of v7, /device:TPU:1, one launch (start us, length us, event | category | flops | bytes accessed | tf_op | source)
XLA Modules:
  0.0 31.8 jit_solution(5680428795247527873)
XLA Ops:
  0.0 29.7 %exchange.1 = f32[10,4,5400]{2,1,0:T(4,128)} custom-call(s32[10,128]{1,0:T(8,128)} %bitcast.4, s32[4,1280]{1,0:T(4,128)} %bitcast.3, s32[10,128]{1,0:T(8,128)} %bitcast.5, f32[10,4,5400]{2,1,0:T(4,128)} %tracers_hbm.1, f32[10,4,5400]{2,1,0:T(4,128)} %velocity_hbm.1, f32[10,5400]{1,0:T(8,128)} %kappa_hbm.1, f32[10,5400]{1,0:T(8,128)} %kmt_hbm.1), custom_call_target="tpu_custom_call" | custom-call | tf_op jit(solution)/shard_map/exchange/pallas_call | solution.py:549
  29.7 2.1 %copy.9 = f32[10,4,5400]{2,1,0:T(4,128)} copy(f32[10,4,5400]{2,1,0:T(4,128)} %exchange.1) | data formatting | bytes 1728000
